TPU v7x, 32 devices: a whole 2x2x4 slice. The times are simulated.
32 devices in a mesh: seq: 8 (over z, y), head: 4 (over x, core).
Axes of the slice: x: 2, y: 2, z: 4, core: 2. Of those that a mesh axis runs over, the one named last changes fastest.
Arguments:
- queries: bfloat16 [1536, 4096], P('seq', 'head'), may hold values from -125 to 125
- key_vectors: bfloat16 [1536, 4096], P('seq', 'head'), may hold values from -21 to 21
- values: bfloat16 [1536, 4096], P('seq', 'head'), may hold values from -6 to 6
- cotangent: bfloat16 [1536, 4096], P('seq', 'head'), may hold values from -6 to 6
- cluster: int32 [1536, 1], P('seq'), may hold values from 0 to 1; in each aligned block of 192 rows (0 to 191, 192 to 383, ...) at most 192 rows name the same one
- block_pattern: int32 [2, 12, 12], replicated, may hold values from 0 to 1, as said below
Outputs:
- attended: bfloat16 [1536, 4096], P('seq', 'head')
- query_grad: bfloat16 [1536, 4096], P('seq', 'head')
- key_grad: bfloat16 [1536, 4096], P('seq', 'head')
- value_grad: bfloat16 [1536, 4096], P('seq', 'head')
Inputs may be any that keep to these rules, and one draw needn't show every extreme that they name: Within the rows of one device no cluster is named by more than 192 rows, and in every draw some cluster is named by exactly 192 rows of some device. Every diagonal entry block_pattern[g, b, b] is 1.
All inputs are finite; a program needn't handle non-finite values.
Results may differ from a plain program's by a relative error of at most 0.0061.
Values may be sent and summed in bfloat16 or wider, within the bound.
No kernel may reach another device: no remote copies, remote signals or barrier semaphores. Data moves between devices by JAX's collectives and lax.ppermute only.
A program may use at most 128 MiB of HBM per device.

v0:
```python
import functools

import jax
import jax.numpy as jnp
from jax import lax
from jax.experimental import pallas as pl
from jax.experimental.pallas import tpu as pltpu
from jax.sharding import PartitionSpec as P

HEADS = 32
HEAD_DIM = 128
GS = 4
BLK = 128


NEG_FILL = -1e30
EPSILON = 1e-05
SCORE_SCALE = HEAD_DIM ** (-0.5)
EXPONENT_SCALE = SCORE_SCALE * 1.4426950408889634
LANES = 128
ID_ROWS = 16
QUERY_TILE = 256
VMEM_BYTES = 48 << 20


def contract_last(left_side, right_side):
    return lax.dot_general(
        left_side, right_side, (((1,), (1,)), ((), ())), preferred_element_type=jnp.float32
    )


def contract_first(left_side, right_side):
    return lax.dot_general(
        left_side, right_side, (((0,), (0,)), ((), ())), preferred_element_type=jnp.float32
    )


def visible_mask(pattern, query_pos, query_live, key_pos, key_live):
    pattern_rows = pattern[query_pos // BLK]
    allowed = jnp.take(pattern_rows, key_pos // BLK, axis=1) == 1
    causal = key_pos[None, :] <= query_pos[:, None]
    return allowed & causal & query_live[:, None] & key_live[None, :]


def cluster_ranks(table, cluster_index):
    source_count, tok_count = table.shape
    in_cluster = table == cluster_index
    token_iota = jnp.arange(tok_count, dtype=jnp.int32)
    earlier_table = (token_iota[:, None] < token_iota[None, :]).astype(jnp.bfloat16)
    earlier = jnp.dot(
        in_cluster.astype(jnp.bfloat16), earlier_table, preferred_element_type=jnp.float32
    ).astype(jnp.int32)
    global_pos = (
        jnp.arange(source_count, dtype=jnp.int32)[:, None] * tok_count + token_iota[None, :]
    )
    return (in_cluster, earlier, global_pos)


def code_positions(slot_code, global_pos, capacity):
    matches = slot_code[:, :, None] == jnp.arange(capacity, dtype=jnp.int32)[None, None, :]
    positions = jnp.sum(jnp.where(matches, global_pos[:, :, None], 0), axis=1)
    occupied = jnp.any(matches, axis=1)
    return (positions, occupied)


def rank_positions(table, cluster_index, capacity):
    in_cluster, earlier, global_pos = cluster_ranks(table, cluster_index)
    rank_code = jnp.where(in_cluster, earlier, -1)
    positions, occupied = code_positions(rank_code, global_pos, capacity)
    return (positions.reshape(-1), occupied.reshape(-1))


def dispatch_rows(outgoing):
    return lax.all_to_all(outgoing, "seq", split_axis=1, concat_axis=1, tiled=True)


def combine_rows(outgoing):
    return lax.all_to_all(outgoing, "seq", split_axis=1, concat_axis=1, tiled=True)


def forward_heads(query_slots, key_slots, value_slots, grad_slots, visible, score_scale):
    query_count, features = query_slots.shape
    key_count = key_slots.shape[0]
    head_count = features // HEAD_DIM
    attended = jnp.zeros((query_count, features), jnp.bfloat16)
    query_grad = jnp.zeros((query_count, features), jnp.bfloat16)
    side_result = jnp.zeros((2, key_count, features), jnp.float32)

    def one_head(head_index, running):
        attended_acc, query_acc, side_acc = running
        column_start = head_index * HEAD_DIM
        query_rows = lax.dynamic_slice_in_dim(query_slots, column_start, HEAD_DIM, 1)
        key_rows = lax.dynamic_slice_in_dim(key_slots, column_start, HEAD_DIM, 1)
        value_rows = lax.dynamic_slice_in_dim(value_slots, column_start, HEAD_DIM, 1)
        grad_rows = lax.dynamic_slice_in_dim(grad_slots, column_start, HEAD_DIM, 1)
        scores = jnp.where(visible, contract_last(query_rows, key_rows) * score_scale, NEG_FILL)
        row_max = jnp.max(scores, axis=1, keepdims=True)
        weights = jnp.where(visible, jnp.exp(scores - row_max), 0.0)
        row_total = jnp.maximum(jnp.sum(weights, axis=1, keepdims=True), 1.0)
        probabilities = weights / row_total
        prob_half = probabilities.astype(jnp.bfloat16)
        attended_head = jnp.dot(prob_half, value_rows, preferred_element_type=jnp.float32).astype(
            jnp.bfloat16
        )
        prob_grad = contract_last(grad_rows, value_rows)
        row_delta = jnp.sum(probabilities * prob_grad, axis=1, keepdims=True)
        score_grad = (probabilities * (prob_grad - row_delta)).astype(jnp.bfloat16)
        query_head = (
            jnp.dot(score_grad, key_rows, preferred_element_type=jnp.float32) * score_scale
        ).astype(jnp.bfloat16)
        attended_acc = lax.dynamic_update_slice_in_dim(attended_acc, attended_head, column_start, 1)
        query_acc = lax.dynamic_update_slice_in_dim(query_acc, query_head, column_start, 1)
        key_part = contract_first(score_grad, query_rows)
        value_part = contract_first(prob_half, grad_rows)
        side_acc = lax.dynamic_update_slice_in_dim(
            side_acc, jnp.stack([key_part, value_part]), column_start, 2
        )
        return (attended_acc, query_acc, side_acc)

    return lax.fori_loop(0, head_count, one_head, (attended, query_grad, side_result))


def per_device(queries, key_vectors, values, cotangent, cluster, block_pattern):
    seq_count = lax.axis_size("seq")
    tok_count, features = queries.shape
    slot_count = 2 * tok_count // seq_count
    group_count = seq_count // GS
    score_scale = HEAD_DIM ** (-0.5)
    my_index = lax.axis_index("seq")
    group_index = my_index // GS
    key_float = key_vectors.astype(jnp.float32)
    square_sum = lax.psum(jnp.sum(key_float * key_float, axis=1), "head")
    key_rms = jnp.sqrt(square_sum / (HEADS * HEAD_DIM) + EPSILON)[:, None]
    normed_float = key_float / key_rms
    normed = normed_float.astype(jnp.bfloat16)
    own_ids = cluster[:, 0]
    everyone = lax.all_gather(own_ids, "seq", axis=0, tiled=True)
    table = everyone.reshape(seq_count, tok_count)
    token_iota = jnp.arange(tok_count, dtype=jnp.int32)
    onehot_own = (own_ids[:, None] == jnp.arange(group_count, dtype=jnp.int32)[None, :]).astype(
        jnp.bfloat16
    )
    before_table = (token_iota[:, None] > token_iota[None, :]).astype(jnp.bfloat16)
    before = jnp.dot(before_table, onehot_own, preferred_element_type=jnp.float32)
    own_rank = jnp.sum(before * onehot_own.astype(jnp.float32), axis=1).astype(jnp.int32)
    pattern = lax.dynamic_index_in_dim(block_pattern, group_index, 0, keepdims=False)
    stacked_inputs = jnp.stack([queries, normed, values, cotangent])
    quarter = features // GS
    capacity = GS * slot_count
    split_inputs = stacked_inputs.reshape(4, tok_count, GS, quarter)
    placed = (
        jnp.zeros((4, group_count, capacity, GS, quarter), jnp.bfloat16)
        .at[:, own_ids, own_rank]
        .set(split_inputs)
    )
    outgoing = placed.transpose(0, 1, 3, 2, 4).reshape(4, seq_count * capacity, quarter)
    arrived = dispatch_rows(outgoing)
    flat_positions, flat_present = rank_positions(table, group_index, capacity)
    visible = visible_mask(pattern, flat_positions, flat_present, flat_positions, flat_present)
    attended, query_grad, both_terms = forward_heads(
        arrived[0], arrived[1], arrived[2], arrived[3], visible, score_scale
    )
    normed_grad = (both_terms[0] * score_scale).astype(jnp.bfloat16)
    value_slots = both_terms[1].astype(jnp.bfloat16)
    outgoing_back = jnp.stack([attended, query_grad, normed_grad, value_slots])
    returned = combine_rows(outgoing_back)
    arranged = returned.reshape(4, group_count, GS, capacity, quarter).transpose(1, 3, 0, 2, 4)
    home_rows = arranged[own_ids, own_rank].transpose(1, 0, 2, 3).reshape(4, tok_count, features)
    grad_float = home_rows[2].astype(jnp.float32)
    inner = lax.psum(jnp.sum(normed_float * grad_float, axis=1), "head")
    key_grad = (
        (grad_float - normed_float * (inner / (HEADS * HEAD_DIM))[:, None]) / key_rms
    ).astype(jnp.bfloat16)
    return (home_rows[0], home_rows[1], key_grad, home_rows[3])


def row_to_column(row, count):
    lanes = row.shape[1]
    diagonal = lax.broadcasted_iota(jnp.int32, (lanes, lanes), 0) == lax.broadcasted_iota(
        jnp.int32, (lanes, lanes), 1
    )
    spread = jnp.where(diagonal, jnp.broadcast_to(row, (lanes, lanes)), 0.0)
    return jnp.sum(spread, axis=1, keepdims=True)[:count]


def column_of(rows_ref, first_row, count):
    pieces = []
    for start in range(0, count, LANES):
        row = rows_ref[first_row + start // LANES : first_row + start // LANES + 1, :LANES]
        pieces.append(row_to_column(row.astype(jnp.float32), min(LANES, count - start)))
    return jnp.concatenate(pieces, axis=0)


def store_as_rows(out_ref, first_row, column):
    count = column.shape[0]
    for start in range(0, count, LANES):
        size = min(LANES, count - start)
        diagonal = lax.broadcasted_iota(jnp.int32, (size, LANES), 0) == lax.broadcasted_iota(
            jnp.int32, (size, LANES), 1
        )
        spread = jnp.where(diagonal, column[start : start + size], 0.0)
        row = first_row + start // LANES
        out_ref[row : row + 1, :] = jnp.sum(spread, axis=0, keepdims=True)


def block_rows(index, size):
    return pl.ds(pl.multiple_of(index * size, 16), size)


def pack_kernel(half_count, query_ref, value_ref, grad_ref, ids_ref, out_ref, sems):
    tokens, features = query_ref.shape
    width = features // half_count
    stride = 3 * tokens + ID_ROWS
    copies = []
    for place, source_ref in enumerate((query_ref, value_ref, grad_ref)):
        for owner in range(half_count):
            copies.append(
                pltpu.make_async_copy(
                    source_ref.at[:, owner * width : (owner + 1) * width],
                    out_ref.at[pl.ds(owner * stride + place * tokens, tokens), :],
                    sems.at[place * half_count + owner],
                )
            )
    for copy in copies:
        copy.start()
    for owner in range(half_count):
        rows = slice(owner * stride + 3 * tokens, (owner + 1) * stride)
        out_ref[rows, :LANES] = ids_ref[...]
        out_ref[rows, LANES:] = jnp.zeros((ID_ROWS, width - LANES), jnp.bfloat16)
    for copy in copies:
        copy.wait()


def pack_keys_kernel(
    half_count, me_ref, query_ref, value_ref, grad_ref, key_ref, rms_ref, ids_ref, *out_refs
):
    tokens, features = key_ref.shape
    width = features // half_count
    single = width // 2
    is_high = me_ref[0] >= half_count
    inside = me_ref[0] & (half_count - 1)
    key_refs, cross_refs = out_refs[:half_count], out_refs[half_count:]
    rms = column_of(rms_ref, 0, tokens)

    def normed_columns(first, size):
        return (key_ref[:, pl.ds(first, size)].astype(jnp.float32) / rms).astype(jnp.bfloat16)

    for distance in range(half_count):
        first = pl.multiple_of((inside ^ distance) * width, LANES)
        cross_ref = cross_refs[distance]
        key_refs[distance][...] = normed_columns(first, width)
        cross_ref[2 * tokens :, :LANES] = ids_ref[...]
        if single > LANES:
            cross_ref[2 * tokens :, LANES:] = jnp.zeros((ID_ROWS, single - LANES), jnp.bfloat16)

        @pl.when(is_high)
        def send_down():
            second = pl.multiple_of(first + single, LANES)
            cross_ref[:tokens, :] = query_ref[:, pl.ds(second, single)]
            cross_ref[tokens : 2 * tokens, :] = grad_ref[:, pl.ds(second, single)]

        @pl.when(jnp.logical_not(is_high))
        def send_up():
            cross_ref[:tokens, :] = normed_columns(first, single)
            cross_ref[tokens : 2 * tokens, :] = value_ref[:, pl.ds(first, single)]


class Slots:
    def __init__(self, shape, me_ref, pattern_ref, packed_ref, key_refs, cross_refs):
        self.tokens, self.half_count, self.cluster_count, self.block_count = shape
        self.half_len = self.tokens * self.half_count
        self.half_blocks = self.half_len // BLK
        self.is_high = me_ref[0] >= self.half_count
        self.inside = me_ref[0] & (self.half_count - 1)
        self.pattern_ref, self.packed_ref = pattern_ref, packed_ref
        self.key_refs, self.cross_refs = key_refs, cross_refs
        lane = lax.broadcasted_iota(jnp.int32, (1, LANES), 1)
        lane_cluster = jnp.zeros((1, LANES), jnp.int32)
        for index in range(1, self.cluster_count + 1):
            lane_cluster = lane_cluster + (lane >= index * self.block_count).astype(jnp.int32)
        self.lane_block = lane - lane_cluster * self.block_count
        self.lane_cluster = lane_cluster.astype(jnp.float32)

    def own_ids(self, ids_all):
        stride = 3 * self.tokens + ID_ROWS
        for source in range(self.half_count):
            ids_all[source * self.tokens : (source + 1) * self.tokens, :] = column_of(
                self.packed_ref, source * stride + 3 * self.tokens, self.tokens
            )

    def cross_ids(self, ids_all):
        for distance in range(self.half_count):
            ids_all[block_rows(self.inside ^ distance, self.tokens), :] = column_of(
                self.cross_refs[distance], 2 * self.tokens, self.tokens
            )

    def query_features(self, ids_all, target, high):
        for block in range(self.half_blocks):
            rows = slice(block * BLK, (block + 1) * BLK)
            place = block + high * self.half_blocks
            allowed = self.pattern_ref[pl.ds(place, 1), :] == 1.0
            same = ids_all[rows, :] == self.lane_cluster
            target[rows, HEAD_DIM:] = jnp.where(same & allowed, 0.0, NEG_FILL).astype(jnp.bfloat16)

    def key_features(self, ids_all, target, high):
        for block in range(self.half_blocks):
            rows = slice(block * BLK, (block + 1) * BLK)
            place = block + high * self.half_blocks
            same = ids_all[rows, :] == self.lane_cluster
            target[rows, HEAD_DIM:] = jnp.where(same & (self.lane_block == place), 1.0, 0.0).astype(
                jnp.bfloat16
            )

    def own(self, column, query_all, key_all, value_all, grad_all):
        columns = slice(column, column + HEAD_DIM)
        stride = 3 * self.tokens + ID_ROWS
        for source in range(self.half_count):
            rows = slice(source * self.tokens, (source + 1) * self.tokens)
            for place, target in enumerate((query_all, value_all, grad_all)):
                first = source * stride + place * self.tokens
                target[rows, :HEAD_DIM] = self.packed_ref[first : first + self.tokens, columns]
        for distance in range(self.half_count):
            rows = block_rows(self.inside ^ distance, self.tokens)
            key_all[rows, :HEAD_DIM] = self.key_refs[distance][:, columns]

    def cross(self, column, first_all, second_all):
        columns = slice(column, column + HEAD_DIM)
        for distance in range(self.half_count):
            rows = block_rows(self.inside ^ distance, self.tokens)
            cross_ref = self.cross_refs[distance]
            first_all[rows, :HEAD_DIM] = cross_ref[: self.tokens, columns]
            second_all[rows, :] = cross_ref[self.tokens : 2 * self.tokens, columns]


def tile_scores(query_tile, pieces):
    results = []
    for key_all, _, limit, first in pieces:
        scores = contract_last(query_tile, key_all[:limit, :])
        if first is not None:
            column_index = lax.broadcasted_iota(jnp.int32, scores.shape, 1)
            row_index = lax.broadcasted_iota(jnp.int32, scores.shape, 0) + first
            scores = jnp.where(column_index <= row_index, scores, NEG_FILL)
        results.append(scores)
    return results


def tile_stats(scores, prob_grads):
    row_max = functools.reduce(
        jnp.maximum, [jnp.max(part, axis=1, keepdims=True) for part in scores]
    )
    weights = [jnp.exp2((part - row_max) * EXPONENT_SCALE) for part in scores]
    row_total = sum(jnp.sum(part, axis=1, keepdims=True) for part in weights)
    row_delta = sum(
        jnp.sum(part * grad, axis=1, keepdims=True) for part, grad in zip(weights, prob_grads)
    )
    return weights, row_max, row_total, row_delta


def tile_backward(query_tile, grad_tile, pieces, sums, stats, is_first):
    scores = tile_scores(query_tile, pieces)
    prob_grads = [contract_last(grad_tile, piece[1][: piece[2], :]) for piece in pieces]
    if stats is None:
        weights, _, row_total, row_delta = tile_stats(scores, prob_grads)
        inverse = 1.0 / jnp.maximum(row_total, 1.0)
        row_delta = row_delta * inverse
    else:
        row_max, inverse, row_delta = stats
        weights = [jnp.exp2((part - row_max) * EXPONENT_SCALE) for part in scores]
    attended, query_grad = 0.0, 0.0
    for index, (key_all, value_all, limit, first) in enumerate(pieces):
        probabilities = weights[index] * inverse
        prob_half = probabilities.astype(jnp.bfloat16)
        score_grad = (probabilities * (prob_grads[index] - row_delta)).astype(jnp.bfloat16)
        attended += jnp.dot(prob_half, value_all[:limit, :], preferred_element_type=jnp.float32)
        query_grad += jnp.dot(
            score_grad, key_all[:limit, :HEAD_DIM], preferred_element_type=jnp.float32
        )
        key_part = contract_first(score_grad, query_tile[:, :HEAD_DIM])
        value_part = contract_first(prob_half, grad_tile)
        key_sum, value_sum = sums[index]
        fresh = 0 if is_first else (limit if first is None else first)
        if fresh:
            key_sum[:fresh, :] += key_part[:fresh]
            value_sum[:fresh, :] += value_part[:fresh]
        if fresh < limit:
            key_sum[fresh:limit, :] = key_part[fresh:]
            value_sum[fresh:limit, :] = value_part[fresh:]
    return attended.astype(jnp.bfloat16), (query_grad * SCORE_SCALE).astype(jnp.bfloat16)


def own_tiles(half_len):
    tile = QUERY_TILE if half_len % QUERY_TILE == 0 else BLK
    return [(first, slice(first, first + tile), first + tile) for first in range(0, half_len, tile)]


def stats_kernel(shape, stat_rows, me_ref, pattern_ref, packed_ref, *refs):
    half_count = shape[1]
    key_refs, cross_refs = refs[:half_count], refs[half_count : 2 * half_count]
    out_ref, query_all, key_all, value_all, grad_all, other_query, other_grad, ids = refs[
        2 * half_count :
    ]
    slots = Slots(shape, me_ref, pattern_ref, packed_ref, key_refs, cross_refs)
    single = packed_ref.shape[1] // 2
    out_ref[...] = jnp.zeros_like(out_ref)
    slots.own_ids(ids)
    slots.key_features(ids, key_all, slots.is_high.astype(jnp.int32))

    @pl.when(slots.is_high)
    def _():
        slots.query_features(ids, query_all, 1)

    @pl.when(jnp.logical_not(slots.is_high))
    def _():
        slots.cross_ids(ids)
        slots.query_features(ids, other_query, 1)

    for head in range(single // HEAD_DIM):
        slots.own(single + head * HEAD_DIM, query_all, key_all, value_all, grad_all)
        first_row = 3 * stat_rows * head

        def note(first, found):
            for place, column in enumerate(found[1:]):
                store_as_rows(
                    out_ref, first_row + place * stat_rows + first // LANES, column
                )

        @pl.when(slots.is_high)
        def _():
            for first, rows, limit in own_tiles(slots.half_len):
                pieces = [(key_all, value_all, limit, first)]
                scores = tile_scores(query_all[rows, :], pieces)
                prob_grad = contract_last(grad_all[rows, :], value_all[:limit, :])
                note(first, tile_stats(scores, [prob_grad]))

        @pl.when(jnp.logical_not(slots.is_high))
        def _():
            slots.cross(head * HEAD_DIM, other_query, other_grad)
            for first, rows, _ in own_tiles(slots.half_len):
                pieces = [(key_all, value_all, slots.half_len, None)]
                scores = tile_scores(other_query[rows, :], pieces)
                prob_grad = contract_last(other_grad[rows, :], value_all[...])
                note(first, tile_stats(scores, [prob_grad]))


def store_own(slots, result_ref, key_refs, column, results, key_sum, value_sum):
    attended, query_grad = results
    tokens = slots.tokens
    columns = slice(column, column + HEAD_DIM)
    stride = result_ref.shape[0] // slots.half_count
    for source in range(slots.half_count):
        rows = slice(source * tokens, (source + 1) * tokens)
        first = source * stride
        result_ref[first : first + tokens, columns] = attended[rows, :]
        result_ref[first + tokens : first + 2 * tokens, columns] = query_grad[rows, :]
        result_ref[first + 2 * tokens : first + 3 * tokens, columns] = value_sum[rows, :].astype(
            jnp.bfloat16
        )
    for distance in range(slots.half_count):
        rows = block_rows(slots.inside ^ distance, tokens)
        key_refs[distance][:, columns] = (key_sum[rows, :] * SCORE_SCALE).astype(jnp.bfloat16)


def first_head_kernel(shape, me_ref, pattern_ref, packed_ref, *refs):
    half_count = shape[1]
    key_refs, cross_refs = refs[:half_count], refs[half_count : 2 * half_count]
    refs = refs[2 * half_count :]
    result_ref, key_out_refs, cross_out_refs = (
        refs[0], refs[1 : 1 + half_count], refs[1 + half_count : 1 + 2 * half_count]
    )
    (query_all, key_all, value_all, grad_all, other_key, other_value, ids, attended, query_grad,
     key_sum, value_sum, other_key_sum, other_value_sum) = refs[1 + 2 * half_count :]
    slots = Slots(shape, me_ref, pattern_ref, packed_ref, key_refs, cross_refs)
    single = packed_ref.shape[1] // 2
    high = slots.is_high.astype(jnp.int32)
    slots.own_ids(ids)
    slots.key_features(ids, key_all, high)
    slots.query_features(ids, query_all, high)

    @pl.when(slots.is_high)
    def _():
        slots.cross_ids(ids)
        slots.key_features(ids, other_key, 0)

    for head in range(single // HEAD_DIM):
        column = head * HEAD_DIM
        slots.own(column, query_all, key_all, value_all, grad_all)

        def run(others, other_sums):
            for first, rows, limit in own_tiles(slots.half_len):
                attended[rows, :], query_grad[rows, :] = tile_backward(
                    query_all[rows, :],
                    grad_all[rows, :],
                    others + [(key_all, value_all, limit, first)],
                    other_sums + [(key_sum, value_sum)],
                    None,
                    first == 0,
                )

        @pl.when(slots.is_high)
        def _():
            slots.cross(column, other_key, other_value)
            run(
                [(other_key, other_value, slots.half_len, None)],
                [(other_key_sum, other_value_sum)],
            )
            for distance in range(half_count):
                rows = block_rows(slots.inside ^ distance, slots.tokens)
                columns = slice(column, column + HEAD_DIM)
                target = cross_out_refs[distance]
                target[: slots.tokens, columns] = (other_key_sum[rows, :] * SCORE_SCALE).astype(
                    jnp.bfloat16
                )
                target[slots.tokens :, columns] = other_value_sum[rows, :].astype(jnp.bfloat16)

        @pl.when(jnp.logical_not(slots.is_high))
        def _():
            run([], [])
            for distance in range(half_count):
                cross_out_refs[distance][...] = jnp.zeros_like(cross_out_refs[distance])

        store_own(slots, result_ref, key_out_refs, column, (attended, query_grad), key_sum, value_sum)


def second_head_kernel(shape, stat_rows, me_ref, pattern_ref, packed_ref, *refs):
    half_count = shape[1]
    key_refs, cross_refs = refs[:half_count], refs[half_count : 2 * half_count]
    own_stats_ref, other_stats_ref, first_result_ref = refs[2 * half_count : 2 * half_count + 3]
    refs = refs[2 * half_count + 3 :]
    first_key_refs, first_cross_refs = refs[:half_count], refs[half_count : 2 * half_count]
    refs = refs[2 * half_count :]
    result_ref, key_out_refs, cross_out_refs = (
        refs[0], refs[1 : 1 + half_count], refs[1 + half_count : 1 + 2 * half_count]
    )
    (query_all, key_all, value_all, grad_all, other_query, other_grad, ids, attended, query_grad,
     key_sum, value_sum, other_attended, other_query_grad) = refs[1 + 2 * half_count :]
    slots = Slots(shape, me_ref, pattern_ref, packed_ref, key_refs, cross_refs)
    single = packed_ref.shape[1] // 2
    high = slots.is_high.astype(jnp.int32)
    slots.own_ids(ids)
    slots.key_features(ids, key_all, high)
    slots.query_features(ids, query_all, high)

    @pl.when(jnp.logical_not(slots.is_high))
    def _():
        slots.cross_ids(ids)
        slots.query_features(ids, other_query, 1)

    result_ref[:, :single] = first_result_ref[...]
    for distance in range(half_count):
        key_out_refs[distance][:, :single] = first_key_refs[distance][...]

    def joint_stats(head, first, size):
        found = [
            [
                column_of(
                    ref, 3 * stat_rows * head + place * stat_rows + first // LANES, size
                )
                for place in range(3)
            ]
            for ref in (own_stats_ref, other_stats_ref)
        ]
        (own_max, own_total, own_delta), (far_max, far_total, far_delta) = found
        row_max = jnp.maximum(own_max, far_max)
        own_part = jnp.exp2((own_max - row_max) * EXPONENT_SCALE)
        far_part = jnp.exp2((far_max - row_max) * EXPONENT_SCALE)
        inverse = 1.0 / jnp.maximum(own_total * own_part + far_total * far_part, 1.0)
        return row_max, inverse, (own_delta * own_part + far_delta * far_part) * inverse

    for head in range(single // HEAD_DIM):
        column = head * HEAD_DIM
        slots.own(single + column, query_all, key_all, value_all, grad_all)

        def run(joint):
            for first, rows, limit in own_tiles(slots.half_len):
                attended[rows, :], query_grad[rows, :] = tile_backward(
                    query_all[rows, :],
                    grad_all[rows, :],
                    [(key_all, value_all, limit, first)],
                    [(key_sum, value_sum)],
                    joint_stats(head, first, limit - first) if joint else None,
                    first == 0,
                )

        @pl.when(slots.is_high)
        def _():
            run(True)
            for distance in range(half_count):
                cross_out_refs[distance][...] = first_cross_refs[distance][...]

        @pl.when(jnp.logical_not(slots.is_high))
        def _():
            slots.cross(column, other_query, other_grad)
            run(False)
            for first, rows, limit in own_tiles(slots.half_len):
                other_attended[rows, :], other_query_grad[rows, :] = tile_backward(
                    other_query[rows, :],
                    other_grad[rows, :],
                    [(key_all, value_all, slots.half_len, None)],
                    [(key_sum, value_sum)],
                    joint_stats(head, first, limit - first),
                    False,
                )
            for distance in range(half_count):
                rows = block_rows(slots.inside ^ distance, slots.tokens)
                columns = slice(column, column + HEAD_DIM)
                target = cross_out_refs[distance]
                target[: slots.tokens, columns] = other_attended[rows, :]
                target[slots.tokens :, columns] = other_query_grad[rows, :]

        store_own(
            slots, result_ref, key_out_refs, single + column, (attended, query_grad), key_sum,
            value_sum,
        )


def normed_grad_of(half_count, me_ref, key_grad_refs, cross_refs, distance, tokens):
    single = key_grad_refs[distance].shape[1] // 2
    is_low = me_ref[0] < half_count
    grad_float = key_grad_refs[distance][...].astype(jnp.float32)
    far = jnp.where(is_low, cross_refs[distance][:tokens, :].astype(jnp.float32), 0.0)
    return jnp.concatenate([grad_float[:, :single] + far, grad_float[:, single:]], axis=1)


def inner_kernel(half_count, me_ref, key_ref, rms_ref, *refs):
    key_grad_refs, cross_refs = refs[:half_count], refs[half_count : 2 * half_count]
    out_ref = refs[2 * half_count]
    tokens, features = key_ref.shape
    width = features // half_count
    inside = me_ref[0] & (half_count - 1)
    total = jnp.zeros((tokens, width), jnp.float32)
    for distance in range(half_count):
        start = pl.multiple_of((inside ^ distance) * width, LANES)
        key_float = key_ref[:, pl.ds(start, width)].astype(jnp.float32)
        total = total + key_float * normed_grad_of(
            half_count, me_ref, key_grad_refs, cross_refs, distance, tokens
        )
    column = jnp.sum(total, axis=1, keepdims=True) / column_of(rms_ref, 0, tokens)
    out_ref[...] = jnp.zeros_like(out_ref)
    store_as_rows(out_ref, 0, column)


def final_kernel(half_count, feature_total, me_ref, key_ref, rms_ref, inner_ref, *refs):
    key_grad_refs, cross_refs = refs[:half_count], refs[half_count : 2 * half_count]
    result_ref, attended_ref, query_ref, key_out_ref, value_ref = refs[2 * half_count :]
    tokens, features = key_ref.shape
    width = features // half_count
    single = width // 2
    is_high = me_ref[0] >= half_count
    inside = me_ref[0] & (half_count - 1)
    rms = column_of(rms_ref, 0, tokens)
    inner = column_of(inner_ref, 0, tokens) / feature_total
    for owner in range(half_count):
        columns = slice(owner * width, (owner + 1) * width)
        for place, target in enumerate((attended_ref, query_ref, value_ref)):
            first = (owner * 3 + place) * tokens
            target[:, columns] = result_ref[first : first + tokens, :]
    for distance in range(half_count):
        start = pl.multiple_of((inside ^ distance) * width, LANES)
        columns = pl.ds(start, width)
        normed_float = key_ref[:, columns].astype(jnp.float32) / rms
        grad_float = normed_grad_of(
            half_count, me_ref, key_grad_refs, cross_refs, distance, tokens
        )
        key_out_ref[:, columns] = ((grad_float - normed_float * inner) / rms).astype(jnp.bfloat16)
        cross_ref = cross_refs[distance]

        def add(target, columns, first):
            far = cross_ref[first : first + tokens, :].astype(jnp.float32)
            target[:, columns] = (target[:, columns].astype(jnp.float32) + far).astype(jnp.bfloat16)

        @pl.when(is_high)
        def _():
            second = pl.ds(pl.multiple_of(start + single, LANES), single)
            add(attended_ref, second, 0)
            add(query_ref, second, tokens)

        @pl.when(jnp.logical_not(is_high))
        def _():
            add(value_ref, pl.ds(start, single), tokens)


def lane_rows(vector, row_count):
    return jnp.pad(vector, (0, row_count * LANES - vector.shape[0])).reshape(row_count, LANES)


def half_array(rows, columns):
    return jax.ShapeDtypeStruct((rows, columns), jnp.bfloat16)


def call(kernel, out_shapes, scalars, arrays, scratch=(), in_hbm=0):
    vmem, anywhere = pl.BlockSpec(memory_space=pltpu.VMEM), pl.BlockSpec(memory_space=pl.ANY)
    return pl.pallas_call(
        kernel,
        out_shape=out_shapes,
        in_specs=[pl.BlockSpec(memory_space=pltpu.SMEM)] * len(scalars)
        + [anywhere] * in_hbm
        + [vmem] * (len(arrays) - in_hbm),
        out_specs=jax.tree.map(lambda shape: vmem, out_shapes),
        scratch_shapes=list(scratch),
        compiler_params=pltpu.CompilerParams(vmem_limit_bytes=VMEM_BYTES),
    )(*scalars, *arrays)


def swap(block, distance):
    count = lax.axis_size("seq")
    return lax.ppermute(block, "seq", [(i, i ^ distance) for i in range(count)])


def swap_inside(blocks):
    return [blocks[0]] + [swap(block, d) for d, block in enumerate(blocks) if d]


def swap_across(blocks):
    return [swap(block, len(blocks) + d) for d, block in enumerate(blocks)]


def exchange_inside(rows):
    count = lax.axis_size("seq")
    groups = [list(range(count // 2)), list(range(count // 2, count))]
    return lax.all_to_all(
        rows, "seq", split_axis=0, concat_axis=0, tiled=True, axis_index_groups=groups
    )


def by_halves(queries, key_vectors, values, cotangent, cluster, block_pattern):
    count = lax.axis_size("seq")
    half_count = count // 2
    tokens, features = queries.shape
    width = features // half_count
    single = width // 2
    cluster_count, block_count, _ = block_pattern.shape
    half_len = half_count * tokens
    shape = (tokens, half_count, cluster_count, block_count)
    row_count = -(-tokens // LANES)
    stat_rows = -(-half_len // LANES)
    me = lax.axis_index("seq").astype(jnp.int32).reshape(1)
    ids = lane_rows(cluster[:, 0], ID_ROWS).astype(jnp.bfloat16)
    packed = call(
        functools.partial(pack_kernel, half_count),
        half_array(half_count * (3 * tokens + ID_ROWS), width),
        [],
        [queries, values, cotangent, ids],
        [pltpu.SemaphoreType.DMA((3 * half_count,))],
        in_hbm=3,
    )
    packed = exchange_inside(packed)
    key_float = key_vectors.astype(jnp.float32)
    square_sum = lax.psum(jnp.sum(key_float * key_float, axis=1), "head")
    feature_total = HEADS * HEAD_DIM
    key_rms = lane_rows(jnp.sqrt(square_sum / feature_total + EPSILON), row_count)
    sent = call(
        functools.partial(pack_keys_kernel, half_count),
        [half_array(tokens, width)] * half_count
        + [half_array(2 * tokens + ID_ROWS, single)] * half_count,
        [me],
        [queries, values, cotangent, key_vectors, key_rms, ids],
    )
    cross = swap_across(sent[half_count:])
    keys = swap_inside(sent[:half_count])
    pattern_rows = block_pattern.transpose(1, 0, 2).reshape(block_count, -1).astype(jnp.float32)
    pattern_rows = jnp.pad(pattern_rows, ((0, 0), (0, LANES - cluster_count * block_count)))
    inputs = [pattern_rows, packed] + keys + cross
    wide = pltpu.VMEM((half_len, 2 * HEAD_DIM), jnp.bfloat16)
    slim = pltpu.VMEM((half_len, HEAD_DIM), jnp.bfloat16)
    sums = pltpu.VMEM((half_len, HEAD_DIM), jnp.float32)
    ids_column = pltpu.VMEM((half_len, 1), jnp.float32)
    stats = call(
        functools.partial(stats_kernel, shape, stat_rows),
        jax.ShapeDtypeStruct((3 * stat_rows * (single // HEAD_DIM), LANES), jnp.float32),
        [me],
        inputs,
        [wide, wide, slim, slim, wide, slim, ids_column],
    )
    far_stats = swap(stats, half_count)
    first = call(
        functools.partial(first_head_kernel, shape),
        [half_array(3 * half_len, single)]
        + [half_array(tokens, single)] * half_count
        + [half_array(2 * tokens, single)] * half_count,
        [me],
        inputs,
        [wide, wide, slim, slim, wide, slim, ids_column, slim, slim, sums, sums, sums, sums],
    )
    results = call(
        functools.partial(second_head_kernel, shape, stat_rows),
        [half_array(3 * half_len, width)]
        + [half_array(tokens, width)] * half_count
        + [half_array(2 * tokens, single)] * half_count,
        [me],
        inputs + [stats, far_stats] + list(first),
        [wide, wide, slim, slim, wide, slim, ids_column, slim, slim, sums, sums, slim, slim],
    )
    key_grads = swap_inside(results[1 : 1 + half_count])
    far_parts = swap_across(results[1 + half_count :])
    main = exchange_inside(results[0])
    inner = call(
        functools.partial(inner_kernel, half_count),
        jax.ShapeDtypeStruct((row_count, LANES), jnp.float32),
        [me],
        [key_vectors, key_rms] + key_grads + far_parts,
    )
    inner = lax.psum(inner, "head")
    return tuple(
        call(
            functools.partial(final_kernel, half_count, feature_total),
            [half_array(tokens, features)] * 4,
            [me],
            [key_vectors, key_rms, inner] + key_grads + far_parts + [main],
        )
    )


def per_device_any(queries, key_vectors, values, cotangent, cluster, block_pattern):
    count = lax.axis_size("seq")
    tokens, features = queries.shape
    cluster_count, block_count, _ = block_pattern.shape
    fits = (
        count % 2 == 0
        and count & (count - 1) == 0
        and features % (count * HEAD_DIM) == 0
        and tokens % ID_ROWS == 0
        and tokens * count % (2 * BLK) == 0
        and cluster_count * block_count <= LANES
    )
    chosen = by_halves if fits else per_device
    return chosen(queries, key_vectors, values, cotangent, cluster, block_pattern)


def solution(mesh):
    in_specs = (
        P("seq", "head"),
        P("seq", "head"),
        P("seq", "head"),
        P("seq", "head"),
        P("seq", None),
        P(),
    )
    out_specs = (P("seq", "head"), P("seq", "head"), P("seq", "head"), P("seq", "head"))
    return jax.shard_map(
        per_device_any, mesh=mesh, in_specs=in_specs, out_specs=out_specs, check_vma=False
    )
```

profile of v0, /device:TPU:0, one launch (start us, length us, event | category | flops | bytes accessed | tf_op | source)
XLA Modules:
  0.0 98.8 jit_solution(1305451237070885286)
XLA Ops:
  5.7 5.4 %all-to-all-start = ((bf16[4,592,256]{2,1,0:T(8,128)(2,1)}), bf16[4,592,256]{2,1,0:T(8,128)(2,1)S(1)}, u32[]{:S(2)}, u32[]{:S(2)}) async-start(bf16[4,592,256]{2,1,0:T(8,128)(2,1)} %bitcast.4), calls=%async_computation | async-start | bytes 2424832 | tf_op jit(solution)/shard_map/all_to_all | solution.py:720
  11.3 6.3 %psum.14 = f32[192]{0:T(256)S(1)} all-reduce(f32[192]{0:T(256)S(1)} %multiply_reduce_fusion), channel_id=1, replica_groups=mesh['seq'=8,'head'=4] {'head'}, use_global_device_ids=true, to_apply=%region_1.2 | all-reduce | flops 192 | bytes 1536 | tf_op jit(solution)/shard_map/psum | solution.py:748
  18.1 2.1 %collective-permute-start = (bf16[192,256]{1,0:T(8,128)(2,1)S(1)}, bf16[192,256]{1,0:T(8,128)(2,1)S(1)}, u32[]{:S(2)}, u32[]{:S(2)}) collective-permute-start(bf16[192,256]{1,0:T(8,128)(2,1)S(1)} %get-tuple-element.31), channel_id=1, source_target_pairs={{0,4},{4,0},{8,12},{12,8},{16,20},{20,16},{24,28},{28,24},{1,5},{5... | collective-permute-start | bytes 294920 | tf_op jit(solution)/shard_map/ppermute | solution.py:706
  21.7 2.6 %collective-permute-start.3 = (bf16[400,128]{1,0:T(8,128)(2,1)S(1)}, bf16[400,128]{1,0:T(8,128)(2,1)S(1)}, u32[]{:S(2)}, u32[]{:S(2)}) collective-permute-start(bf16[400,128]{1,0:T(8,128)(2,1)S(1)} %get-tuple-element.34), channel_id=1, source_target_pairs={{0,16},{4,20},{8,24},{12,28},{16,0},{20,4},{24,8},{28,12},{1,17},{... | collective-permute-start | bytes 307208 | tf_op jit(solution)/shard_map/ppermute | solution.py:706
  24.3 1.7 %collective-permute-start.4 = (bf16[400,128]{1,0:T(8,128)(2,1)S(1)}, bf16[400,128]{1,0:T(8,128)(2,1)S(1)}, u32[]{:S(2)}, u32[]{:S(2)}) collective-permute-start(bf16[400,128]{1,0:T(8,128)(2,1)S(1)} %get-tuple-element.35), channel_id=1, source_target_pairs={{0,20},{4,16},{8,28},{12,24},{16,4},{20,0},{24,12},{28,8},{1,21},{... | collective-permute-start | bytes 307208 | tf_op jit(solution)/shard_map/ppermute | solution.py:706
  26.0 3.7 %collective-permute-done.refs_1_ = bf16[192,256]{1,0:T(8,128)(2,1)S(1)} collective-permute-done((bf16[192,256]{1,0:T(8,128)(2,1)S(1)}, bf16[192,256]{1,0:T(8,128)(2,1)S(1)}, u32[]{:S(2)}, u32[]{:S(2)}) %collective-permute-start) | collective-permute-done | bytes 98336 | tf_op jit(solution)/shard_map/ppermute | solution.py:706
  29.7 4.6 %collective-permute-start.5 = (bf16[400,128]{1,0:T(8,128)(2,1)S(1)}, bf16[400,128]{1,0:T(8,128)(2,1)S(1)}, u32[]{:S(2)}, u32[]{:S(2)}) collective-permute-start(bf16[400,128]{1,0:T(8,128)(2,1)S(1)} %get-tuple-element.36), channel_id=1, source_target_pairs={{0,24},{4,28},{8,16},{12,20},{16,8},{20,12},{24,0},{28,4},{1,25},{... | collective-permute-start | bytes 307208 | tf_op jit(solution)/shard_map/ppermute | solution.py:706
  34.3 3.3 %collective-permute-start.6 = (bf16[400,128]{1,0:T(8,128)(2,1)S(1)}, bf16[400,128]{1,0:T(8,128)(2,1)S(1)}, u32[]{:S(2)}, u32[]{:S(2)}) collective-permute-start(bf16[400,128]{1,0:T(8,128)(2,1)S(1)} %get-tuple-element.37), channel_id=1, source_target_pairs={{0,28},{4,24},{8,20},{12,16},{16,12},{20,8},{24,4},{28,0},{1,29},{... | collective-permute-start | bytes 307208 | tf_op jit(solution)/shard_map/ppermute | solution.py:706
  37.7 2.9 %collective-permute-done.5.refs_6_ = bf16[400,128]{1,0:T(8,128)(2,1)S(1)} collective-permute-done((bf16[400,128]{1,0:T(8,128)(2,1)S(1)}, bf16[400,128]{1,0:T(8,128)(2,1)S(1)}, u32[]{:S(2)}, u32[]{:S(2)}) %collective-permute-start.5) | collective-permute-done | bytes 102432 | tf_op jit(solution)/shard_map/ppermute | solution.py:706
  40.5 2.0 %collective-permute-done.6.refs_7_ = bf16[400,128]{1,0:T(8,128)(2,1)S(1)} collective-permute-done((bf16[400,128]{1,0:T(8,128)(2,1)S(1)}, bf16[400,128]{1,0:T(8,128)(2,1)S(1)}, u32[]{:S(2)}, u32[]{:S(2)}) %collective-permute-start.6) | collective-permute-done | bytes 102432 | tf_op jit(solution)/shard_map/ppermute | solution.py:706
  42.5 2.0 %shard_map.95.refs_8_ = f32[18,128]{1,0:T(8,128)S(1)} custom-call(s32[1]{0:T(128)} %bitcast.me_ref, f32[12,128]{1,0:T(8,128)S(1)} %pad.14.pattern_ref, bf16[2368,256]{1,0:T(8,128)(2,1)S(1)} %bitcast.11, bf16[192,256]{1,0:T(8,128)(2,1)S(1)} %get-tuple-element.30.refs_0_, bf16[192,256]{1,0:T(8,128)(2,1)S(1)} %collective-permute-done.refs_1_, ...), custom_call_target="tpu_custom_call" | custom-call | tf_op jit(solution)/shard_map/pallas_call | solution.py:692
  44.5 2.6 %collective-permute-start.7 = (f32[18,128]{1,0:T(8,128)S(1)}, f32[18,128]{1,0:T(8,128)S(1)}, u32[]{:S(2)}, u32[]{:S(2)}) collective-permute-start(f32[18,128]{1,0:T(8,128)S(1)} %shard_map.95.refs_8_), channel_id=1, source_target_pairs={{0,16},{4,20},{8,24},{12,28},{16,0},{20,4},{24,8},{28,12},{1,17},{... | collective-permute-start | bytes 27656 | tf_op jit(solution)/shard_map/ppermute | solution.py:706
  47.1 3.1 %shard_map.96 = (bf16[2304,128]{1,0:T(8,128)(2,1)S(1)}, bf16[192,128]{1,0:T(8,128)(2,1)S(1)}, bf16[192,128]{1,0:T(8,128)(2,1)S(1)}, bf16[192,128]{1,0:T(8,128)(2...) custom-call(s32[1]{0:T(128)} %bitcast.me_ref, ...), custom_call_target="tpu_custom_call" | custom-call | tf_op jit(solution)/shard_map/pallas_call | solution.py:692
  50.2 6.7 %shard_map.97 = (bf16[2304,256]{1,0:T(8,128)(2,1)}, bf16[192,256]{1,0:T(8,128)(2,1)S(1)}, bf16[192,256]{1,0:T(8,128)(2,1)S(1)}, bf16[192,256]{1,0:T(8,128)(2,1)S...) custom-call(s32[1]{0:T(128)} %bitcast.me_ref, ...), custom_call_target="tpu_custom_call" | custom-call | tf_op jit(solution)/shard_map/pallas_call | solution.py:692
  57.0 4.6 %all-to-all-start.1 = ((bf16[4,576,256]{2,1,0:T(8,128)(2,1)}), bf16[4,576,256]{2,1,0:T(8,128)(2,1)S(1)}, u32[]{:S(2)}, u32[]{:S(2)}) async-start(bf16[4,576,256]{2,1,0:T(8,128)(2,1)} %bitcast.6), calls=%async_computation.1 | async-start | bytes 2359296 | tf_op jit(solution)/shard_map/all_to_all | solution.py:720
  61.5 2.0 %collective-permute-start.8 = (bf16[192,256]{1,0:T(8,128)(2,1)S(1)}, bf16[192,256]{1,0:T(8,128)(2,1)S(1)}, u32[]{:S(2)}, u32[]{:S(2)}) collective-permute-start(bf16[192,256]{1,0:T(8,128)(2,1)S(1)} %get-tuple-element.48), channel_id=1, source_target_pairs={{0,4},{4,0},{8,12},{12,8},{16,20},{20,16},{24,28},{28,24},{1,5},{5... | collective-permute-start | bytes 294920 | tf_op jit(solution)/shard_map/ppermute | solution.py:706
  66.6 2.8 %collective-permute-start.12 = (bf16[384,128]{1,0:T(8,128)(2,1)S(1)}, bf16[384,128]{1,0:T(8,128)(2,1)S(1)}, u32[]{:S(2)}, u32[]{:S(2)}) collective-permute-start(bf16[384,128]{1,0:T(8,128)(2,1)S(1)} %get-tuple-element.52), channel_id=1, source_target_pairs={{0,20},{4,16},{8,28},{12,24},{16,4},{20,0},{24,12},{28,8},{1,21},{... | collective-permute-start | bytes 294920 | tf_op jit(solution)/shard_map/ppermute | solution.py:706
  69.4 10.0 %collective-permute-done.8.refs_1_ = bf16[192,256]{1,0:T(8,128)(2,1)S(1)} collective-permute-done((bf16[192,256]{1,0:T(8,128)(2,1)S(1)}, bf16[192,256]{1,0:T(8,128)(2,1)S(1)}, u32[]{:S(2)}, u32[]{:S(2)}) %collective-permute-start.8) | collective-permute-done | bytes 98336 | tf_op jit(solution)/shard_map/ppermute | solution.py:706
  79.4 3.3 %collective-permute-start.13 = (bf16[384,128]{1,0:T(8,128)(2,1)S(1)}, bf16[384,128]{1,0:T(8,128)(2,1)S(1)}, u32[]{:S(2)}, u32[]{:S(2)}) collective-permute-start(bf16[384,128]{1,0:T(8,128)(2,1)S(1)} %get-tuple-element.53), channel_id=1, source_target_pairs={{0,24},{4,28},{8,16},{12,20},{16,8},{20,12},{24,0},{28,4},{1,25},{... | collective-permute-start | bytes 294920 | tf_op jit(solution)/shard_map/ppermute | solution.py:706
  82.7 3.3 %collective-permute-start.14 = (bf16[384,128]{1,0:T(8,128)(2,1)S(1)}, bf16[384,128]{1,0:T(8,128)(2,1)S(1)}, u32[]{:S(2)}, u32[]{:S(2)}) collective-permute-start(bf16[384,128]{1,0:T(8,128)(2,1)S(1)} %get-tuple-element.54), channel_id=1, source_target_pairs={{0,28},{4,24},{8,20},{12,16},{16,12},{20,8},{24,4},{28,0},{1,29},{... | collective-permute-start | bytes 294920 | tf_op jit(solution)/shard_map/ppermute | solution.py:706
  86.0 2.9 %collective-permute-done.13.refs_6_ = bf16[384,128]{1,0:T(8,128)(2,1)S(1)} collective-permute-done((bf16[384,128]{1,0:T(8,128)(2,1)S(1)}, bf16[384,128]{1,0:T(8,128)(2,1)S(1)}, u32[]{:S(2)}, u32[]{:S(2)}) %collective-permute-start.13) | collective-permute-done | bytes 98336 | tf_op jit(solution)/shard_map/ppermute | solution.py:706
  88.9 1.8 %collective-permute-done.14.refs_7_ = bf16[384,128]{1,0:T(8,128)(2,1)S(1)} collective-permute-done((bf16[384,128]{1,0:T(8,128)(2,1)S(1)}, bf16[384,128]{1,0:T(8,128)(2,1)S(1)}, u32[]{:S(2)}, u32[]{:S(2)}) %collective-permute-start.14) | collective-permute-done | bytes 98336 | tf_op jit(solution)/shard_map/ppermute | solution.py:706
  91.1 6.0 %psum.15.inner_ref = f32[2,128]{1,0:T(2,128)S(1)} all-reduce(f32[2,128]{1,0:T(2,128)S(1)} %shard_map.98), channel_id=1, replica_groups=mesh['seq'=8,'head'=4] {'head'}, use_global_device_ids=true, to_apply=%region_2.3 | all-reduce | flops 256 | bytes 2048 | tf_op jit(solution)/shard_map/psum | solution.py:802
  97.1 1.7 %shard_map.99 = (bf16[192,1024]{1,0:T(8,128)(2,1)}, bf16[192,1024]{1,0:T(8,128)(2,1)}, bf16[192,1024]{1,0:T(8,128)(2,1)}, bf16[192,1024]{1,0:T(8,128)(2,1)}) custom-call(s32[1]{0:T(128)} %bitcast.me_ref, bf16[192,1024]{1,0:T(8,128)(2,1)S(1)} %copy-done, f32[2,128]{1,0:T(2,128)S(1)} %pad_bitcast_fusion.1.rms_ref, f32[2,128]{1,0:T(2,128)S(1)} %psum.15.inner_ref, ...), custom_call_target="tpu_custom_call" | custom-call | tf_op jit(solution)/shard_map/pallas_call | solution.py:692
  (43 shorter events, 10.7 us)
Async XLA Ops:
  1.3 1.0 %copy-start.1 = (bf16[192,1024]{1,0:T(8,128)(2,1)S(1)}, bf16[192,1024]{1,0:T(8,128)(2,1)}, u32[]{:S(2)}) copy-start(bf16[192,1024]{1,0:T(8,128)(2,1)} %query_ref.3) | copy-start | bytes 1179652
  2.3 1.0 %copy-start.3 = (bf16[192,1024]{1,0:T(8,128)(2,1)S(1)}, bf16[192,1024]{1,0:T(8,128)(2,1)}, u32[]{:S(2)}) copy-start(bf16[192,1024]{1,0:T(8,128)(2,1)} %value_ref.3) | copy-start | bytes 1179652
  5.7 5.4 %copy-start = (bf16[192,1024]{1,0:T(8,128)(2,1)S(1)}, bf16[192,1024]{1,0:T(8,128)(2,1)}, u32[]{:S(2)}) copy-start(bf16[192,1024]{1,0:T(8,128)(2,1)} %key_ref.5) | copy-start | bytes 1179652
  5.7 12.0 %copy-start.2 = (bf16[192,1024]{1,0:T(8,128)(2,1)S(1)}, bf16[192,1024]{1,0:T(8,128)(2,1)}, u32[]{:S(2)}) copy-start(bf16[192,1024]{1,0:T(8,128)(2,1)} %query_ref.3) | copy-start | bytes 1179652
  5.7 11.9 %copy-start.4 = (bf16[192,1024]{1,0:T(8,128)(2,1)S(1)}, bf16[192,1024]{1,0:T(8,128)(2,1)}, u32[]{:S(2)}) copy-start(bf16[192,1024]{1,0:T(8,128)(2,1)} %value_ref.3) | copy-start | bytes 1179652
  5.7 11.9 %copy-start.6 = (bf16[192,1024]{1,0:T(8,128)(2,1)S(1)}, bf16[192,1024]{1,0:T(8,128)(2,1)}, u32[]{:S(2)}) copy-start(bf16[192,1024]{1,0:T(8,128)(2,1)} %grad_ref.3) | copy-start | bytes 1179652
  5.7 36.8 %all-to-all-start = ((bf16[4,592,256]{2,1,0:T(8,128)(2,1)}), bf16[4,592,256]{2,1,0:T(8,128)(2,1)S(1)}, u32[]{:S(2)}, u32[]{:S(2)}) async-start(bf16[4,592,256]{2,1,0:T(8,128)(2,1)} %bitcast.4), calls=%async_computation | async-start | bytes 2424832 | tf_op jit(solution)/shard_map/all_to_all | solution.py:720
  11.1 26.4 %copy-start.7 = (s32[2,12,12]{2,0,1:T(2,128)S(1)}, s32[2,12,12]{2,0,1:T(2,128)}, u32[]{:S(2)}) copy-start(s32[2,12,12]{2,0,1:T(2,128)} %param.11) | copy-start | bytes 3460
  18.1 11.6 %collective-permute-start = (bf16[192,256]{1,0:T(8,128)(2,1)S(1)}, bf16[192,256]{1,0:T(8,128)(2,1)S(1)}, u32[]{:S(2)}, u32[]{:S(2)}) collective-permute-start(bf16[192,256]{1,0:T(8,128)(2,1)S(1)} %get-tuple-element.31), channel_id=1, source_target_pairs={{0,4},{4,0},{8,12},{12,8},{16,20},{20,16},{24,28},{28,24},{1,5},{5... | collective-permute-start | bytes 294920 | tf_op jit(solution)/shard_map/ppermute | solution.py:706
  20.1 14.1 %collective-permute-start.1 = (bf16[192,256]{1,0:T(8,128)(2,1)S(1)}, bf16[192,256]{1,0:T(8,128)(2,1)S(1)}, u32[]{:S(2)}, u32[]{:S(2)}) collective-permute-start(bf16[192,256]{1,0:T(8,128)(2,1)S(1)} %get-tuple-element.32), channel_id=1, source_target_pairs={{0,8},{4,12},{8,0},{12,4},{16,24},{20,28},{24,16},{28,20},{1,9},{5... | collective-permute-start | bytes 294920 | tf_op jit(solution)/shard_map/ppermute | solution.py:706
  21.6 16.1 %collective-permute-start.2 = (bf16[192,256]{1,0:T(8,128)(2,1)S(1)}, bf16[192,256]{1,0:T(8,128)(2,1)S(1)}, u32[]{:S(2)}, u32[]{:S(2)}) collective-permute-start(bf16[192,256]{1,0:T(8,128)(2,1)S(1)} %get-tuple-element.33), channel_id=1, source_target_pairs={{0,12},{4,8},{8,4},{12,0},{16,28},{20,24},{24,20},{28,16},{1,13},{... | collective-permute-start | bytes 294920 | tf_op jit(solution)/shard_map/ppermute | solution.py:706
  21.7 16.0 %collective-permute-start.3 = (bf16[400,128]{1,0:T(8,128)(2,1)S(1)}, bf16[400,128]{1,0:T(8,128)(2,1)S(1)}, u32[]{:S(2)}, u32[]{:S(2)}) collective-permute-start(bf16[400,128]{1,0:T(8,128)(2,1)S(1)} %get-tuple-element.34), channel_id=1, source_target_pairs={{0,16},{4,20},{8,24},{12,28},{16,0},{20,4},{24,8},{28,12},{1,17},{... | collective-permute-start | bytes 307208 | tf_op jit(solution)/shard_map/ppermute | solution.py:706
  24.3 13.4 %collective-permute-start.4 = (bf16[400,128]{1,0:T(8,128)(2,1)S(1)}, bf16[400,128]{1,0:T(8,128)(2,1)S(1)}, u32[]{:S(2)}, u32[]{:S(2)}) collective-permute-start(bf16[400,128]{1,0:T(8,128)(2,1)S(1)} %get-tuple-element.35), channel_id=1, source_target_pairs={{0,20},{4,16},{8,28},{12,24},{16,4},{20,0},{24,12},{28,8},{1,21},{... | collective-permute-start | bytes 307208 | tf_op jit(solution)/shard_map/ppermute | solution.py:706
  29.7 10.9 %collective-permute-start.5 = (bf16[400,128]{1,0:T(8,128)(2,1)S(1)}, bf16[400,128]{1,0:T(8,128)(2,1)S(1)}, u32[]{:S(2)}, u32[]{:S(2)}) collective-permute-start(bf16[400,128]{1,0:T(8,128)(2,1)S(1)} %get-tuple-element.36), channel_id=1, source_target_pairs={{0,24},{4,28},{8,16},{12,20},{16,8},{20,12},{24,0},{28,4},{1,25},{... | collective-permute-start | bytes 307208 | tf_op jit(solution)/shard_map/ppermute | solution.py:706
  34.3 8.3 %collective-permute-start.6 = (bf16[400,128]{1,0:T(8,128)(2,1)S(1)}, bf16[400,128]{1,0:T(8,128)(2,1)S(1)}, u32[]{:S(2)}, u32[]{:S(2)}) collective-permute-start(bf16[400,128]{1,0:T(8,128)(2,1)S(1)} %get-tuple-element.37), channel_id=1, source_target_pairs={{0,28},{4,24},{8,20},{12,16},{16,12},{20,8},{24,4},{28,0},{1,29},{... | collective-permute-start | bytes 307208 | tf_op jit(solution)/shard_map/ppermute | solution.py:706
  44.5 5.7 %collective-permute-start.7 = (f32[18,128]{1,0:T(8,128)S(1)}, f32[18,128]{1,0:T(8,128)S(1)}, u32[]{:S(2)}, u32[]{:S(2)}) collective-permute-start(f32[18,128]{1,0:T(8,128)S(1)} %shard_map.95.refs_8_), channel_id=1, source_target_pairs={{0,16},{4,20},{8,24},{12,28},{16,0},{20,4},{24,8},{28,12},{1,17},{... | collective-permute-start | bytes 27656 | tf_op jit(solution)/shard_map/ppermute | solution.py:706
  57.0 40.1 %all-to-all-start.1 = ((bf16[4,576,256]{2,1,0:T(8,128)(2,1)}), bf16[4,576,256]{2,1,0:T(8,128)(2,1)S(1)}, u32[]{:S(2)}, u32[]{:S(2)}) async-start(bf16[4,576,256]{2,1,0:T(8,128)(2,1)} %bitcast.6), calls=%async_computation.1 | async-start | bytes 2359296 | tf_op jit(solution)/shard_map/all_to_all | solution.py:720
  61.5 17.9 %collective-permute-start.8 = (bf16[192,256]{1,0:T(8,128)(2,1)S(1)}, bf16[192,256]{1,0:T(8,128)(2,1)S(1)}, u32[]{:S(2)}, u32[]{:S(2)}) collective-permute-start(bf16[192,256]{1,0:T(8,128)(2,1)S(1)} %get-tuple-element.48), channel_id=1, source_target_pairs={{0,4},{4,0},{8,12},{12,8},{16,20},{20,16},{24,28},{28,24},{1,5},{5... | collective-permute-start | bytes 294920 | tf_op jit(solution)/shard_map/ppermute | solution.py:706
  63.6 19.2 %collective-permute-start.9 = (bf16[192,256]{1,0:T(8,128)(2,1)S(1)}, bf16[192,256]{1,0:T(8,128)(2,1)S(1)}, u32[]{:S(2)}, u32[]{:S(2)}) collective-permute-start(bf16[192,256]{1,0:T(8,128)(2,1)S(1)} %get-tuple-element.49), channel_id=1, source_target_pairs={{0,8},{4,12},{8,0},{12,4},{16,24},{20,28},{24,16},{28,20},{1,9},{5... | collective-permute-start | bytes 294920 | tf_op jit(solution)/shard_map/ppermute | solution.py:706
  65.0 21.0 %collective-permute-start.10 = (bf16[192,256]{1,0:T(8,128)(2,1)S(1)}, bf16[192,256]{1,0:T(8,128)(2,1)S(1)}, u32[]{:S(2)}, u32[]{:S(2)}) collective-permute-start(bf16[192,256]{1,0:T(8,128)(2,1)S(1)} %get-tuple-element.50), channel_id=1, source_target_pairs={{0,12},{4,8},{8,4},{12,0},{16,28},{20,24},{24,20},{28,16},{1,13},{... | collective-permute-start | bytes 294920 | tf_op jit(solution)/shard_map/ppermute | solution.py:706
  65.0 21.0 %collective-permute-start.11 = (bf16[384,128]{1,0:T(8,128)(2,1)S(1)}, bf16[384,128]{1,0:T(8,128)(2,1)S(1)}, u32[]{:S(2)}, u32[]{:S(2)}) collective-permute-start(bf16[384,128]{1,0:T(8,128)(2,1)S(1)} %get-tuple-element.51), channel_id=1, source_target_pairs={{0,16},{4,20},{8,24},{12,28},{16,0},{20,4},{24,8},{28,12},{1,17},{... | collective-permute-start | bytes 294920 | tf_op jit(solution)/shard_map/ppermute | solution.py:706
  66.6 19.4 %collective-permute-start.12 = (bf16[384,128]{1,0:T(8,128)(2,1)S(1)}, bf16[384,128]{1,0:T(8,128)(2,1)S(1)}, u32[]{:S(2)}, u32[]{:S(2)}) collective-permute-start(bf16[384,128]{1,0:T(8,128)(2,1)S(1)} %get-tuple-element.52), channel_id=1, source_target_pairs={{0,20},{4,16},{8,28},{12,24},{16,4},{20,0},{24,12},{28,8},{1,21},{... | collective-permute-start | bytes 294920 | tf_op jit(solution)/shard_map/ppermute | solution.py:706
  79.4 9.5 %collective-permute-start.13 = (bf16[384,128]{1,0:T(8,128)(2,1)S(1)}, bf16[384,128]{1,0:T(8,128)(2,1)S(1)}, u32[]{:S(2)}, u32[]{:S(2)}) collective-permute-start(bf16[384,128]{1,0:T(8,128)(2,1)S(1)} %get-tuple-element.53), channel_id=1, source_target_pairs={{0,24},{4,28},{8,16},{12,20},{16,8},{20,12},{24,0},{28,4},{1,25},{... | collective-permute-start | bytes 294920 | tf_op jit(solution)/shard_map/ppermute | solution.py:706
  82.7 8.0 %collective-permute-start.14 = (bf16[384,128]{1,0:T(8,128)(2,1)S(1)}, bf16[384,128]{1,0:T(8,128)(2,1)S(1)}, u32[]{:S(2)}, u32[]{:S(2)}) collective-permute-start(bf16[384,128]{1,0:T(8,128)(2,1)S(1)} %get-tuple-element.54), channel_id=1, source_target_pairs={{0,28},{4,24},{8,20},{12,16},{16,12},{20,8},{24,4},{28,0},{1,29},{... | collective-permute-start | bytes 294920 | tf_op jit(solution)/shard_map/ppermute | solution.py:706
  (1 other events, 1.0 us)
where the time goes:
time: 100 us; the launch traced here: 98.8 us
  starting transfers between devices  42.8 us (43%)
  waiting for transfers between devices  23.3 us (23%)
  Pallas kernels  15.6 us (16%)
  blocking collectives  12.4 us (12%)
  local copies, waits for them, and re-layouts  3.11 us (3%)
    ppermute x15, starting transfers between devices, swap(): return lax.ppermute(block, 'seq', [(i, i ^ distance) for i in range(count)])  32.8 us
    ppermute x15, waiting for transfers between devices, swap(): return lax.ppermute(block, 'seq', [(i, i ^ distance) for i in range(count)])  23.3 us
    pallas_call x7, Pallas kernels, call(): pl.pallas_call(kernel, out_shape=out_shapes, in_specs=[pl.BlockSpec(memor...  15.6 us
    all_to_all x2, starting transfers between devices, exchange_inside(): lax.all_to_all(rows, 'seq', split_axis=0, concat_axis=0, tiled=True, axis...  9.94 us
    psum x1, blocking collectives, by_halves(): square_sum = lax.psum(jnp.sum(key_float * key_float, axis=1), 'head')  6.34 us
    psum x1, blocking collectives, by_halves(): inner = lax.psum(inner, 'head')  6.04 us
    unnamed x16, local copies, waits for them, and re-layouts  3.01 us
  transfers between devices with their start and end apart: 17, of which 6 were waited for; matrix products, arithmetic and copies ran while one was open for 0% of the time, Pallas kernels for 4%

commit v1 on v0

--- a/solution.py
+++ b/solution.py
@@ -20,7 +20,8 @@
 LANES = 128
 ID_ROWS = 16
 QUERY_TILE = 256
-VMEM_BYTES = 48 << 20
+VMEM_BYTES = 32 << 20
+PACK_VMEM_BYTES = 60 << 20
 
 
 def contract_last(left_side, right_side):
@@ -174,21 +175,18 @@
     return (home_rows[0], home_rows[1], key_grad, home_rows[3])
 
 
-def row_to_column(row, count):
-    lanes = row.shape[1]
-    diagonal = lax.broadcasted_iota(jnp.int32, (lanes, lanes), 0) == lax.broadcasted_iota(
-        jnp.int32, (lanes, lanes), 1
-    )
-    spread = jnp.where(diagonal, jnp.broadcast_to(row, (lanes, lanes)), 0.0)
-    return jnp.sum(spread, axis=1, keepdims=True)[:count]
-
-
-def column_of(rows_ref, first_row, count):
+def column_of(rows, first_row, count):
+    turned = jnp.transpose(rows)
     pieces = []
     for start in range(0, count, LANES):
-        row = rows_ref[first_row + start // LANES : first_row + start // LANES + 1, :LANES]
-        pieces.append(row_to_column(row.astype(jnp.float32), min(LANES, count - start)))
+        place = first_row + start // LANES
+        pieces.append(turned[: min(LANES, count - start), place : place + 1])
     return jnp.concatenate(pieces, axis=0)
+
+
+def ids_of(ref, first_row, count):
+    rows = ref[first_row : first_row + ID_ROWS, :LANES].astype(jnp.float32)
+    return column_of(rows, 0, count)
 
 
 def store_as_rows(out_ref, first_row, column):
@@ -207,26 +205,26 @@
     return pl.ds(pl.multiple_of(index * size, 16), size)
 
 
-def pack_kernel(half_count, query_ref, value_ref, grad_ref, ids_ref, out_ref, sems):
+def pack_kernel(half_count, query_ref, value_ref, grad_ref, out_ref, held, sorted_rows, in_sems, out_sems):
     tokens, features = query_ref.shape
     width = features // half_count
-    stride = 3 * tokens + ID_ROWS
+    arrivals = [
+        pltpu.make_async_copy(source_ref, held.at[place], in_sems.at[place])
+        for place, source_ref in enumerate((query_ref, value_ref, grad_ref))
+    ]
+    for arrival in arrivals:
+        arrival.start()
     copies = []
-    for place, source_ref in enumerate((query_ref, value_ref, grad_ref)):
+    for place, arrival in enumerate(arrivals):
+        arrival.wait()
         for owner in range(half_count):
-            copies.append(
-                pltpu.make_async_copy(
-                    source_ref.at[:, owner * width : (owner + 1) * width],
-                    out_ref.at[pl.ds(owner * stride + place * tokens, tokens), :],
-                    sems.at[place * half_count + owner],
-                )
+            rows = pl.ds((owner * 3 + place) * tokens, tokens)
+            sorted_rows[rows, :] = held[place, :, owner * width : (owner + 1) * width]
+            copy = pltpu.make_async_copy(
+                sorted_rows.at[rows, :], out_ref.at[rows, :], out_sems.at[place * half_count + owner]
             )
-    for copy in copies:
-        copy.start()
-    for owner in range(half_count):
-        rows = slice(owner * stride + 3 * tokens, (owner + 1) * stride)
-        out_ref[rows, :LANES] = ids_ref[...]
-        out_ref[rows, LANES:] = jnp.zeros((ID_ROWS, width - LANES), jnp.bfloat16)
+            copy.start()
+            copies.append(copy)
     for copy in copies:
         copy.wait()
 
@@ -240,7 +238,7 @@
     is_high = me_ref[0] >= half_count
     inside = me_ref[0] & (half_count - 1)
     key_refs, cross_refs = out_refs[:half_count], out_refs[half_count:]
-    rms = column_of(rms_ref, 0, tokens)
+    rms = column_of(rms_ref[...], 0, tokens)
 
     def normed_columns(first, size):
         return (key_ref[:, pl.ds(first, size)].astype(jnp.float32) / rms).astype(jnp.bfloat16)
@@ -248,7 +246,9 @@
     for distance in range(half_count):
         first = pl.multiple_of((inside ^ distance) * width, LANES)
         cross_ref = cross_refs[distance]
-        key_refs[distance][...] = normed_columns(first, width)
+        key_refs[distance][:tokens, :] = normed_columns(first, width)
+        key_refs[distance][tokens:, :LANES] = ids_ref[...]
+        key_refs[distance][tokens:, LANES:] = jnp.zeros((ID_ROWS, width - LANES), jnp.bfloat16)
         cross_ref[2 * tokens :, :LANES] = ids_ref[...]
         if single > LANES:
             cross_ref[2 * tokens :, LANES:] = jnp.zeros((ID_ROWS, single - LANES), jnp.bfloat16)
@@ -282,15 +282,14 @@
         self.lane_cluster = lane_cluster.astype(jnp.float32)
 
     def own_ids(self, ids_all):
-        stride = 3 * self.tokens + ID_ROWS
-        for source in range(self.half_count):
-            ids_all[source * self.tokens : (source + 1) * self.tokens, :] = column_of(
-                self.packed_ref, source * stride + 3 * self.tokens, self.tokens
+        for distance in range(self.half_count):
+            ids_all[block_rows(self.inside ^ distance, self.tokens), :] = ids_of(
+                self.key_refs[distance], self.tokens, self.tokens
             )
 
     def cross_ids(self, ids_all):
         for distance in range(self.half_count):
-            ids_all[block_rows(self.inside ^ distance, self.tokens), :] = column_of(
+            ids_all[block_rows(self.inside ^ distance, self.tokens), :] = ids_of(
                 self.cross_refs[distance], 2 * self.tokens, self.tokens
             )
 
@@ -313,7 +312,7 @@
 
     def own(self, column, query_all, key_all, value_all, grad_all):
         columns = slice(column, column + HEAD_DIM)
-        stride = 3 * self.tokens + ID_ROWS
+        stride = 3 * self.tokens
         for source in range(self.half_count):
             rows = slice(source * self.tokens, (source + 1) * self.tokens)
             for place, target in enumerate((query_all, value_all, grad_all)):
@@ -321,7 +320,7 @@
                 target[rows, :HEAD_DIM] = self.packed_ref[first : first + self.tokens, columns]
         for distance in range(self.half_count):
             rows = block_rows(self.inside ^ distance, self.tokens)
-            key_all[rows, :HEAD_DIM] = self.key_refs[distance][:, columns]
+            key_all[rows, :HEAD_DIM] = self.key_refs[distance][: self.tokens, columns]
 
     def cross(self, column, first_all, second_all):
         columns = slice(column, column + HEAD_DIM)
@@ -393,12 +392,15 @@
     return [(first, slice(first, first + tile), first + tile) for first in range(0, half_len, tile)]
 
 
+def note_stats(out_ref, stat_rows, head, first, found):
+    for place, column in enumerate(found[1:]):
+        store_as_rows(out_ref, (3 * head + place) * stat_rows + first // LANES, column)
+
+
 def stats_kernel(shape, stat_rows, me_ref, pattern_ref, packed_ref, *refs):
     half_count = shape[1]
-    key_refs, cross_refs = refs[:half_count], refs[half_count : 2 * half_count]
-    out_ref, query_all, key_all, value_all, grad_all, other_query, other_grad, ids = refs[
-        2 * half_count :
-    ]
+    cross_refs, key_refs = refs[:half_count], refs[half_count : 2 * half_count]
+    out_ref, query_all, key_all, value_all, grad_all, ids, other_ids = refs[2 * half_count :]
     slots = Slots(shape, me_ref, pattern_ref, packed_ref, key_refs, cross_refs)
     single = packed_ref.shape[1] // 2
     out_ref[...] = jnp.zeros_like(out_ref)
@@ -411,101 +413,90 @@
 
     @pl.when(jnp.logical_not(slots.is_high))
     def _():
-        slots.cross_ids(ids)
-        slots.query_features(ids, other_query, 1)
+        slots.cross_ids(other_ids)
+        slots.query_features(other_ids, query_all, 1)
 
     for head in range(single // HEAD_DIM):
-        slots.own(single + head * HEAD_DIM, query_all, key_all, value_all, grad_all)
-        first_row = 3 * stat_rows * head
-
-        def note(first, found):
-            for place, column in enumerate(found[1:]):
-                store_as_rows(
-                    out_ref, first_row + place * stat_rows + first // LANES, column
-                )
+        column = head * HEAD_DIM
+        slots.own(single + column, query_all, key_all, value_all, grad_all)
+
+        def note(first, rows, limit, causal_from):
+            pieces = [(key_all, value_all, limit, causal_from)]
+            scores = tile_scores(query_all[rows, :], pieces)
+            prob_grad = contract_last(grad_all[rows, :], value_all[:limit, :])
+            for place, found in enumerate(tile_stats(scores, [prob_grad])[1:]):
+                store_as_rows(out_ref, (3 * head + place) * stat_rows + first // LANES, found)
 
         @pl.when(slots.is_high)
         def _():
             for first, rows, limit in own_tiles(slots.half_len):
-                pieces = [(key_all, value_all, limit, first)]
-                scores = tile_scores(query_all[rows, :], pieces)
-                prob_grad = contract_last(grad_all[rows, :], value_all[:limit, :])
-                note(first, tile_stats(scores, [prob_grad]))
+                note(first, rows, limit, first)
 
         @pl.when(jnp.logical_not(slots.is_high))
         def _():
-            slots.cross(head * HEAD_DIM, other_query, other_grad)
+            slots.cross(column, query_all, grad_all)
             for first, rows, _ in own_tiles(slots.half_len):
-                pieces = [(key_all, value_all, slots.half_len, None)]
-                scores = tile_scores(other_query[rows, :], pieces)
-                prob_grad = contract_last(other_grad[rows, :], value_all[...])
-                note(first, tile_stats(scores, [prob_grad]))
-
-
-def store_own(slots, result_ref, key_refs, column, results, key_sum, value_sum):
-    attended, query_grad = results
+                note(first, rows, slots.half_len, None)
+
+
+def store_own(slots, result_refs, column, attended, query_grad, value_sum, key_sum):
     tokens = slots.tokens
     columns = slice(column, column + HEAD_DIM)
-    stride = result_ref.shape[0] // slots.half_count
-    for source in range(slots.half_count):
-        rows = slice(source * tokens, (source + 1) * tokens)
-        first = source * stride
-        result_ref[first : first + tokens, columns] = attended[rows, :]
-        result_ref[first + tokens : first + 2 * tokens, columns] = query_grad[rows, :]
-        result_ref[first + 2 * tokens : first + 3 * tokens, columns] = value_sum[rows, :].astype(
-            jnp.bfloat16
-        )
-    for distance in range(slots.half_count):
+    for distance, target in enumerate(result_refs):
         rows = block_rows(slots.inside ^ distance, tokens)
-        key_refs[distance][:, columns] = (key_sum[rows, :] * SCORE_SCALE).astype(jnp.bfloat16)
-
-
-def first_head_kernel(shape, me_ref, pattern_ref, packed_ref, *refs):
+        target[:tokens, columns] = attended[rows, :]
+        target[tokens : 2 * tokens, columns] = query_grad[rows, :]
+        target[2 * tokens : 3 * tokens, columns] = value_sum[rows, :].astype(jnp.bfloat16)
+        target[3 * tokens :, columns] = (key_sum[rows, :] * SCORE_SCALE).astype(jnp.bfloat16)
+
+
+def first_kernel(shape, me_ref, pattern_ref, packed_ref, *refs):
     half_count = shape[1]
-    key_refs, cross_refs = refs[:half_count], refs[half_count : 2 * half_count]
-    refs = refs[2 * half_count :]
-    result_ref, key_out_refs, cross_out_refs = (
-        refs[0], refs[1 : 1 + half_count], refs[1 + half_count : 1 + 2 * half_count]
-    )
-    (query_all, key_all, value_all, grad_all, other_key, other_value, ids, attended, query_grad,
-     key_sum, value_sum, other_key_sum, other_value_sum) = refs[1 + 2 * half_count :]
+    cross_refs, key_refs = refs[:half_count], refs[half_count : 2 * half_count]
+    refs = refs[2 * half_count + 1 :]
+    result_refs, cross_out_refs = refs[:half_count], refs[half_count : 2 * half_count]
+    second_ref, sums_ref = refs[2 * half_count : 2 * half_count + 2]
+    (query_all, key_all, value_all, grad_all, other_key, other_value, ids, other_ids, attended,
+     query_grad, key_sum, value_sum, other_key_sum, other_value_sum) = refs[2 * half_count + 2 :]
     slots = Slots(shape, me_ref, pattern_ref, packed_ref, key_refs, cross_refs)
     single = packed_ref.shape[1] // 2
+    half_len = slots.half_len
     high = slots.is_high.astype(jnp.int32)
     slots.own_ids(ids)
     slots.key_features(ids, key_all, high)
     slots.query_features(ids, query_all, high)
 
+    def run(others, other_sums, attended_out, query_grad_out, key_out, value_out):
+        for first, rows, limit in own_tiles(half_len):
+            attended_out[rows, :], query_grad_out[rows, :] = tile_backward(
+                query_all[rows, :],
+                grad_all[rows, :],
+                others + [(key_all, value_all, limit, first)],
+                other_sums + [(key_out, value_out)],
+                None,
+                first == 0,
+            )
+
     @pl.when(slots.is_high)
     def _():
-        slots.cross_ids(ids)
-        slots.key_features(ids, other_key, 0)
+        slots.cross_ids(other_ids)
+        slots.key_features(other_ids, other_key, 0)
 
     for head in range(single // HEAD_DIM):
         column = head * HEAD_DIM
+        columns = slice(column, column + HEAD_DIM)
         slots.own(column, query_all, key_all, value_all, grad_all)
-
-        def run(others, other_sums):
-            for first, rows, limit in own_tiles(slots.half_len):
-                attended[rows, :], query_grad[rows, :] = tile_backward(
-                    query_all[rows, :],
-                    grad_all[rows, :],
-                    others + [(key_all, value_all, limit, first)],
-                    other_sums + [(key_sum, value_sum)],
-                    None,
-                    first == 0,
-                )
 
         @pl.when(slots.is_high)
         def _():
             slots.cross(column, other_key, other_value)
             run(
-                [(other_key, other_value, slots.half_len, None)],
+                [(other_key, other_value, half_len, None)],
                 [(other_key_sum, other_value_sum)],
+                attended, query_grad, key_sum, value_sum,
             )
             for distance in range(half_count):
                 rows = block_rows(slots.inside ^ distance, slots.tokens)
-                columns = slice(column, column + HEAD_DIM)
                 target = cross_out_refs[distance]
                 target[: slots.tokens, columns] = (other_key_sum[rows, :] * SCORE_SCALE).astype(
                     jnp.bfloat16
@@ -514,155 +505,167 @@
 
         @pl.when(jnp.logical_not(slots.is_high))
         def _():
-            run([], [])
-            for distance in range(half_count):
-                cross_out_refs[distance][...] = jnp.zeros_like(cross_out_refs[distance])
-
-        store_own(slots, result_ref, key_out_refs, column, (attended, query_grad), key_sum, value_sum)
+            run([], [], attended, query_grad, key_sum, value_sum)
+
+        store_own(slots, result_refs, column, attended, query_grad, value_sum, key_sum)
+
+        @pl.when(jnp.logical_not(slots.is_high))
+        def _():
+            slots.own(single + column, query_all, key_all, value_all, grad_all)
+            run(
+                [], [],
+                second_ref.at[:half_len, columns],
+                second_ref.at[half_len:, columns],
+                sums_ref.at[:half_len, columns],
+                sums_ref.at[half_len:, columns],
+            )
+
+
+def joint_rows(stat_rows, head, own_stats_ref, far_stats_ref):
+    (own_max, own_total, own_delta), (far_max, far_total, far_delta) = [
+        [
+            ref[(3 * head + place) * stat_rows : (3 * head + place + 1) * stat_rows, :]
+            for place in range(3)
+        ]
+        for ref in (own_stats_ref, far_stats_ref)
+    ]
+    row_max = jnp.maximum(own_max, far_max)
+    own_part = jnp.exp2((own_max - row_max) * EXPONENT_SCALE)
+    far_part = jnp.exp2((far_max - row_max) * EXPONENT_SCALE)
+    inverse = 1.0 / jnp.maximum(own_total * own_part + far_total * far_part, 1.0)
+    return row_max, inverse, (own_delta * own_part + far_delta * far_part) * inverse
 
 
 def second_head_kernel(shape, stat_rows, me_ref, pattern_ref, packed_ref, *refs):
     half_count = shape[1]
-    key_refs, cross_refs = refs[:half_count], refs[half_count : 2 * half_count]
-    own_stats_ref, other_stats_ref, first_result_ref = refs[2 * half_count : 2 * half_count + 3]
-    refs = refs[2 * half_count + 3 :]
-    first_key_refs, first_cross_refs = refs[:half_count], refs[half_count : 2 * half_count]
-    refs = refs[2 * half_count :]
-    result_ref, key_out_refs, cross_out_refs = (
-        refs[0], refs[1 : 1 + half_count], refs[1 + half_count : 1 + 2 * half_count]
-    )
-    (query_all, key_all, value_all, grad_all, other_query, other_grad, ids, attended, query_grad,
-     key_sum, value_sum, other_attended, other_query_grad) = refs[1 + 2 * half_count :]
+    cross_refs, key_refs = refs[:half_count], refs[half_count : 2 * half_count]
+    own_stats_ref, far_stats_ref, early_ref, sums_ref = refs[2 * half_count : 2 * half_count + 4]
+    refs = refs[2 * half_count + 4 :]
+    first_cross_refs, result_refs, cross_out_refs = [
+        refs[place * half_count : (place + 1) * half_count] for place in range(3)
+    ]
+    (query_all, key_all, value_all, grad_all, other_query, other_grad, ids, other_ids, attended,
+     query_grad, key_sum, value_sum, other_attended, other_query_grad) = refs[3 * half_count :]
     slots = Slots(shape, me_ref, pattern_ref, packed_ref, key_refs, cross_refs)
     single = packed_ref.shape[1] // 2
-    high = slots.is_high.astype(jnp.int32)
+    half_len, tokens = slots.half_len, slots.tokens
     slots.own_ids(ids)
-    slots.key_features(ids, key_all, high)
-    slots.query_features(ids, query_all, high)
+    slots.key_features(ids, key_all, slots.is_high.astype(jnp.int32))
+
+    @pl.when(slots.is_high)
+    def _():
+        slots.query_features(ids, query_all, 1)
+        for distance in range(half_count):
+            cross_out_refs[distance][...] = first_cross_refs[distance][...]
 
     @pl.when(jnp.logical_not(slots.is_high))
     def _():
-        slots.cross_ids(ids)
-        slots.query_features(ids, other_query, 1)
-
-    result_ref[:, :single] = first_result_ref[...]
-    for distance in range(half_count):
-        key_out_refs[distance][:, :single] = first_key_refs[distance][...]
-
-    def joint_stats(head, first, size):
-        found = [
-            [
-                column_of(
-                    ref, 3 * stat_rows * head + place * stat_rows + first // LANES, size
-                )
-                for place in range(3)
-            ]
-            for ref in (own_stats_ref, other_stats_ref)
-        ]
-        (own_max, own_total, own_delta), (far_max, far_total, far_delta) = found
-        row_max = jnp.maximum(own_max, far_max)
-        own_part = jnp.exp2((own_max - row_max) * EXPONENT_SCALE)
-        far_part = jnp.exp2((far_max - row_max) * EXPONENT_SCALE)
-        inverse = 1.0 / jnp.maximum(own_total * own_part + far_total * far_part, 1.0)
-        return row_max, inverse, (own_delta * own_part + far_delta * far_part) * inverse
+        slots.cross_ids(other_ids)
+        slots.query_features(other_ids, other_query, 1)
 
     for head in range(single // HEAD_DIM):
         column = head * HEAD_DIM
+        columns = slice(column, column + HEAD_DIM)
         slots.own(single + column, query_all, key_all, value_all, grad_all)
-
-        def run(joint):
-            for first, rows, limit in own_tiles(slots.half_len):
+        joint_table = joint_rows(stat_rows, head, own_stats_ref, far_stats_ref)
+
+        def joint_stats(first, size):
+            return [column_of(rows, first // LANES, size) for rows in joint_table]
+
+        @pl.when(slots.is_high)
+        def _():
+            for first, rows, limit in own_tiles(half_len):
                 attended[rows, :], query_grad[rows, :] = tile_backward(
                     query_all[rows, :],
                     grad_all[rows, :],
                     [(key_all, value_all, limit, first)],
                     [(key_sum, value_sum)],
-                    joint_stats(head, first, limit - first) if joint else None,
+                    joint_stats(first, limit - first),
                     first == 0,
                 )
-
-        @pl.when(slots.is_high)
-        def _():
-            run(True)
-            for distance in range(half_count):
-                cross_out_refs[distance][...] = first_cross_refs[distance][...]
 
         @pl.when(jnp.logical_not(slots.is_high))
         def _():
             slots.cross(column, other_query, other_grad)
-            run(False)
-            for first, rows, limit in own_tiles(slots.half_len):
+            attended[...] = early_ref[:half_len, columns]
+            query_grad[...] = early_ref[half_len:, columns]
+            key_sum[...] = sums_ref[:half_len, columns]
+            value_sum[...] = sums_ref[half_len:, columns]
+            for first, rows, limit in own_tiles(half_len):
                 other_attended[rows, :], other_query_grad[rows, :] = tile_backward(
                     other_query[rows, :],
                     other_grad[rows, :],
-                    [(key_all, value_all, slots.half_len, None)],
+                    [(key_all, value_all, half_len, None)],
                     [(key_sum, value_sum)],
-                    joint_stats(head, first, limit - first),
+                    joint_stats(first, limit - first),
                     False,
                 )
             for distance in range(half_count):
-                rows = block_rows(slots.inside ^ distance, slots.tokens)
-                columns = slice(column, column + HEAD_DIM)
+                rows = block_rows(slots.inside ^ distance, tokens)
                 target = cross_out_refs[distance]
-                target[: slots.tokens, columns] = other_attended[rows, :]
-                target[slots.tokens :, columns] = other_query_grad[rows, :]
-
-        store_own(
-            slots, result_ref, key_out_refs, single + column, (attended, query_grad), key_sum,
-            value_sum,
-        )
-
-
-def normed_grad_of(half_count, me_ref, key_grad_refs, cross_refs, distance, tokens):
-    single = key_grad_refs[distance].shape[1] // 2
+                target[:tokens, columns] = other_attended[rows, :]
+                target[tokens:, columns] = other_query_grad[rows, :]
+
+        store_own(slots, result_refs, column, attended, query_grad, value_sum, key_sum)
+
+
+def normed_grad_of(half_count, me_ref, first_ref, second_ref, cross_ref):
+    tokens = second_ref.shape[0] // 4
     is_low = me_ref[0] < half_count
-    grad_float = key_grad_refs[distance][...].astype(jnp.float32)
-    far = jnp.where(is_low, cross_refs[distance][:tokens, :].astype(jnp.float32), 0.0)
-    return jnp.concatenate([grad_float[:, :single] + far, grad_float[:, single:]], axis=1)
+    far = jnp.where(is_low, cross_ref[:tokens, :].astype(jnp.float32), 0.0)
+    first_float = first_ref[3 * tokens :, :].astype(jnp.float32) + far
+    second_float = second_ref[3 * tokens :, :].astype(jnp.float32)
+    return jnp.concatenate([first_float, second_float], axis=1)
 
 
 def inner_kernel(half_count, me_ref, key_ref, rms_ref, *refs):
-    key_grad_refs, cross_refs = refs[:half_count], refs[half_count : 2 * half_count]
-    out_ref = refs[2 * half_count]
+    cross_refs, first_refs, second_refs = [
+        refs[place * half_count : (place + 1) * half_count] for place in range(3)
+    ]
+    out_ref = refs[3 * half_count]
     tokens, features = key_ref.shape
     width = features // half_count
     inside = me_ref[0] & (half_count - 1)
     total = jnp.zeros((tokens, width), jnp.float32)
     for distance in range(half_count):
-        start = pl.multiple_of((inside ^ distance) * width, LANES)
+        owner = inside ^ distance
+        start = pl.multiple_of(owner * width, LANES)
         key_float = key_ref[:, pl.ds(start, width)].astype(jnp.float32)
         total = total + key_float * normed_grad_of(
-            half_count, me_ref, key_grad_refs, cross_refs, distance, tokens
+            half_count, me_ref, first_refs[distance], second_refs[distance], cross_refs[distance]
         )
-    column = jnp.sum(total, axis=1, keepdims=True) / column_of(rms_ref, 0, tokens)
+    column = jnp.sum(total, axis=1, keepdims=True) / column_of(rms_ref[...], 0, tokens)
     out_ref[...] = jnp.zeros_like(out_ref)
     store_as_rows(out_ref, 0, column)
 
 
 def final_kernel(half_count, feature_total, me_ref, key_ref, rms_ref, inner_ref, *refs):
-    key_grad_refs, cross_refs = refs[:half_count], refs[half_count : 2 * half_count]
-    result_ref, attended_ref, query_ref, key_out_ref, value_ref = refs[2 * half_count :]
+    cross_refs, first_refs, second_refs = [
+        refs[place * half_count : (place + 1) * half_count] for place in range(3)
+    ]
+    attended_ref, query_ref, key_out_ref, value_ref = refs[3 * half_count :]
     tokens, features = key_ref.shape
     width = features // half_count
     single = width // 2
     is_high = me_ref[0] >= half_count
     inside = me_ref[0] & (half_count - 1)
-    rms = column_of(rms_ref, 0, tokens)
-    inner = column_of(inner_ref, 0, tokens) / feature_total
-    for owner in range(half_count):
-        columns = slice(owner * width, (owner + 1) * width)
-        for place, target in enumerate((attended_ref, query_ref, value_ref)):
-            first = (owner * 3 + place) * tokens
-            target[:, columns] = result_ref[first : first + tokens, :]
+    rms = column_of(rms_ref[...], 0, tokens)
+    inner = column_of(inner_ref[...], 0, tokens) / feature_total
     for distance in range(half_count):
-        start = pl.multiple_of((inside ^ distance) * width, LANES)
+        owner = inside ^ distance
+        start = pl.multiple_of(owner * width, LANES)
         columns = pl.ds(start, width)
         normed_float = key_ref[:, columns].astype(jnp.float32) / rms
         grad_float = normed_grad_of(
-            half_count, me_ref, key_grad_refs, cross_refs, distance, tokens
+            half_count, me_ref, first_refs[distance], second_refs[distance], cross_refs[distance]
         )
         key_out_ref[:, columns] = ((grad_float - normed_float * inner) / rms).astype(jnp.bfloat16)
         cross_ref = cross_refs[distance]
+        second = pl.ds(pl.multiple_of(start + single, LANES), single)
+        for place, target in enumerate((attended_ref, query_ref, value_ref)):
+            rows = slice(place * tokens, (place + 1) * tokens)
+            target[:, pl.ds(start, single)] = first_refs[distance][rows, :]
+            target[:, second] = second_refs[distance][rows, :]
 
         def add(target, columns, first):
             far = cross_ref[first : first + tokens, :].astype(jnp.float32)
@@ -670,7 +673,6 @@
 
         @pl.when(is_high)
         def _():
-            second = pl.ds(pl.multiple_of(start + single, LANES), single)
             add(attended_ref, second, 0)
             add(query_ref, second, tokens)
 
@@ -687,7 +689,7 @@
     return jax.ShapeDtypeStruct((rows, columns), jnp.bfloat16)
 
 
-def call(kernel, out_shapes, scalars, arrays, scratch=(), in_hbm=0):
+def call(kernel, out_shapes, scalars, arrays, scratch=(), in_hbm=0, out_hbm=False, flops=0):
     vmem, anywhere = pl.BlockSpec(memory_space=pltpu.VMEM), pl.BlockSpec(memory_space=pl.ANY)
     return pl.pallas_call(
         kernel,
@@ -695,9 +697,10 @@
         in_specs=[pl.BlockSpec(memory_space=pltpu.SMEM)] * len(scalars)
         + [anywhere] * in_hbm
         + [vmem] * (len(arrays) - in_hbm),
-        out_specs=jax.tree.map(lambda shape: vmem, out_shapes),
+        out_specs=jax.tree.map(lambda shape: anywhere if out_hbm else vmem, out_shapes),
         scratch_shapes=list(scratch),
-        compiler_params=pltpu.CompilerParams(vmem_limit_bytes=VMEM_BYTES),
+        compiler_params=pltpu.CompilerParams(vmem_limit_bytes=PACK_VMEM_BYTES if in_hbm else VMEM_BYTES),
+        cost_estimate=pl.CostEstimate(flops=flops, bytes_accessed=0, transcendentals=0) if flops else None,
     )(*scalars, *arrays)
 
 
@@ -714,11 +717,21 @@
     return [swap(block, len(blocks) + d) for d, block in enumerate(blocks)]
 
 
-def exchange_inside(rows):
-    count = lax.axis_size("seq")
-    groups = [list(range(count // 2)), list(range(count // 2, count))]
+def exchange_inside(rows, half_count):
+    count = 2 * half_count
+    groups = [list(range(half_count)), list(range(half_count, count))]
+    parts = rows.reshape(half_count, -1, rows.shape[1])
     return lax.all_to_all(
-        rows, "seq", split_axis=0, concat_axis=0, tiled=True, axis_index_groups=groups
+        parts, "seq", split_axis=0, concat_axis=0, tiled=True, axis_index_groups=groups
+    ).reshape(rows.shape)
+
+
+def sum_over_head(block):
+    count = lax.axis_size("head")
+    if count & (count - 1):
+        return lax.psum(block, "head")
+    return block + sum(
+        lax.ppermute(block, "head", [(i, i ^ d) for i in range(count)]) for d in range(1, count)
     )
 
 
@@ -731,81 +744,104 @@
     cluster_count, block_count, _ = block_pattern.shape
     half_len = half_count * tokens
     shape = (tokens, half_count, cluster_count, block_count)
-    row_count = -(-tokens // LANES)
-    stat_rows = -(-half_len // LANES)
+    row_count = -(-tokens // (8 * LANES)) * 8
+    stat_rows = -(-half_len // (8 * LANES)) * 8
     me = lax.axis_index("seq").astype(jnp.int32).reshape(1)
-    ids = lane_rows(cluster[:, 0], ID_ROWS).astype(jnp.bfloat16)
+    packed_shape = half_array(half_count * 3 * tokens, width)
     packed = call(
         functools.partial(pack_kernel, half_count),
-        half_array(half_count * (3 * tokens + ID_ROWS), width),
+        packed_shape,
         [],
-        [queries, values, cotangent, ids],
-        [pltpu.SemaphoreType.DMA((3 * half_count,))],
+        [queries, values, cotangent],
+        [
+            pltpu.VMEM((3, tokens, features), jnp.bfloat16),
+            pltpu.VMEM(packed_shape.shape, jnp.bfloat16),
+            pltpu.SemaphoreType.DMA((3,)),
+            pltpu.SemaphoreType.DMA((3 * half_count,)),
+        ],
         in_hbm=3,
-    )
-    packed = exchange_inside(packed)
+        out_hbm=True,
+    )
+    packed, key_vectors, cluster = lax.optimization_barrier((packed, key_vectors, cluster))
+    packed = exchange_inside(packed, half_count)
+    ids = lane_rows(cluster[:, 0], ID_ROWS).astype(jnp.bfloat16)
     key_float = key_vectors.astype(jnp.float32)
-    square_sum = lax.psum(jnp.sum(key_float * key_float, axis=1), "head")
+    square_sum = sum_over_head(lane_rows(jnp.sum(key_float * key_float, axis=1), row_count))
     feature_total = HEADS * HEAD_DIM
-    key_rms = lane_rows(jnp.sqrt(square_sum / feature_total + EPSILON), row_count)
+    key_rms = jnp.sqrt(square_sum / feature_total + EPSILON)
     sent = call(
         functools.partial(pack_keys_kernel, half_count),
-        [half_array(tokens, width)] * half_count
+        [half_array(tokens + ID_ROWS, width)] * half_count
         + [half_array(2 * tokens + ID_ROWS, single)] * half_count,
         [me],
         [queries, values, cotangent, key_vectors, key_rms, ids],
     )
-    cross = swap_across(sent[half_count:])
     keys = swap_inside(sent[:half_count])
+    cross_sent = list(sent[half_count:])
+    for distance in range(half_count // 2, half_count):
+        cross_sent[distance], keys[1] = lax.optimization_barrier((cross_sent[distance], keys[1]))
+    cross = swap_across(cross_sent)
     pattern_rows = block_pattern.transpose(1, 0, 2).reshape(block_count, -1).astype(jnp.float32)
     pattern_rows = jnp.pad(pattern_rows, ((0, 0), (0, LANES - cluster_count * block_count)))
-    inputs = [pattern_rows, packed] + keys + cross
     wide = pltpu.VMEM((half_len, 2 * HEAD_DIM), jnp.bfloat16)
     slim = pltpu.VMEM((half_len, HEAD_DIM), jnp.bfloat16)
     sums = pltpu.VMEM((half_len, HEAD_DIM), jnp.float32)
     ids_column = pltpu.VMEM((half_len, 1), jnp.float32)
+    block_flops = 12 * half_len * half_len * single
+    inputs = [pattern_rows, packed] + cross + keys
     stats = call(
         functools.partial(stats_kernel, shape, stat_rows),
         jax.ShapeDtypeStruct((3 * stat_rows * (single // HEAD_DIM), LANES), jnp.float32),
         [me],
         inputs,
-        [wide, wide, slim, slim, wide, slim, ids_column],
+        [wide, wide, slim, slim, ids_column, ids_column],
+        flops=block_flops // 3,
     )
     far_stats = swap(stats, half_count)
-    first = call(
-        functools.partial(first_head_kernel, shape),
-        [half_array(3 * half_len, single)]
-        + [half_array(tokens, single)] * half_count
+    firsts = call(
+        functools.partial(first_kernel, shape),
+        [half_array(4 * tokens, single)] * half_count
+        + [half_array(2 * tokens, single)] * half_count
+        + [
+            half_array(2 * half_len, single),
+            jax.ShapeDtypeStruct((2 * half_len, single), jnp.float32),
+        ],
+        [me],
+        inputs + [stats],
+        [wide, wide, slim, slim, wide, slim, ids_column, ids_column, slim, slim]
+        + [sums, sums, sums, sums],
+        flops=block_flops + block_flops // 2,
+    )
+    *firsts, far_stats = lax.optimization_barrier((*firsts, far_stats))
+    rest = firsts[half_count:]
+    firsts = swap_inside(firsts[:half_count])
+    results = call(
+        functools.partial(second_head_kernel, shape, stat_rows),
+        [half_array(4 * tokens, single)] * half_count
         + [half_array(2 * tokens, single)] * half_count,
         [me],
-        inputs,
-        [wide, wide, slim, slim, wide, slim, ids_column, slim, slim, sums, sums, sums, sums],
-    )
-    results = call(
-        functools.partial(second_head_kernel, shape, stat_rows),
-        [half_array(3 * half_len, width)]
-        + [half_array(tokens, width)] * half_count
-        + [half_array(2 * tokens, single)] * half_count,
-        [me],
-        inputs + [stats, far_stats] + list(first),
-        [wide, wide, slim, slim, wide, slim, ids_column, slim, slim, sums, sums, slim, slim],
-    )
-    key_grads = swap_inside(results[1 : 1 + half_count])
-    far_parts = swap_across(results[1 + half_count :])
-    main = exchange_inside(results[0])
+        inputs + [stats, far_stats] + rest[half_count:] + rest[:half_count],
+        [wide, wide, slim, slim, wide, slim, ids_column, ids_column, slim, slim]
+        + [sums, sums, slim, slim],
+        flops=block_flops,
+    )
+    far_sent = list(results[half_count:])
+    far_sent, firsts = lax.optimization_barrier((far_sent, firsts))
+    far_parts = swap_across(far_sent)
+    seconds = swap_inside(results[:half_count])
     inner = call(
         functools.partial(inner_kernel, half_count),
         jax.ShapeDtypeStruct((row_count, LANES), jnp.float32),
         [me],
-        [key_vectors, key_rms] + key_grads + far_parts,
-    )
-    inner = lax.psum(inner, "head")
+        [key_vectors, key_rms] + far_parts + firsts + seconds,
+    )
+    inner = sum_over_head(inner)
     return tuple(
         call(
             functools.partial(final_kernel, half_count, feature_total),
             [half_array(tokens, features)] * 4,
             [me],
-            [key_vectors, key_rms, inner] + key_grads + far_parts + [main],
+            [key_vectors, key_rms, inner] + far_parts + firsts + seconds,
         )
     )
 

time: 100 us -> 84.8 us (0.85)
  blocking collectives: 12.4 us -> 0 us
  waiting for transfers between devices: 23.3 us -> 29.3 us
  starting transfers between devices: 42.8 us -> 38.4 us
  local copies, waits for them, and re-layouts: 3.11 us -> 0.14 us
    psum x2 -> x0, blocking collectives: 12.4 us -> none  [the longest x1 6.34 us: by_halves(): square_sum = lax.psum(jnp.sum(key_float * key_float, axis=1), 'head')]
    all_to_all x2 -> x1, starting transfers between devices: 9.94 us -> 5.39 us  [exchange_inside(): lax.all_to_all(parts, 'seq', split_axis=0, concat_axis=0, tiled=True, axi...]
    ppermute x0 -> x6, waiting for transfers between devices: none -> 4.22 us  [sum_over_head(): lax.ppermute(block, 'head', [(i, i ^ d) for i in range(count)])]
    ppermute x0 -> x6, starting transfers between devices: none -> 3.84 us  [sum_over_head(): lax.ppermute(block, 'head', [(i, i ^ d) for i in range(count)])]
    ppermute x15 -> x18, starting transfers between devices: 32.8 us -> 29.1 us  [swap(): return lax.ppermute(block, 'seq', [(i, i ^ distance) for i in range(count)])]
    unnamed x16 -> x12, local copies, waits for them, and re-layouts: 3.01 us -> 0.04 us
    ppermute x15 -> x18, waiting for transfers between devices: 23.3 us -> 25.1 us  [swap(): return lax.ppermute(block, 'seq', [(i, i ^ distance) for i in range(count)])]
  transfers between devices with their start and end apart: 17 -> 25, of which waited for: 6 -> 10; matrix products, arithmetic and copies ran while one was open for 0% -> 0% of each run, Pallas kernels for 4% -> 11%
where the time goes in v1:
time: 84.8 us; the launch traced here: 84.3 us
  starting transfers between devices  38.4 us (45%)
  waiting for transfers between devices  29.3 us (35%)
  Pallas kernels  15.5 us (18%)
    ppermute x18, starting transfers between devices, swap(): return lax.ppermute(block, 'seq', [(i, i ^ distance) for i in range(count)])  29.1 us
    ppermute x18, waiting for transfers between devices, swap(): return lax.ppermute(block, 'seq', [(i, i ^ distance) for i in range(count)])  25.1 us
    pallas_call x7, Pallas kernels, call(): pl.pallas_call(kernel, out_shape=out_shapes, in_specs=[pl.BlockSpec(memor...  15.5 us
    all_to_all x1, starting transfers between devices, exchange_inside(): lax.all_to_all(parts, 'seq', split_axis=0, concat_axis=0, tiled=True, axi...  5.39 us
    ppermute x6, waiting for transfers between devices, sum_over_head(): lax.ppermute(block, 'head', [(i, i ^ d) for i in range(count)])  4.22 us
    ppermute x6, starting transfers between devices, sum_over_head(): lax.ppermute(block, 'head', [(i, i ^ d) for i in range(count)])  3.84 us
  transfers between devices with their start and end apart: 25, of which 10 were waited for; matrix products, arithmetic and copies ran while one was open for 0% of the time, Pallas kernels for 11%

profile of v1, /device:TPU:0, one launch (start us, length us, event | category | flops | bytes accessed | tf_op | source)
XLA Modules:
  0.0 84.3 jit_solution(7670721661823259664)
XLA Ops:
  0.6 2.2 %shard_map.93 = bf16[2304,256]{1,0:T(8,128)(2,1)} custom-call(bf16[192,1024]{1,0:T(8,128)(2,1)} %query_ref.3, bf16[192,1024]{1,0:T(8,128)(2,1)} %value_ref.3, bf16[192,1024]{1,0:T(8,128)(2,1)} %grad_ref.3), custom_call_target="tpu_custom_call" | custom-call | tf_op jit(solution)/shard_map/pallas_call | solution.py:694
  2.9 5.4 %all-to-all-start = ((bf16[4,576,256]{2,1,0:T(8,128)(2,1)}), bf16[4,576,256]{2,1,0:T(8,128)(2,1)S(1)}, u32[]{:S(2)}, u32[]{:S(2)}) async-start(bf16[4,576,256]{2,1,0:T(8,128)(2,1)} %bitcast.14), calls=%async_computation | async-start | bytes 2359296 | tf_op jit(solution)/shard_map/all_to_all | solution.py:724
  13.2 1.8 %collective-permute-start.5 = (bf16[208,256]{1,0:T(8,128)(2,1)S(1)}, bf16[208,256]{1,0:T(8,128)(2,1)S(1)}, u32[]{:S(2)}, u32[]{:S(2)}) collective-permute-start(bf16[208,256]{1,0:T(8,128)(2,1)S(1)} %get-tuple-element.62), channel_id=1, source_target_pairs={{0,4},{4,0},{8,12},{12,8},{16,20},{20,16},{24,28},{28,24},{1,5},{5... | collective-permute-start | bytes 319496 | tf_op jit(solution)/shard_map/ppermute | solution.py:709
  15.0 2.6 %collective-permute-start.3 = (bf16[400,128]{1,0:T(8,128)(2,1)S(1)}, bf16[400,128]{1,0:T(8,128)(2,1)S(1)}, u32[]{:S(2)}, u32[]{:S(2)}) collective-permute-start(bf16[400,128]{1,0:T(8,128)(2,1)S(1)} %get-tuple-element.59), channel_id=1, source_target_pairs={{0,16},{4,20},{8,24},{12,28},{16,0},{20,4},{24,8},{28,12},{1,17},{... | collective-permute-start | bytes 307208 | tf_op jit(solution)/shard_map/ppermute | solution.py:709
  17.7 1.7 %collective-permute-start.8 = (bf16[208,256]{1,0:T(8,128)(2,1)S(1)}, bf16[208,256]{1,0:T(8,128)(2,1)S(1)}, u32[]{:S(2)}, u32[]{:S(2)}) collective-permute-start(bf16[208,256]{1,0:T(8,128)(2,1)S(1)} %get-tuple-element.69), channel_id=1, source_target_pairs={{0,8},{4,12},{8,0},{12,4},{16,24},{20,28},{24,16},{28,20},{1,9},{5... | collective-permute-start | bytes 319496 | tf_op jit(solution)/shard_map/ppermute | solution.py:709
  19.4 1.5 %collective-permute-start.9 = (bf16[208,256]{1,0:T(8,128)(2,1)S(1)}, bf16[208,256]{1,0:T(8,128)(2,1)S(1)}, u32[]{:S(2)}, u32[]{:S(2)}) collective-permute-start(bf16[208,256]{1,0:T(8,128)(2,1)S(1)} %get-tuple-element.70), channel_id=1, source_target_pairs={{0,12},{4,8},{8,4},{12,0},{16,28},{20,24},{24,20},{28,16},{1,13},{... | collective-permute-start | bytes 319496 | tf_op jit(solution)/shard_map/ppermute | solution.py:709
  20.9 6.8 %collective-permute-done.5.refs_5_ = bf16[208,256]{1,0:T(8,128)(2,1)S(1)} collective-permute-done((bf16[208,256]{1,0:T(8,128)(2,1)S(1)}, bf16[208,256]{1,0:T(8,128)(2,1)S(1)}, u32[]{:S(2)}, u32[]{:S(2)}) %collective-permute-start.5) | collective-permute-done | bytes 106528 | tf_op jit(solution)/shard_map/ppermute | solution.py:709
  27.7 2.5 %collective-permute-start.7 = (bf16[400,128]{1,0:T(8,128)(2,1)S(1)}, bf16[400,128]{1,0:T(8,128)(2,1)S(1)}, u32[]{:S(2)}, u32[]{:S(2)}) collective-permute-start(bf16[400,128]{1,0:T(8,128)(2,1)S(1)} %get-tuple-element.66), channel_id=1, source_target_pairs={{0,28},{4,24},{8,20},{12,16},{16,12},{20,8},{24,4},{28,0},{1,29},{... | collective-permute-start | bytes 307208 | tf_op jit(solution)/shard_map/ppermute | solution.py:709
  31.4 1.8 %collective-permute-done.9.refs_7_ = bf16[208,256]{1,0:T(8,128)(2,1)S(1)} collective-permute-done((bf16[208,256]{1,0:T(8,128)(2,1)S(1)}, bf16[208,256]{1,0:T(8,128)(2,1)S(1)}, u32[]{:S(2)}, u32[]{:S(2)}) %collective-permute-start.9) | collective-permute-done | bytes 106528 | tf_op jit(solution)/shard_map/ppermute | solution.py:709
  33.2 5.4 %collective-permute-done.7.refs_3_ = bf16[400,128]{1,0:T(8,128)(2,1)S(1)} collective-permute-done((bf16[400,128]{1,0:T(8,128)(2,1)S(1)}, bf16[400,128]{1,0:T(8,128)(2,1)S(1)}, u32[]{:S(2)}, u32[]{:S(2)}) %collective-permute-start.7) | collective-permute-done | bytes 102432 | tf_op jit(solution)/shard_map/ppermute | solution.py:709
  38.8 2.0 %shard_map.95.refs_8_ = f32[24,128]{1,0:T(8,128)S(1)} custom-call(s32[1]{0:T(128)} %bitcast.me_ref, f32[12,128]{1,0:T(8,128)S(1)} %pad.14.pattern_ref, bf16[2304,256]{1,0:T(8,128)(2,1)S(1)} %bitcast.11, bf16[400,128]{1,0:T(8,128)(2,1)S(1)} %collective-permute-done.3.refs_0_, bf16[400,128]{1,0:T(8,128)(2,1)S(1)} %collective-permute-done.4.refs_1_, ...), custom_call_target="tpu_custom_call" | custom-call | flops 301989888 | tf_op jit(solution)/shard_map/pallas_call | solution.py:694
  40.9 5.5 %shard_map.96 = (bf16[768,128]{1,0:T(8,128)(2,1)S(1)}, bf16[768,128]{1,0:T(8,128)(2,1)S(1)}, bf16[768,128]{1,0:T(8,128)(2,1)S(1)}, bf16[768,128]{1,0:T(8,128)(2,...) custom-call(s32[1]{0:T(128)} %bitcast.me_ref, ...), custom_call_target="tpu_custom_call" | custom-call | flops 1358954496 | tf_op jit(solution)/shard_map/pallas_call | solution.py:694
  46.3 1.6 %collective-permute-start.11 = (bf16[768,128]{1,0:T(8,128)(2,1)S(1)}, bf16[768,128]{1,0:T(8,128)(2,1)S(1)}, u32[]{:S(2)}, u32[]{:S(2)}) collective-permute-start(bf16[768,128]{1,0:T(8,128)(2,1)S(1)} %get-tuple-element.93), channel_id=1, source_target_pairs={{0,4},{4,0},{8,12},{12,8},{16,20},{20,16},{24,28},{28,24},{1,5},{5... | collective-permute-start | bytes 589832 | tf_op jit(solution)/shard_map/ppermute | solution.py:709
  48.0 1.5 %collective-permute-start.12 = (bf16[768,128]{1,0:T(8,128)(2,1)S(1)}, bf16[768,128]{1,0:T(8,128)(2,1)S(1)}, u32[]{:S(2)}, u32[]{:S(2)}) collective-permute-start(bf16[768,128]{1,0:T(8,128)(2,1)S(1)} %get-tuple-element.94), channel_id=1, source_target_pairs={{0,8},{4,12},{8,0},{12,4},{16,24},{20,28},{24,16},{28,20},{1,9},{5... | collective-permute-start | bytes 589832 | tf_op jit(solution)/shard_map/ppermute | solution.py:709
  49.9 3.2 %shard_map.97 = (bf16[768,128]{1,0:T(8,128)(2,1)S(1)}, bf16[768,128]{1,0:T(8,128)(2,1)S(1)}, bf16[768,128]{1,0:T(8,128)(2,1)S(1)}, bf16[768,128]{1,0:T(8,128)(2,...) custom-call(s32[1]{0:T(128)} %bitcast.me_ref, ...), custom_call_target="tpu_custom_call" | custom-call | flops 905969664 | tf_op jit(solution)/shard_map/pallas_call | solution.py:694
  53.1 1.6 %collective-permute-start.18 = (bf16[768,128]{1,0:T(8,128)(2,1)S(1)}, bf16[768,128]{1,0:T(8,128)(2,1)S(1)}, u32[]{:S(2)}, u32[]{:S(2)}) collective-permute-start(bf16[768,128]{1,0:T(8,128)(2,1)S(1)} %get-tuple-element.105), channel_id=1, source_target_pairs={{0,4},{4,0},{8,12},{12,8},{16,20},{20,16},{24,28},{28,24},{1,5},{5... | collective-permute-start | bytes 589832 | tf_op jit(solution)/shard_map/ppermute | solution.py:709
  54.8 1.6 %collective-permute-start.19 = (bf16[768,128]{1,0:T(8,128)(2,1)S(1)}, bf16[768,128]{1,0:T(8,128)(2,1)S(1)}, u32[]{:S(2)}, u32[]{:S(2)}) collective-permute-start(bf16[768,128]{1,0:T(8,128)(2,1)S(1)} %get-tuple-element.106), channel_id=1, source_target_pairs={{0,8},{4,12},{8,0},{12,4},{16,24},{20,28},{24,16},{28,20},{1,9},{5... | collective-permute-start | bytes 589832 | tf_op jit(solution)/shard_map/ppermute | solution.py:709
  56.7 2.9 %collective-permute-done.13.refs_7_ = bf16[768,128]{1,0:T(8,128)(2,1)S(1)} collective-permute-done((bf16[768,128]{1,0:T(8,128)(2,1)S(1)}, bf16[768,128]{1,0:T(8,128)(2,1)S(1)}, u32[]{:S(2)}, u32[]{:S(2)}) %collective-permute-start.13) | collective-permute-done | bytes 196640 | tf_op jit(solution)/shard_map/ppermute | solution.py:709
  59.6 3.3 %collective-permute-start.14 = (bf16[384,128]{1,0:T(8,128)(2,1)S(1)}, bf16[384,128]{1,0:T(8,128)(2,1)S(1)}, u32[]{:S(2)}, u32[]{:S(2)}) collective-permute-start(bf16[384,128]{1,0:T(8,128)(2,1)S(1)} %get-tuple-element.96), channel_id=1, source_target_pairs={{0,16},{4,20},{8,24},{12,28},{16,0},{20,4},{24,8},{28,12},{1,17},{... | collective-permute-start | bytes 294920 | tf_op jit(solution)/shard_map/ppermute | solution.py:709
  62.9 1.3 %collective-permute-start.15 = (bf16[384,128]{1,0:T(8,128)(2,1)S(1)}, bf16[384,128]{1,0:T(8,128)(2,1)S(1)}, u32[]{:S(2)}, u32[]{:S(2)}) collective-permute-start(bf16[384,128]{1,0:T(8,128)(2,1)S(1)} %get-tuple-element.97), channel_id=1, source_target_pairs={{0,20},{4,16},{8,28},{12,24},{16,4},{20,0},{24,12},{28,8},{1,21},{... | collective-permute-start | bytes 294920 | tf_op jit(solution)/shard_map/ppermute | solution.py:709
  64.2 6.1 %collective-permute-start.16 = (bf16[384,128]{1,0:T(8,128)(2,1)S(1)}, bf16[384,128]{1,0:T(8,128)(2,1)S(1)}, u32[]{:S(2)}, u32[]{:S(2)}) collective-permute-start(bf16[384,128]{1,0:T(8,128)(2,1)S(1)} %get-tuple-element.98), channel_id=1, source_target_pairs={{0,24},{4,28},{8,16},{12,20},{16,8},{20,12},{24,0},{28,4},{1,25},{... | collective-permute-start | bytes 294920 | tf_op jit(solution)/shard_map/ppermute | solution.py:709
  70.4 8.0 %collective-permute-done.15.refs_1_ = bf16[384,128]{1,0:T(8,128)(2,1)S(1)} collective-permute-done((bf16[384,128]{1,0:T(8,128)(2,1)S(1)}, bf16[384,128]{1,0:T(8,128)(2,1)S(1)}, u32[]{:S(2)}, u32[]{:S(2)}) %collective-permute-start.15) | collective-permute-done | bytes 98336 | tf_op jit(solution)/shard_map/ppermute | solution.py:709
  78.8 1.6 %collective-permute-start.22 = (f32[8,128]{1,0:T(8,128)S(1)}, f32[8,128]{1,0:T(8,128)S(1)}, u32[]{:S(2)}, u32[]{:S(2)}) collective-permute-start(f32[8,128]{1,0:T(8,128)S(1)} %shard_map.98), channel_id=1, source_target_pairs={{0,2},{1,3},{2,0},{3,1},{4,6},{5,7},{6,4},{7,5},{8,10},{9,11},{10,... | collective-permute-start | bytes 12296 | tf_op jit(solution)/shard_map/ppermute | solution.py:734
  82.4 1.9 %shard_map.99 = (bf16[192,1024]{1,0:T(8,128)(2,1)}, bf16[192,1024]{1,0:T(8,128)(2,1)}, bf16[192,1024]{1,0:T(8,128)(2,1)}, bf16[192,1024]{1,0:T(8,128)(2,1)}) custom-call(s32[1]{0:T(128)} %bitcast.me_ref, bf16[192,1024]{1,0:T(8,128)(2,1)S(1)} %copy-done, f32[8,128]{1,0:T(8,128)S(1)} %add_sqrt_fusion.rms_ref, f32[8,128]{1,0:T(8,128)S(1)} %add_add_fusion.inner_ref, ...), custom_call_target="tpu_custom_call" | custom-call | tf_op jit(solution)/shard_map/pallas_call | solution.py:694
  (54 shorter events, 9.9 us)
Async XLA Ops:
  2.9 35.9 %all-to-all-start = ((bf16[4,576,256]{2,1,0:T(8,128)(2,1)}), bf16[4,576,256]{2,1,0:T(8,128)(2,1)S(1)}, u32[]{:S(2)}, u32[]{:S(2)}) async-start(bf16[4,576,256]{2,1,0:T(8,128)(2,1)} %bitcast.14), calls=%async_computation | async-start | bytes 2359296 | tf_op jit(solution)/shard_map/all_to_all | solution.py:724
  8.4 3.1 %collective-permute-start.2 = (f32[8,128]{1,0:T(8,128)S(1)}, f32[8,128]{1,0:T(8,128)S(1)}, u32[]{:S(2)}, u32[]{:S(2)}) collective-permute-start(f32[8,128]{1,0:T(8,128)S(1)} %pad_bitcast_fusion.1), channel_id=1, source_target_pairs={{0,3},{1,2},{2,1},{3,0},{4,7},{5,6},{6,5},{7,4},{8,11},{9,10},{10,... | collective-permute-start | bytes 12296 | tf_op jit(solution)/shard_map/ppermute | solution.py:734
  9.2 3.6 %collective-permute-start.1 = (f32[8,128]{1,0:T(8,128)S(1)}, f32[8,128]{1,0:T(8,128)S(1)}, u32[]{:S(2)}, u32[]{:S(2)}) collective-permute-start(f32[8,128]{1,0:T(8,128)S(1)} %pad_bitcast_fusion.1), channel_id=1, source_target_pairs={{0,2},{1,3},{2,0},{3,1},{4,6},{5,7},{6,4},{7,5},{8,10},{9,11},{10,... | collective-permute-start | bytes 12296 | tf_op jit(solution)/shard_map/ppermute | solution.py:734
  10.1 2.7 %collective-permute-start = (f32[8,128]{1,0:T(8,128)S(1)}, f32[8,128]{1,0:T(8,128)S(1)}, u32[]{:S(2)}, u32[]{:S(2)}) collective-permute-start(f32[8,128]{1,0:T(8,128)S(1)} %pad_bitcast_fusion.1), channel_id=1, source_target_pairs={{0,1},{1,0},{2,3},{3,2},{4,5},{5,4},{6,7},{7,6},{8,9},{9,8},{10,11... | collective-permute-start | bytes 12296 | tf_op jit(solution)/shard_map/ppermute | solution.py:734
  13.2 14.5 %collective-permute-start.5 = (bf16[208,256]{1,0:T(8,128)(2,1)S(1)}, bf16[208,256]{1,0:T(8,128)(2,1)S(1)}, u32[]{:S(2)}, u32[]{:S(2)}) collective-permute-start(bf16[208,256]{1,0:T(8,128)(2,1)S(1)} %get-tuple-element.62), channel_id=1, source_target_pairs={{0,4},{4,0},{8,12},{12,8},{16,20},{20,16},{24,28},{28,24},{1,5},{5... | collective-permute-start | bytes 319496 | tf_op jit(solution)/shard_map/ppermute | solution.py:709
  15.0 15.2 %collective-permute-start.3 = (bf16[400,128]{1,0:T(8,128)(2,1)S(1)}, bf16[400,128]{1,0:T(8,128)(2,1)S(1)}, u32[]{:S(2)}, u32[]{:S(2)}) collective-permute-start(bf16[400,128]{1,0:T(8,128)(2,1)S(1)} %get-tuple-element.59), channel_id=1, source_target_pairs={{0,16},{4,20},{8,24},{12,28},{16,0},{20,4},{24,8},{28,12},{1,17},{... | collective-permute-start | bytes 307208 | tf_op jit(solution)/shard_map/ppermute | solution.py:709
  17.6 13.8 %collective-permute-start.4 = (bf16[400,128]{1,0:T(8,128)(2,1)S(1)}, bf16[400,128]{1,0:T(8,128)(2,1)S(1)}, u32[]{:S(2)}, u32[]{:S(2)}) collective-permute-start(bf16[400,128]{1,0:T(8,128)(2,1)S(1)} %get-tuple-element.60), channel_id=1, source_target_pairs={{0,20},{4,16},{8,28},{12,24},{16,4},{20,0},{24,12},{28,8},{1,21},{... | collective-permute-start | bytes 307208 | tf_op jit(solution)/shard_map/ppermute | solution.py:709
  17.7 13.7 %collective-permute-start.8 = (bf16[208,256]{1,0:T(8,128)(2,1)S(1)}, bf16[208,256]{1,0:T(8,128)(2,1)S(1)}, u32[]{:S(2)}, u32[]{:S(2)}) collective-permute-start(bf16[208,256]{1,0:T(8,128)(2,1)S(1)} %get-tuple-element.69), channel_id=1, source_target_pairs={{0,8},{4,12},{8,0},{12,4},{16,24},{20,28},{24,16},{28,20},{1,9},{5... | collective-permute-start | bytes 319496 | tf_op jit(solution)/shard_map/ppermute | solution.py:709
  19.4 13.7 %collective-permute-start.9 = (bf16[208,256]{1,0:T(8,128)(2,1)S(1)}, bf16[208,256]{1,0:T(8,128)(2,1)S(1)}, u32[]{:S(2)}, u32[]{:S(2)}) collective-permute-start(bf16[208,256]{1,0:T(8,128)(2,1)S(1)} %get-tuple-element.70), channel_id=1, source_target_pairs={{0,12},{4,8},{8,4},{12,0},{16,28},{20,24},{24,20},{28,16},{1,13},{... | collective-permute-start | bytes 319496 | tf_op jit(solution)/shard_map/ppermute | solution.py:709
  27.7 10.8 %collective-permute-start.7 = (bf16[400,128]{1,0:T(8,128)(2,1)S(1)}, bf16[400,128]{1,0:T(8,128)(2,1)S(1)}, u32[]{:S(2)}, u32[]{:S(2)}) collective-permute-start(bf16[400,128]{1,0:T(8,128)(2,1)S(1)} %get-tuple-element.66), channel_id=1, source_target_pairs={{0,28},{4,24},{8,20},{12,16},{16,12},{20,8},{24,4},{28,0},{1,29},{... | collective-permute-start | bytes 307208 | tf_op jit(solution)/shard_map/ppermute | solution.py:709
  30.2 8.6 %collective-permute-start.6 = (bf16[400,128]{1,0:T(8,128)(2,1)S(1)}, bf16[400,128]{1,0:T(8,128)(2,1)S(1)}, u32[]{:S(2)}, u32[]{:S(2)}) collective-permute-start(bf16[400,128]{1,0:T(8,128)(2,1)S(1)} %get-tuple-element.63), channel_id=1, source_target_pairs={{0,24},{4,28},{8,16},{12,20},{16,8},{20,12},{24,0},{28,4},{1,25},{... | collective-permute-start | bytes 307208 | tf_op jit(solution)/shard_map/ppermute | solution.py:709
  40.8 5.6 %collective-permute-start.10 = (f32[24,128]{1,0:T(8,128)S(1)}, f32[24,128]{1,0:T(8,128)S(1)}, u32[]{:S(2)}, u32[]{:S(2)}) collective-permute-start(f32[24,128]{1,0:T(8,128)S(1)} %shard_map.95.refs_8_), channel_id=1, source_target_pairs={{0,16},{4,20},{8,24},{12,28},{16,0},{20,4},{24,8},{28,12},{1,17},{... | collective-permute-start | bytes 36872 | tf_op jit(solution)/shard_map/ppermute | solution.py:709
  46.3 10.0 %collective-permute-start.11 = (bf16[768,128]{1,0:T(8,128)(2,1)S(1)}, bf16[768,128]{1,0:T(8,128)(2,1)S(1)}, u32[]{:S(2)}, u32[]{:S(2)}) collective-permute-start(bf16[768,128]{1,0:T(8,128)(2,1)S(1)} %get-tuple-element.93), channel_id=1, source_target_pairs={{0,4},{4,0},{8,12},{12,8},{16,20},{20,16},{24,28},{28,24},{1,5},{5... | collective-permute-start | bytes 589832 | tf_op jit(solution)/shard_map/ppermute | solution.py:709
  48.0 8.7 %collective-permute-start.12 = (bf16[768,128]{1,0:T(8,128)(2,1)S(1)}, bf16[768,128]{1,0:T(8,128)(2,1)S(1)}, u32[]{:S(2)}, u32[]{:S(2)}) collective-permute-start(bf16[768,128]{1,0:T(8,128)(2,1)S(1)} %get-tuple-element.94), channel_id=1, source_target_pairs={{0,8},{4,12},{8,0},{12,4},{16,24},{20,28},{24,16},{28,20},{1,9},{5... | collective-permute-start | bytes 589832 | tf_op jit(solution)/shard_map/ppermute | solution.py:709
  49.5 10.1 %collective-permute-start.13 = (bf16[768,128]{1,0:T(8,128)(2,1)S(1)}, bf16[768,128]{1,0:T(8,128)(2,1)S(1)}, u32[]{:S(2)}, u32[]{:S(2)}) collective-permute-start(bf16[768,128]{1,0:T(8,128)(2,1)S(1)} %get-tuple-element.95), channel_id=1, source_target_pairs={{0,12},{4,8},{8,4},{12,0},{16,28},{20,24},{24,20},{28,16},{1,13},{... | collective-permute-start | bytes 589832 | tf_op jit(solution)/shard_map/ppermute | solution.py:709
  53.1 11.1 %collective-permute-start.18 = (bf16[768,128]{1,0:T(8,128)(2,1)S(1)}, bf16[768,128]{1,0:T(8,128)(2,1)S(1)}, u32[]{:S(2)}, u32[]{:S(2)}) collective-permute-start(bf16[768,128]{1,0:T(8,128)(2,1)S(1)} %get-tuple-element.105), channel_id=1, source_target_pairs={{0,4},{4,0},{8,12},{12,8},{16,20},{20,16},{24,28},{28,24},{1,5},{5... | collective-permute-start | bytes 589832 | tf_op jit(solution)/shard_map/ppermute | solution.py:709
  54.8 15.6 %collective-permute-start.19 = (bf16[768,128]{1,0:T(8,128)(2,1)S(1)}, bf16[768,128]{1,0:T(8,128)(2,1)S(1)}, u32[]{:S(2)}, u32[]{:S(2)}) collective-permute-start(bf16[768,128]{1,0:T(8,128)(2,1)S(1)} %get-tuple-element.106), channel_id=1, source_target_pairs={{0,8},{4,12},{8,0},{12,4},{16,24},{20,28},{24,16},{28,20},{1,9},{5... | collective-permute-start | bytes 589832 | tf_op jit(solution)/shard_map/ppermute | solution.py:709
  56.3 14.0 %collective-permute-start.20 = (bf16[768,128]{1,0:T(8,128)(2,1)S(1)}, bf16[768,128]{1,0:T(8,128)(2,1)S(1)}, u32[]{:S(2)}, u32[]{:S(2)}) collective-permute-start(bf16[768,128]{1,0:T(8,128)(2,1)S(1)} %get-tuple-element.107), channel_id=1, source_target_pairs={{0,12},{4,8},{8,4},{12,0},{16,28},{20,24},{24,20},{28,16},{1,13},{... | collective-permute-start | bytes 589832 | tf_op jit(solution)/shard_map/ppermute | solution.py:709
  59.6 10.7 %collective-permute-start.14 = (bf16[384,128]{1,0:T(8,128)(2,1)S(1)}, bf16[384,128]{1,0:T(8,128)(2,1)S(1)}, u32[]{:S(2)}, u32[]{:S(2)}) collective-permute-start(bf16[384,128]{1,0:T(8,128)(2,1)S(1)} %get-tuple-element.96), channel_id=1, source_target_pairs={{0,16},{4,20},{8,24},{12,28},{16,0},{20,4},{24,8},{28,12},{1,17},{... | collective-permute-start | bytes 294920 | tf_op jit(solution)/shard_map/ppermute | solution.py:709
  62.9 15.4 %collective-permute-start.15 = (bf16[384,128]{1,0:T(8,128)(2,1)S(1)}, bf16[384,128]{1,0:T(8,128)(2,1)S(1)}, u32[]{:S(2)}, u32[]{:S(2)}) collective-permute-start(bf16[384,128]{1,0:T(8,128)(2,1)S(1)} %get-tuple-element.97), channel_id=1, source_target_pairs={{0,20},{4,16},{8,28},{12,24},{16,4},{20,0},{24,12},{28,8},{1,21},{... | collective-permute-start | bytes 294920 | tf_op jit(solution)/shard_map/ppermute | solution.py:709
  64.2 14.1 %collective-permute-start.16 = (bf16[384,128]{1,0:T(8,128)(2,1)S(1)}, bf16[384,128]{1,0:T(8,128)(2,1)S(1)}, u32[]{:S(2)}, u32[]{:S(2)}) collective-permute-start(bf16[384,128]{1,0:T(8,128)(2,1)S(1)} %get-tuple-element.98), channel_id=1, source_target_pairs={{0,24},{4,28},{8,16},{12,20},{16,8},{20,12},{24,0},{28,4},{1,25},{... | collective-permute-start | bytes 294920 | tf_op jit(solution)/shard_map/ppermute | solution.py:709
  70.3 8.0 %collective-permute-start.17 = (bf16[384,128]{1,0:T(8,128)(2,1)S(1)}, bf16[384,128]{1,0:T(8,128)(2,1)S(1)}, u32[]{:S(2)}, u32[]{:S(2)}) collective-permute-start(bf16[384,128]{1,0:T(8,128)(2,1)S(1)} %get-tuple-element.99), channel_id=1, source_target_pairs={{0,28},{4,24},{8,20},{12,16},{16,12},{20,8},{24,4},{28,0},{1,29},{... | collective-permute-start | bytes 294920 | tf_op jit(solution)/shard_map/ppermute | solution.py:709
  78.7 3.1 %collective-permute-start.23 = (f32[8,128]{1,0:T(8,128)S(1)}, f32[8,128]{1,0:T(8,128)S(1)}, u32[]{:S(2)}, u32[]{:S(2)}) collective-permute-start(f32[8,128]{1,0:T(8,128)S(1)} %shard_map.98), channel_id=1, source_target_pairs={{0,3},{1,2},{2,1},{3,0},{4,7},{5,6},{6,5},{7,4},{8,11},{9,10},{10,... | collective-permute-start | bytes 12296 | tf_op jit(solution)/shard_map/ppermute | solution.py:734
  78.8 3.7 %collective-permute-start.22 = (f32[8,128]{1,0:T(8,128)S(1)}, f32[8,128]{1,0:T(8,128)S(1)}, u32[]{:S(2)}, u32[]{:S(2)}) collective-permute-start(f32[8,128]{1,0:T(8,128)S(1)} %shard_map.98), channel_id=1, source_target_pairs={{0,2},{1,3},{2,0},{3,1},{4,6},{5,7},{6,4},{7,5},{8,10},{9,11},{10,... | collective-permute-start | bytes 12296 | tf_op jit(solution)/shard_map/ppermute | solution.py:734
  (7 other events, 68.0 us)

commit v2 on v1

--- a/solution.py
+++ b/solution.py
@@ -331,33 +331,68 @@
             second_all[rows, :] = cross_ref[self.tokens : 2 * self.tokens, columns]
 
 
-def tile_scores(query_tile, pieces):
-    results = []
-    for key_all, _, limit, first in pieces:
-        scores = contract_last(query_tile, key_all[:limit, :])
-        if first is not None:
-            column_index = lax.broadcasted_iota(jnp.int32, scores.shape, 1)
-            row_index = lax.broadcasted_iota(jnp.int32, scores.shape, 0) + first
-            scores = jnp.where(column_index <= row_index, scores, NEG_FILL)
-        results.append(scores)
-    return results
+class Keys:
+    def __init__(self, key, value, key_turned=None, value_turned=None):
+        self.key, self.value = key, value
+        self.key_turned, self.value_turned = key_turned, value_turned
+
+    def turn(self):
+        self.key_turned[...] = jnp.transpose(self.key[:, :HEAD_DIM])
+        self.value_turned[...] = jnp.transpose(self.value[...])
+
+
+def tile_scores(query_tile, keys, limit, first):
+    scores = contract_last(keys.key[:limit, :], query_tile)
+    if first is not None:
+        key_index = lax.broadcasted_iota(jnp.int32, scores.shape, 0)
+        query_index = lax.broadcasted_iota(jnp.int32, scores.shape, 1) + first
+        scores = jnp.where(key_index <= query_index, scores, NEG_FILL)
+    return scores
 
 
 def tile_stats(scores, prob_grads):
     row_max = functools.reduce(
-        jnp.maximum, [jnp.max(part, axis=1, keepdims=True) for part in scores]
+        jnp.maximum, [jnp.max(part, axis=0, keepdims=True) for part in scores]
     )
     weights = [jnp.exp2((part - row_max) * EXPONENT_SCALE) for part in scores]
-    row_total = sum(jnp.sum(part, axis=1, keepdims=True) for part in weights)
+    row_total = sum(jnp.sum(part, axis=0, keepdims=True) for part in weights)
     row_delta = sum(
-        jnp.sum(part * grad, axis=1, keepdims=True) for part, grad in zip(weights, prob_grads)
+        jnp.sum(part * grad, axis=0, keepdims=True) for part, grad in zip(weights, prob_grads)
     )
     return weights, row_max, row_total, row_delta
 
 
-def tile_backward(query_tile, grad_tile, pieces, sums, stats, is_first):
-    scores = tile_scores(query_tile, pieces)
-    prob_grads = [contract_last(grad_tile, piece[1][: piece[2], :]) for piece in pieces]
+def tile_products(query_tile, grad_tile, pieces):
+    scores = [tile_scores(query_tile, *piece) for piece in pieces]
+    return scores, [contract_last(keys.value[:limit, :], grad_tile) for keys, limit, _ in pieces]
+
+
+def all_tiles(query_all, grad_all, half_len, pieces_of, sums, stats_of, keep, add=False):
+    tiles = own_tiles(half_len)
+    ready = None
+    for index, (first, rows, limit) in enumerate(tiles):
+        now = ready or tile_products(query_all[rows, :], grad_all[rows, :], pieces_of(first, limit))
+        ready = None
+        if index + 1 < len(tiles):
+            later, later_rows, later_limit = tiles[index + 1]
+            ready = tile_products(
+                query_all[later_rows, :], grad_all[later_rows, :], pieces_of(later, later_limit)
+            )
+        keep(
+            rows,
+            *tile_backward(
+                query_all[rows, :],
+                grad_all[rows, :],
+                pieces_of(first, limit),
+                sums,
+                stats_of(first, limit - first) if stats_of else None,
+                first == 0 and not add,
+                *now,
+            ),
+        )
+
+
+def tile_backward(query_tile, grad_tile, pieces, sums, stats, is_first, scores, prob_grads):
     if stats is None:
         weights, _, row_total, row_delta = tile_stats(scores, prob_grads)
         inverse = 1.0 / jnp.maximum(row_total, 1.0)
@@ -366,16 +401,20 @@
         row_max, inverse, row_delta = stats
         weights = [jnp.exp2((part - row_max) * EXPONENT_SCALE) for part in scores]
     attended, query_grad = 0.0, 0.0
-    for index, (key_all, value_all, limit, first) in enumerate(pieces):
+    for index, (keys, limit, first) in enumerate(pieces):
         probabilities = weights[index] * inverse
         prob_half = probabilities.astype(jnp.bfloat16)
         score_grad = (probabilities * (prob_grads[index] - row_delta)).astype(jnp.bfloat16)
-        attended += jnp.dot(prob_half, value_all[:limit, :], preferred_element_type=jnp.float32)
+        attended += jnp.dot(
+            keys.value_turned[:, :limit], prob_half, preferred_element_type=jnp.float32
+        )
         query_grad += jnp.dot(
-            score_grad, key_all[:limit, :HEAD_DIM], preferred_element_type=jnp.float32
+            keys.key_turned[:, :limit], score_grad, preferred_element_type=jnp.float32
         )
-        key_part = contract_first(score_grad, query_tile[:, :HEAD_DIM])
-        value_part = contract_first(prob_half, grad_tile)
+        key_part = jnp.dot(
+            score_grad, query_tile[:, :HEAD_DIM], preferred_element_type=jnp.float32
+        )
+        value_part = jnp.dot(prob_half, grad_tile, preferred_element_type=jnp.float32)
         key_sum, value_sum = sums[index]
         fresh = 0 if is_first else (limit if first is None else first)
         if fresh:
@@ -384,7 +423,10 @@
         if fresh < limit:
             key_sum[fresh:limit, :] = key_part[fresh:]
             value_sum[fresh:limit, :] = value_part[fresh:]
-    return attended.astype(jnp.bfloat16), (query_grad * SCORE_SCALE).astype(jnp.bfloat16)
+    return (
+        jnp.transpose(attended).astype(jnp.bfloat16),
+        jnp.transpose(query_grad * SCORE_SCALE).astype(jnp.bfloat16),
+    )
 
 
 def own_tiles(half_len):
@@ -421,11 +463,14 @@
         slots.own(single + column, query_all, key_all, value_all, grad_all)
 
         def note(first, rows, limit, causal_from):
-            pieces = [(key_all, value_all, limit, causal_from)]
-            scores = tile_scores(query_all[rows, :], pieces)
-            prob_grad = contract_last(grad_all[rows, :], value_all[:limit, :])
-            for place, found in enumerate(tile_stats(scores, [prob_grad])[1:]):
-                store_as_rows(out_ref, (3 * head + place) * stat_rows + first // LANES, found)
+            scores = tile_scores(query_all[rows, :], Keys(key_all, value_all), limit, causal_from)
+            prob_grad = contract_last(value_all[:limit, :], grad_all[rows, :])
+            for place, found in enumerate(tile_stats([scores], [prob_grad])[1:]):
+                row = (3 * head + place) * stat_rows + first // LANES
+                for start in range(0, found.shape[1], LANES):
+                    out_ref[row + start // LANES : row + start // LANES + 1, :] = found[
+                        :, start : start + LANES
+                    ]
 
         @pl.when(slots.is_high)
         def _():
@@ -457,7 +502,10 @@
     result_refs, cross_out_refs = refs[:half_count], refs[half_count : 2 * half_count]
     second_ref, sums_ref = refs[2 * half_count : 2 * half_count + 2]
     (query_all, key_all, value_all, grad_all, other_key, other_value, ids, other_ids, attended,
-     query_grad, key_sum, value_sum, other_key_sum, other_value_sum) = refs[2 * half_count + 2 :]
+     query_grad, key_sum, value_sum, other_key_sum, other_value_sum, *turned) = refs[
+        2 * half_count + 2 :
+    ]
+    own, other = Keys(key_all, value_all, *turned[:2]), Keys(other_key, other_value, *turned[2:])
     slots = Slots(shape, me_ref, pattern_ref, packed_ref, key_refs, cross_refs)
     single = packed_ref.shape[1] // 2
     half_len = slots.half_len
@@ -467,15 +515,18 @@
     slots.query_features(ids, query_all, high)
 
     def run(others, other_sums, attended_out, query_grad_out, key_out, value_out):
-        for first, rows, limit in own_tiles(half_len):
-            attended_out[rows, :], query_grad_out[rows, :] = tile_backward(
-                query_all[rows, :],
-                grad_all[rows, :],
-                others + [(key_all, value_all, limit, first)],
-                other_sums + [(key_out, value_out)],
-                None,
-                first == 0,
-            )
+        def keep(rows, attended_tile, query_grad_tile):
+            attended_out[rows, :], query_grad_out[rows, :] = attended_tile, query_grad_tile
+
+        all_tiles(
+            query_all,
+            grad_all,
+            half_len,
+            lambda first, limit: others + [(own, limit, first)],
+            other_sums + [(key_out, value_out)],
+            None,
+            keep,
+        )
 
     @pl.when(slots.is_high)
     def _():
@@ -486,12 +537,14 @@
         column = head * HEAD_DIM
         columns = slice(column, column + HEAD_DIM)
         slots.own(column, query_all, key_all, value_all, grad_all)
+        own.turn()
 
         @pl.when(slots.is_high)
         def _():
             slots.cross(column, other_key, other_value)
+            other.turn()
             run(
-                [(other_key, other_value, half_len, None)],
+                [(other, half_len, None)],
                 [(other_key_sum, other_value_sum)],
                 attended, query_grad, key_sum, value_sum,
             )
@@ -512,6 +565,7 @@
         @pl.when(jnp.logical_not(slots.is_high))
         def _():
             slots.own(single + column, query_all, key_all, value_all, grad_all)
+            own.turn()
             run(
                 [], [],
                 second_ref.at[:half_len, columns],
@@ -545,7 +599,10 @@
         refs[place * half_count : (place + 1) * half_count] for place in range(3)
     ]
     (query_all, key_all, value_all, grad_all, other_query, other_grad, ids, other_ids, attended,
-     query_grad, key_sum, value_sum, other_attended, other_query_grad) = refs[3 * half_count :]
+     query_grad, key_sum, value_sum, other_attended, other_query_grad, *turned) = refs[
+        3 * half_count :
+    ]
+    own = Keys(key_all, value_all, *turned)
     slots = Slots(shape, me_ref, pattern_ref, packed_ref, key_refs, cross_refs)
     single = packed_ref.shape[1] // 2
     half_len, tokens = slots.half_len, slots.tokens
@@ -567,22 +624,30 @@
         column = head * HEAD_DIM
         columns = slice(column, column + HEAD_DIM)
         slots.own(single + column, query_all, key_all, value_all, grad_all)
+        own.turn()
         joint_table = joint_rows(stat_rows, head, own_stats_ref, far_stats_ref)
 
         def joint_stats(first, size):
-            return [column_of(rows, first // LANES, size) for rows in joint_table]
+            places = range(first // LANES, (first + size) // LANES)
+            return [
+                jnp.concatenate([rows[place : place + 1, :] for place in places], axis=1)
+                for rows in joint_table
+            ]
 
         @pl.when(slots.is_high)
         def _():
-            for first, rows, limit in own_tiles(half_len):
-                attended[rows, :], query_grad[rows, :] = tile_backward(
-                    query_all[rows, :],
-                    grad_all[rows, :],
-                    [(key_all, value_all, limit, first)],
-                    [(key_sum, value_sum)],
-                    joint_stats(first, limit - first),
-                    first == 0,
-                )
+            def keep(rows, attended_tile, query_grad_tile):
+                attended[rows, :], query_grad[rows, :] = attended_tile, query_grad_tile
+
+            all_tiles(
+                query_all,
+                grad_all,
+                half_len,
+                lambda first, limit: [(own, limit, first)],
+                [(key_sum, value_sum)],
+                joint_stats,
+                keep,
+            )
 
         @pl.when(jnp.logical_not(slots.is_high))
         def _():
@@ -591,15 +656,20 @@
             query_grad[...] = early_ref[half_len:, columns]
             key_sum[...] = sums_ref[:half_len, columns]
             value_sum[...] = sums_ref[half_len:, columns]
-            for first, rows, limit in own_tiles(half_len):
-                other_attended[rows, :], other_query_grad[rows, :] = tile_backward(
-                    other_query[rows, :],
-                    other_grad[rows, :],
-                    [(key_all, value_all, half_len, None)],
-                    [(key_sum, value_sum)],
-                    joint_stats(first, limit - first),
-                    False,
-                )
+
+            def keep(rows, attended_tile, query_grad_tile):
+                other_attended[rows, :], other_query_grad[rows, :] = attended_tile, query_grad_tile
+
+            all_tiles(
+                other_query,
+                other_grad,
+                half_len,
+                lambda first, limit: [(own, half_len, None)],
+                [(key_sum, value_sum)],
+                joint_stats,
+                keep,
+                add=True,
+            )
             for distance in range(half_count):
                 rows = block_rows(slots.inside ^ distance, tokens)
                 target = cross_out_refs[distance]
@@ -639,46 +709,65 @@
     store_as_rows(out_ref, 0, column)
 
 
-def final_kernel(half_count, feature_total, me_ref, key_ref, rms_ref, inner_ref, *refs):
+def key_kernel(half_count, feature_total, me_ref, key_ref, rms_ref, inner_ref, *refs):
     cross_refs, first_refs, second_refs = [
         refs[place * half_count : (place + 1) * half_count] for place in range(3)
     ]
-    attended_ref, query_ref, key_out_ref, value_ref = refs[3 * half_count :]
+    key_out_ref = refs[3 * half_count]
     tokens, features = key_ref.shape
     width = features // half_count
-    single = width // 2
-    is_high = me_ref[0] >= half_count
     inside = me_ref[0] & (half_count - 1)
     rms = column_of(rms_ref[...], 0, tokens)
     inner = column_of(inner_ref[...], 0, tokens) / feature_total
     for distance in range(half_count):
-        owner = inside ^ distance
-        start = pl.multiple_of(owner * width, LANES)
-        columns = pl.ds(start, width)
+        columns = pl.ds(pl.multiple_of((inside ^ distance) * width, LANES), width)
         normed_float = key_ref[:, columns].astype(jnp.float32) / rms
         grad_float = normed_grad_of(
             half_count, me_ref, first_refs[distance], second_refs[distance], cross_refs[distance]
         )
         key_out_ref[:, columns] = ((grad_float - normed_float * inner) / rms).astype(jnp.bfloat16)
+
+
+def final_kernel(half_count, me_ref, *refs):
+    cross_refs, first_refs, second_refs = [
+        refs[place * half_count : (place + 1) * half_count] for place in range(3)
+    ]
+    attended_ref, query_ref, value_ref = refs[3 * half_count :]
+    tokens, features = attended_ref.shape
+    width = features // half_count
+    single = width // 2
+    is_high = me_ref[0] >= half_count
+    inside = me_ref[0] & (half_count - 1)
+    for distance in range(half_count):
+        start = pl.multiple_of((inside ^ distance) * width, LANES)
+        first = pl.ds(start, single)
+        second = pl.ds(pl.multiple_of(start + single, LANES), single)
         cross_ref = cross_refs[distance]
-        second = pl.ds(pl.multiple_of(start + single, LANES), single)
-        for place, target in enumerate((attended_ref, query_ref, value_ref)):
-            rows = slice(place * tokens, (place + 1) * tokens)
-            target[:, pl.ds(start, single)] = first_refs[distance][rows, :]
-            target[:, second] = second_refs[distance][rows, :]
-
-        def add(target, columns, first):
-            far = cross_ref[first : first + tokens, :].astype(jnp.float32)
-            target[:, columns] = (target[:, columns].astype(jnp.float32) + far).astype(jnp.bfloat16)
+
+        def block(refs, place):
+            return refs[distance][place * tokens : (place + 1) * tokens, :]
+
+        def joined(refs, place, far):
+            whole = block(refs, place).astype(jnp.float32) + cross_ref[
+                far * tokens : (far + 1) * tokens, :
+            ].astype(jnp.float32)
+            return whole.astype(jnp.bfloat16)
+
+        attended_ref[:, first] = block(first_refs, 0)
+        query_ref[:, first] = block(first_refs, 1)
+        value_ref[:, second] = block(second_refs, 2)
 
         @pl.when(is_high)
         def _():
-            add(attended_ref, second, 0)
-            add(query_ref, second, tokens)
+            attended_ref[:, second] = joined(second_refs, 0, 0)
+            query_ref[:, second] = joined(second_refs, 1, 1)
+            value_ref[:, first] = block(first_refs, 2)
 
         @pl.when(jnp.logical_not(is_high))
         def _():
-            add(value_ref, pl.ds(start, single), tokens)
+            attended_ref[:, second] = block(second_refs, 0)
+            query_ref[:, second] = block(second_refs, 1)
+            value_ref[:, first] = joined(first_refs, 2, 1)
 
 
 def lane_rows(vector, row_count):
@@ -778,7 +867,7 @@
     )
     keys = swap_inside(sent[:half_count])
     cross_sent = list(sent[half_count:])
-    for distance in range(half_count // 2, half_count):
+    for distance in range(half_count // 2):
         cross_sent[distance], keys[1] = lax.optimization_barrier((cross_sent[distance], keys[1]))
     cross = swap_across(cross_sent)
     pattern_rows = block_pattern.transpose(1, 0, 2).reshape(block_count, -1).astype(jnp.float32)
@@ -786,6 +875,7 @@
     wide = pltpu.VMEM((half_len, 2 * HEAD_DIM), jnp.bfloat16)
     slim = pltpu.VMEM((half_len, HEAD_DIM), jnp.bfloat16)
     sums = pltpu.VMEM((half_len, HEAD_DIM), jnp.float32)
+    turned = pltpu.VMEM((HEAD_DIM, half_len), jnp.bfloat16)
     ids_column = pltpu.VMEM((half_len, 1), jnp.float32)
     block_flops = 12 * half_len * half_len * single
     inputs = [pattern_rows, packed] + cross + keys
@@ -809,7 +899,7 @@
         [me],
         inputs + [stats],
         [wide, wide, slim, slim, wide, slim, ids_column, ids_column, slim, slim]
-        + [sums, sums, sums, sums],
+        + [sums, sums, sums, sums] + [turned] * 4,
         flops=block_flops + block_flops // 2,
     )
     *firsts, far_stats = lax.optimization_barrier((*firsts, far_stats))
@@ -822,13 +912,15 @@
         [me],
         inputs + [stats, far_stats] + rest[half_count:] + rest[:half_count],
         [wide, wide, slim, slim, wide, slim, ids_column, ids_column, slim, slim]
-        + [sums, sums, slim, slim],
+        + [sums, sums, slim, slim] + [turned] * 2,
         flops=block_flops,
     )
-    far_sent = list(results[half_count:])
-    far_sent, firsts = lax.optimization_barrier((far_sent, firsts))
+    far_sent, seconds = list(results[half_count:]), list(results[:half_count])
+    near = half_count // 2
+    far_sent[:near], firsts = lax.optimization_barrier((far_sent[:near], firsts))
     far_parts = swap_across(far_sent)
-    seconds = swap_inside(results[:half_count])
+    seconds, far_parts[-1] = lax.optimization_barrier((seconds, far_parts[-1]))
+    seconds = swap_inside(seconds)
     inner = call(
         functools.partial(inner_kernel, half_count),
         jax.ShapeDtypeStruct((row_count, LANES), jnp.float32),
@@ -836,14 +928,19 @@
         [key_vectors, key_rms] + far_parts + firsts + seconds,
     )
     inner = sum_over_head(inner)
-    return tuple(
-        call(
-            functools.partial(final_kernel, half_count, feature_total),
-            [half_array(tokens, features)] * 4,
-            [me],
-            [key_vectors, key_rms, inner] + far_parts + firsts + seconds,
-        )
-    )
+    attended, query_grad, value_grad = call(
+        functools.partial(final_kernel, half_count),
+        [half_array(tokens, features)] * 3,
+        [me],
+        far_parts + firsts + seconds,
+    )
+    key_grad = call(
+        functools.partial(key_kernel, half_count, feature_total),
+        half_array(tokens, features),
+        [me],
+        [key_vectors, key_rms, inner] + far_parts + firsts + seconds,
+    )
+    return attended, query_grad, key_grad, value_grad
 
 
 def per_device_any(queries, key_vectors, values, cotangent, cluster, block_pattern):

time: 84.8 us -> 82.9 us (0.978)
  starting transfers between devices: 38.4 us -> 36.9 us
    ppermute x18, waiting for transfers between devices: 25.1 us -> 27.1 us  [swap(): return lax.ppermute(block, 'seq', [(i, i ^ distance) for i in range(count)])]
    ppermute x18, starting transfers between devices: 29.1 us -> 27.6 us  [swap(): return lax.ppermute(block, 'seq', [(i, i ^ distance) for i in range(count)])]
    ppermute x6, waiting for transfers between devices: 4.22 us -> 2.85 us  [sum_over_head(): lax.ppermute(block, 'head', [(i, i ^ d) for i in range(count)])]
    pallas_call x7 -> x8, Pallas kernels: 15.5 us -> 14.7 us  [call(): pl.pallas_call(kernel, out_shape=out_shapes, in_specs=[pl.BlockSpec(memor...]
  transfers between devices with their start and end apart: 25 -> 25, of which waited for: 10 -> 13; matrix products, arithmetic and copies ran while one was open for 0% -> 0% of each run, Pallas kernels for 11% -> 11%
where the time goes in v2:
time: 82.9 us; the launch traced here: 82.7 us
  starting transfers between devices  36.9 us (45%)
  waiting for transfers between devices  30 us (36%)
  Pallas kernels  14.7 us (18%)
    ppermute x18, starting transfers between devices, swap(): return lax.ppermute(block, 'seq', [(i, i ^ distance) for i in range(count)])  27.6 us
    ppermute x18, waiting for transfers between devices, swap(): return lax.ppermute(block, 'seq', [(i, i ^ distance) for i in range(count)])  27.1 us
    pallas_call x8, Pallas kernels, call(): pl.pallas_call(kernel, out_shape=out_shapes, in_specs=[pl.BlockSpec(memor...  14.7 us
    all_to_all x1, starting transfers between devices, exchange_inside(): lax.all_to_all(parts, 'seq', split_axis=0, concat_axis=0, tiled=True, axi...  5.39 us
    ppermute x6, starting transfers between devices, sum_over_head(): lax.ppermute(block, 'head', [(i, i ^ d) for i in range(count)])  3.84 us
    ppermute x6, waiting for transfers between devices, sum_over_head(): lax.ppermute(block, 'head', [(i, i ^ d) for i in range(count)])  2.85 us
  transfers between devices with their start and end apart: 25, of which 13 were waited for; matrix products, arithmetic and copies ran while one was open for 0% of the time, Pallas kernels for 11%

profile of v2, /device:TPU:0, one launch (start us, length us, event | category | flops | bytes accessed | tf_op | source)
XLA Modules:
  0.0 82.7 jit_solution(17599433181275908423)
XLA Ops:
  0.6 2.2 %shard_map.93 = bf16[2304,256]{1,0:T(8,128)(2,1)} custom-call(bf16[192,1024]{1,0:T(8,128)(2,1)} %query_ref.3, bf16[192,1024]{1,0:T(8,128)(2,1)} %value_ref.3, bf16[192,1024]{1,0:T(8,128)(2,1)} %grad_ref.3), custom_call_target="tpu_custom_call" | custom-call | tf_op jit(solution)/shard_map/pallas_call | solution.py:783
  2.9 5.4 %all-to-all-start = ((bf16[4,576,256]{2,1,0:T(8,128)(2,1)}), bf16[4,576,256]{2,1,0:T(8,128)(2,1)S(1)}, u32[]{:S(2)}, u32[]{:S(2)}) async-start(bf16[4,576,256]{2,1,0:T(8,128)(2,1)} %bitcast.14), calls=%async_computation | async-start | bytes 2359296 | tf_op jit(solution)/shard_map/all_to_all | solution.py:813
  13.2 1.8 %collective-permute-start.3 = (bf16[208,256]{1,0:T(8,128)(2,1)S(1)}, bf16[208,256]{1,0:T(8,128)(2,1)S(1)}, u32[]{:S(2)}, u32[]{:S(2)}) collective-permute-start(bf16[208,256]{1,0:T(8,128)(2,1)S(1)} %get-tuple-element.66), channel_id=1, source_target_pairs={{0,4},{4,0},{8,12},{12,8},{16,20},{20,16},{24,28},{28,24},{1,5},{5... | collective-permute-start | bytes 319496 | tf_op jit(solution)/shard_map/ppermute | solution.py:798
  15.0 3.5 %collective-permute-start.6 = (bf16[400,128]{1,0:T(8,128)(2,1)S(1)}, bf16[400,128]{1,0:T(8,128)(2,1)S(1)}, u32[]{:S(2)}, u32[]{:S(2)}) collective-permute-start(bf16[400,128]{1,0:T(8,128)(2,1)S(1)} %get-tuple-element.71), channel_id=1, source_target_pairs={{0,24},{4,28},{8,16},{12,20},{16,8},{20,12},{24,0},{28,4},{1,25},{... | collective-permute-start | bytes 307208 | tf_op jit(solution)/shard_map/ppermute | solution.py:798
  18.6 3.2 %collective-permute-start.9 = (bf16[208,256]{1,0:T(8,128)(2,1)S(1)}, bf16[208,256]{1,0:T(8,128)(2,1)S(1)}, u32[]{:S(2)}, u32[]{:S(2)}) collective-permute-start(bf16[208,256]{1,0:T(8,128)(2,1)S(1)} %get-tuple-element.76), channel_id=1, source_target_pairs={{0,12},{4,8},{8,4},{12,0},{16,28},{20,24},{24,20},{28,16},{1,13},{... | collective-permute-start | bytes 319496 | tf_op jit(solution)/shard_map/ppermute | solution.py:798
  21.8 3.8 %collective-permute-done.3.refs_5_ = bf16[208,256]{1,0:T(8,128)(2,1)S(1)} collective-permute-done((bf16[208,256]{1,0:T(8,128)(2,1)S(1)}, bf16[208,256]{1,0:T(8,128)(2,1)S(1)}, u32[]{:S(2)}, u32[]{:S(2)}) %collective-permute-start.3) | collective-permute-done | bytes 106528 | tf_op jit(solution)/shard_map/ppermute | solution.py:798
  25.6 4.4 %collective-permute-start.5 = (bf16[400,128]{1,0:T(8,128)(2,1)S(1)}, bf16[400,128]{1,0:T(8,128)(2,1)S(1)}, u32[]{:S(2)}, u32[]{:S(2)}) collective-permute-start(bf16[400,128]{1,0:T(8,128)(2,1)S(1)} %get-tuple-element.70), channel_id=1, source_target_pairs={{0,20},{4,16},{8,28},{12,24},{16,4},{20,0},{24,12},{28,8},{1,21},{... | collective-permute-start | bytes 307208 | tf_op jit(solution)/shard_map/ppermute | solution.py:798
  30.4 1.6 %collective-permute-done.7.refs_3_ = bf16[400,128]{1,0:T(8,128)(2,1)S(1)} collective-permute-done((bf16[400,128]{1,0:T(8,128)(2,1)S(1)}, bf16[400,128]{1,0:T(8,128)(2,1)S(1)}, u32[]{:S(2)}, u32[]{:S(2)}) %collective-permute-start.7) | collective-permute-done | bytes 102432 | tf_op jit(solution)/shard_map/ppermute | solution.py:798
  32.0 1.5 %collective-permute-done.8.refs_6_ = bf16[208,256]{1,0:T(8,128)(2,1)S(1)} collective-permute-done((bf16[208,256]{1,0:T(8,128)(2,1)S(1)}, bf16[208,256]{1,0:T(8,128)(2,1)S(1)}, u32[]{:S(2)}, u32[]{:S(2)}) %collective-permute-start.8) | collective-permute-done | bytes 106528 | tf_op jit(solution)/shard_map/ppermute | solution.py:798
  33.6 3.4 %collective-permute-done.9.refs_7_ = bf16[208,256]{1,0:T(8,128)(2,1)S(1)} collective-permute-done((bf16[208,256]{1,0:T(8,128)(2,1)S(1)}, bf16[208,256]{1,0:T(8,128)(2,1)S(1)}, u32[]{:S(2)}, u32[]{:S(2)}) %collective-permute-start.9) | collective-permute-done | bytes 106528 | tf_op jit(solution)/shard_map/ppermute | solution.py:798
  37.0 2.5 %collective-permute-done.4.refs_0_ = bf16[400,128]{1,0:T(8,128)(2,1)S(1)} collective-permute-done((bf16[400,128]{1,0:T(8,128)(2,1)S(1)}, bf16[400,128]{1,0:T(8,128)(2,1)S(1)}, u32[]{:S(2)}, u32[]{:S(2)}) %collective-permute-start.4) | collective-permute-done | bytes 102432 | tf_op jit(solution)/shard_map/ppermute | solution.py:798
  39.5 2.2 %shard_map.95.refs_8_ = f32[24,128]{1,0:T(8,128)S(1)} custom-call(s32[1]{0:T(128)} %bitcast.me_ref, f32[12,128]{1,0:T(8,128)S(1)} %pad.13.pattern_ref, bf16[2304,256]{1,0:T(8,128)(2,1)S(1)} %bitcast.11, bf16[400,128]{1,0:T(8,128)(2,1)S(1)} %collective-permute-done.4.refs_0_, bf16[400,128]{1,0:T(8,128)(2,1)S(1)} %collective-permute-done.5.refs_1_, ...), custom_call_target="tpu_custom_call" | custom-call | flops 301989888 | tf_op jit(solution)/shard_map/pallas_call | solution.py:783
  41.8 4.3 %shard_map.96 = (bf16[768,128]{1,0:T(8,128)(2,1)S(1)}, bf16[768,128]{1,0:T(8,128)(2,1)S(1)}, bf16[768,128]{1,0:T(8,128)(2,1)S(1)}, bf16[768,128]{1,0:T(8,128)(2,...) custom-call(s32[1]{0:T(128)} %bitcast.me_ref, ...), custom_call_target="tpu_custom_call" | custom-call | flops 1358954496 | tf_op jit(solution)/shard_map/pallas_call | solution.py:783
  47.6 2.8 %collective-permute-start.12 = (bf16[768,128]{1,0:T(8,128)(2,1)S(1)}, bf16[768,128]{1,0:T(8,128)(2,1)S(1)}, u32[]{:S(2)}, u32[]{:S(2)}) collective-permute-start(bf16[768,128]{1,0:T(8,128)(2,1)S(1)} %get-tuple-element.98), channel_id=1, source_target_pairs={{0,8},{4,12},{8,0},{12,4},{16,24},{20,28},{24,16},{28,20},{1,9},{5... | collective-permute-start | bytes 589832 | tf_op jit(solution)/shard_map/ppermute | solution.py:798
  50.4 2.8 %shard_map.97 = (bf16[768,128]{1,0:T(8,128)(2,1)S(1)}, bf16[768,128]{1,0:T(8,128)(2,1)S(1)}, bf16[768,128]{1,0:T(8,128)(2,1)S(1)}, bf16[768,128]{1,0:T(8,128)(2,...) custom-call(s32[1]{0:T(128)} %bitcast.me_ref, ...), custom_call_target="tpu_custom_call" | custom-call | flops 905969664 | tf_op jit(solution)/shard_map/pallas_call | solution.py:783
  53.1 1.9 %collective-permute-start.17 = (bf16[384,128]{1,0:T(8,128)(2,1)S(1)}, bf16[384,128]{1,0:T(8,128)(2,1)S(1)}, u32[]{:S(2)}, u32[]{:S(2)}) collective-permute-start(bf16[384,128]{1,0:T(8,128)(2,1)S(1)} %get-tuple-element.107), channel_id=1, source_target_pairs={{0,28},{4,24},{8,20},{12,16},{16,12},{20,8},{24,4},{28,0},{1,29},{... | collective-permute-start | bytes 294920 | tf_op jit(solution)/shard_map/ppermute | solution.py:798
  55.1 1.9 %collective-permute-start.16 = (bf16[384,128]{1,0:T(8,128)(2,1)S(1)}, bf16[384,128]{1,0:T(8,128)(2,1)S(1)}, u32[]{:S(2)}, u32[]{:S(2)}) collective-permute-start(bf16[384,128]{1,0:T(8,128)(2,1)S(1)} %get-tuple-element.102), channel_id=1, source_target_pairs={{0,24},{4,28},{8,16},{12,20},{16,8},{20,12},{24,0},{28,4},{1,25},{... | collective-permute-start | bytes 294920 | tf_op jit(solution)/shard_map/ppermute | solution.py:798
  57.0 4.7 %collective-permute-done.17.refs_3_ = bf16[384,128]{1,0:T(8,128)(2,1)S(1)} collective-permute-done((bf16[384,128]{1,0:T(8,128)(2,1)S(1)}, bf16[384,128]{1,0:T(8,128)(2,1)S(1)}, u32[]{:S(2)}, u32[]{:S(2)}) %collective-permute-start.17) | collective-permute-done | bytes 98336 | tf_op jit(solution)/shard_map/ppermute | solution.py:798
  62.0 3.3 %collective-permute-start.20 = (bf16[768,128]{1,0:T(8,128)(2,1)S(1)}, bf16[768,128]{1,0:T(8,128)(2,1)S(1)}, u32[]{:S(2)}, u32[]{:S(2)}) collective-permute-start(bf16[768,128]{1,0:T(8,128)(2,1)S(1)} %get-tuple-element.116), channel_id=1, source_target_pairs={{0,12},{4,8},{8,4},{12,0},{16,28},{20,24},{24,20},{28,16},{1,13},{... | collective-permute-start | bytes 589832 | tf_op jit(solution)/shard_map/ppermute | solution.py:798
  65.6 2.8 %collective-permute-start.14 = (bf16[384,128]{1,0:T(8,128)(2,1)S(1)}, bf16[384,128]{1,0:T(8,128)(2,1)S(1)}, u32[]{:S(2)}, u32[]{:S(2)}) collective-permute-start(bf16[384,128]{1,0:T(8,128)(2,1)S(1)} %get-tuple-element.100), channel_id=1, source_target_pairs={{0,16},{4,20},{8,24},{12,28},{16,0},{20,4},{24,8},{28,12},{1,17},{... | collective-permute-start | bytes 294920 | tf_op jit(solution)/shard_map/ppermute | solution.py:798
  68.6 4.3 %collective-permute-done.19.refs_10_ = bf16[768,128]{1,0:T(8,128)(2,1)S(1)} collective-permute-done((bf16[768,128]{1,0:T(8,128)(2,1)S(1)}, bf16[768,128]{1,0:T(8,128)(2,1)S(1)}, u32[]{:S(2)}, u32[]{:S(2)}) %collective-permute-start.19) | collective-permute-done | bytes 196640 | tf_op jit(solution)/shard_map/ppermute | solution.py:798
  72.9 4.5 %collective-permute-done.20.refs_11_ = bf16[768,128]{1,0:T(8,128)(2,1)S(1)} collective-permute-done((bf16[768,128]{1,0:T(8,128)(2,1)S(1)}, bf16[768,128]{1,0:T(8,128)(2,1)S(1)}, u32[]{:S(2)}, u32[]{:S(2)}) %collective-permute-start.20) | collective-permute-done | bytes 196640 | tf_op jit(solution)/shard_map/ppermute | solution.py:798
  77.8 1.6 %collective-permute-start.22 = (f32[8,128]{1,0:T(8,128)S(1)}, f32[8,128]{1,0:T(8,128)S(1)}, u32[]{:S(2)}, u32[]{:S(2)}) collective-permute-start(f32[8,128]{1,0:T(8,128)S(1)} %shard_map.99), channel_id=1, source_target_pairs={{0,2},{1,3},{2,0},{3,1},{4,6},{5,7},{6,4},{7,5},{8,10},{9,11},{10,... | collective-permute-start | bytes 12296 | tf_op jit(solution)/shard_map/ppermute | solution.py:823
  79.7 1.4 %shard_map.98 = (bf16[192,1024]{1,0:T(8,128)(2,1)}, bf16[192,1024]{1,0:T(8,128)(2,1)}, bf16[192,1024]{1,0:T(8,128)(2,1)}) custom-call(s32[1]{0:T(128)} %bitcast.me_ref, bf16[384,128]{1,0:T(8,128)(2,1)S(1)} %collective-permute-done.14.refs_0_, bf16[384,128]{1,0:T(8,128)(2,1)S(1)} %collective-permute-done.15.refs_1_, ...), custom_call_target="tpu_custom_call" | custom-call | tf_op jit(solution)/shard_map/pallas_call | solution.py:783
  (55 shorter events, 10.0 us)
Async XLA Ops:
  2.9 36.7 %all-to-all-start = ((bf16[4,576,256]{2,1,0:T(8,128)(2,1)}), bf16[4,576,256]{2,1,0:T(8,128)(2,1)S(1)}, u32[]{:S(2)}, u32[]{:S(2)}) async-start(bf16[4,576,256]{2,1,0:T(8,128)(2,1)} %bitcast.14), calls=%async_computation | async-start | bytes 2359296 | tf_op jit(solution)/shard_map/all_to_all | solution.py:813
  8.4 3.1 %collective-permute-start.2 = (f32[8,128]{1,0:T(8,128)S(1)}, f32[8,128]{1,0:T(8,128)S(1)}, u32[]{:S(2)}, u32[]{:S(2)}) collective-permute-start(f32[8,128]{1,0:T(8,128)S(1)} %pad_bitcast_fusion.1), channel_id=1, source_target_pairs={{0,3},{1,2},{2,1},{3,0},{4,7},{5,6},{6,5},{7,4},{8,11},{9,10},{10,... | collective-permute-start | bytes 12296 | tf_op jit(solution)/shard_map/ppermute | solution.py:823
  9.2 3.6 %collective-permute-start.1 = (f32[8,128]{1,0:T(8,128)S(1)}, f32[8,128]{1,0:T(8,128)S(1)}, u32[]{:S(2)}, u32[]{:S(2)}) collective-permute-start(f32[8,128]{1,0:T(8,128)S(1)} %pad_bitcast_fusion.1), channel_id=1, source_target_pairs={{0,2},{1,3},{2,0},{3,1},{4,6},{5,7},{6,4},{7,5},{8,10},{9,11},{10,... | collective-permute-start | bytes 12296 | tf_op jit(solution)/shard_map/ppermute | solution.py:823
  10.1 2.7 %collective-permute-start = (f32[8,128]{1,0:T(8,128)S(1)}, f32[8,128]{1,0:T(8,128)S(1)}, u32[]{:S(2)}, u32[]{:S(2)}) collective-permute-start(f32[8,128]{1,0:T(8,128)S(1)} %pad_bitcast_fusion.1), channel_id=1, source_target_pairs={{0,1},{1,0},{2,3},{3,2},{4,5},{5,4},{6,7},{7,6},{8,9},{9,8},{10,11... | collective-permute-start | bytes 12296 | tf_op jit(solution)/shard_map/ppermute | solution.py:823
  13.2 12.4 %collective-permute-start.3 = (bf16[208,256]{1,0:T(8,128)(2,1)S(1)}, bf16[208,256]{1,0:T(8,128)(2,1)S(1)}, u32[]{:S(2)}, u32[]{:S(2)}) collective-permute-start(bf16[208,256]{1,0:T(8,128)(2,1)S(1)} %get-tuple-element.66), channel_id=1, source_target_pairs={{0,4},{4,0},{8,12},{12,8},{16,20},{20,16},{24,28},{28,24},{1,5},{5... | collective-permute-start | bytes 319496 | tf_op jit(solution)/shard_map/ppermute | solution.py:798
  15.0 15.0 %collective-permute-start.6 = (bf16[400,128]{1,0:T(8,128)(2,1)S(1)}, bf16[400,128]{1,0:T(8,128)(2,1)S(1)}, u32[]{:S(2)}, u32[]{:S(2)}) collective-permute-start(bf16[400,128]{1,0:T(8,128)(2,1)S(1)} %get-tuple-element.71), channel_id=1, source_target_pairs={{0,24},{4,28},{8,16},{12,20},{16,8},{20,12},{24,0},{28,4},{1,25},{... | collective-permute-start | bytes 307208 | tf_op jit(solution)/shard_map/ppermute | solution.py:798
  18.5 13.5 %collective-permute-start.7 = (bf16[400,128]{1,0:T(8,128)(2,1)S(1)}, bf16[400,128]{1,0:T(8,128)(2,1)S(1)}, u32[]{:S(2)}, u32[]{:S(2)}) collective-permute-start(bf16[400,128]{1,0:T(8,128)(2,1)S(1)} %get-tuple-element.72), channel_id=1, source_target_pairs={{0,28},{4,24},{8,20},{12,16},{16,12},{20,8},{24,4},{28,0},{1,29},{... | collective-permute-start | bytes 307208 | tf_op jit(solution)/shard_map/ppermute | solution.py:798
  18.6 15.0 %collective-permute-start.8 = (bf16[208,256]{1,0:T(8,128)(2,1)S(1)}, bf16[208,256]{1,0:T(8,128)(2,1)S(1)}, u32[]{:S(2)}, u32[]{:S(2)}) collective-permute-start(bf16[208,256]{1,0:T(8,128)(2,1)S(1)} %get-tuple-element.75), channel_id=1, source_target_pairs={{0,8},{4,12},{8,0},{12,4},{16,24},{20,28},{24,16},{28,20},{1,9},{5... | collective-permute-start | bytes 319496 | tf_op jit(solution)/shard_map/ppermute | solution.py:798
  18.6 18.4 %collective-permute-start.9 = (bf16[208,256]{1,0:T(8,128)(2,1)S(1)}, bf16[208,256]{1,0:T(8,128)(2,1)S(1)}, u32[]{:S(2)}, u32[]{:S(2)}) collective-permute-start(bf16[208,256]{1,0:T(8,128)(2,1)S(1)} %get-tuple-element.76), channel_id=1, source_target_pairs={{0,12},{4,8},{8,4},{12,0},{16,28},{20,24},{24,20},{28,16},{1,13},{... | collective-permute-start | bytes 319496 | tf_op jit(solution)/shard_map/ppermute | solution.py:798
  25.6 11.4 %collective-permute-start.5 = (bf16[400,128]{1,0:T(8,128)(2,1)S(1)}, bf16[400,128]{1,0:T(8,128)(2,1)S(1)}, u32[]{:S(2)}, u32[]{:S(2)}) collective-permute-start(bf16[400,128]{1,0:T(8,128)(2,1)S(1)} %get-tuple-element.70), channel_id=1, source_target_pairs={{0,20},{4,16},{8,28},{12,24},{16,4},{20,0},{24,12},{28,8},{1,21},{... | collective-permute-start | bytes 307208 | tf_op jit(solution)/shard_map/ppermute | solution.py:798
  30.0 9.5 %collective-permute-start.4 = (bf16[400,128]{1,0:T(8,128)(2,1)S(1)}, bf16[400,128]{1,0:T(8,128)(2,1)S(1)}, u32[]{:S(2)}, u32[]{:S(2)}) collective-permute-start(bf16[400,128]{1,0:T(8,128)(2,1)S(1)} %get-tuple-element.67), channel_id=1, source_target_pairs={{0,16},{4,20},{8,24},{12,28},{16,0},{20,4},{24,8},{28,12},{1,17},{... | collective-permute-start | bytes 307208 | tf_op jit(solution)/shard_map/ppermute | solution.py:798
  41.7 4.7 %collective-permute-start.10 = (f32[24,128]{1,0:T(8,128)S(1)}, f32[24,128]{1,0:T(8,128)S(1)}, u32[]{:S(2)}, u32[]{:S(2)}) collective-permute-start(f32[24,128]{1,0:T(8,128)S(1)} %shard_map.95.refs_8_), channel_id=1, source_target_pairs={{0,16},{4,20},{8,24},{12,28},{16,0},{20,4},{24,8},{28,12},{1,17},{... | collective-permute-start | bytes 36872 | tf_op jit(solution)/shard_map/ppermute | solution.py:798
  46.4 15.6 %collective-permute-start.11 = (bf16[768,128]{1,0:T(8,128)(2,1)S(1)}, bf16[768,128]{1,0:T(8,128)(2,1)S(1)}, u32[]{:S(2)}, u32[]{:S(2)}) collective-permute-start(bf16[768,128]{1,0:T(8,128)(2,1)S(1)} %get-tuple-element.97), channel_id=1, source_target_pairs={{0,4},{4,0},{8,12},{12,8},{16,20},{20,16},{24,28},{28,24},{1,5},{5... | collective-permute-start | bytes 589832 | tf_op jit(solution)/shard_map/ppermute | solution.py:798
  47.6 14.4 %collective-permute-start.12 = (bf16[768,128]{1,0:T(8,128)(2,1)S(1)}, bf16[768,128]{1,0:T(8,128)(2,1)S(1)}, u32[]{:S(2)}, u32[]{:S(2)}) collective-permute-start(bf16[768,128]{1,0:T(8,128)(2,1)S(1)} %get-tuple-element.98), channel_id=1, source_target_pairs={{0,8},{4,12},{8,0},{12,4},{16,24},{20,28},{24,16},{28,20},{1,9},{5... | collective-permute-start | bytes 589832 | tf_op jit(solution)/shard_map/ppermute | solution.py:798
  53.1 8.6 %collective-permute-start.17 = (bf16[384,128]{1,0:T(8,128)(2,1)S(1)}, bf16[384,128]{1,0:T(8,128)(2,1)S(1)}, u32[]{:S(2)}, u32[]{:S(2)}) collective-permute-start(bf16[384,128]{1,0:T(8,128)(2,1)S(1)} %get-tuple-element.107), channel_id=1, source_target_pairs={{0,28},{4,24},{8,20},{12,16},{16,12},{20,8},{24,4},{28,0},{1,29},{... | collective-permute-start | bytes 294920 | tf_op jit(solution)/shard_map/ppermute | solution.py:798
  55.0 10.6 %collective-permute-start.13 = (bf16[768,128]{1,0:T(8,128)(2,1)S(1)}, bf16[768,128]{1,0:T(8,128)(2,1)S(1)}, u32[]{:S(2)}, u32[]{:S(2)}) collective-permute-start(bf16[768,128]{1,0:T(8,128)(2,1)S(1)} %get-tuple-element.99), channel_id=1, source_target_pairs={{0,12},{4,8},{8,4},{12,0},{16,28},{20,24},{24,20},{28,16},{1,13},{... | collective-permute-start | bytes 589832 | tf_op jit(solution)/shard_map/ppermute | solution.py:798
  55.1 13.4 %collective-permute-start.16 = (bf16[384,128]{1,0:T(8,128)(2,1)S(1)}, bf16[384,128]{1,0:T(8,128)(2,1)S(1)}, u32[]{:S(2)}, u32[]{:S(2)}) collective-permute-start(bf16[384,128]{1,0:T(8,128)(2,1)S(1)} %get-tuple-element.102), channel_id=1, source_target_pairs={{0,24},{4,28},{8,16},{12,20},{16,8},{20,12},{24,0},{28,4},{1,25},{... | collective-permute-start | bytes 294920 | tf_op jit(solution)/shard_map/ppermute | solution.py:798
  61.8 6.8 %collective-permute-start.18 = (bf16[768,128]{1,0:T(8,128)(2,1)S(1)}, bf16[768,128]{1,0:T(8,128)(2,1)S(1)}, u32[]{:S(2)}, u32[]{:S(2)}) collective-permute-start(bf16[768,128]{1,0:T(8,128)(2,1)S(1)} %get-tuple-element.114), channel_id=1, source_target_pairs={{0,4},{4,0},{8,12},{12,8},{16,20},{20,16},{24,28},{28,24},{1,5},{5... | collective-permute-start | bytes 589832 | tf_op jit(solution)/shard_map/ppermute | solution.py:798
  62.0 10.9 %collective-permute-start.19 = (bf16[768,128]{1,0:T(8,128)(2,1)S(1)}, bf16[768,128]{1,0:T(8,128)(2,1)S(1)}, u32[]{:S(2)}, u32[]{:S(2)}) collective-permute-start(bf16[768,128]{1,0:T(8,128)(2,1)S(1)} %get-tuple-element.115), channel_id=1, source_target_pairs={{0,8},{4,12},{8,0},{12,4},{16,24},{20,28},{24,16},{28,20},{1,9},{5... | collective-permute-start | bytes 589832 | tf_op jit(solution)/shard_map/ppermute | solution.py:798
  62.0 15.4 %collective-permute-start.20 = (bf16[768,128]{1,0:T(8,128)(2,1)S(1)}, bf16[768,128]{1,0:T(8,128)(2,1)S(1)}, u32[]{:S(2)}, u32[]{:S(2)}) collective-permute-start(bf16[768,128]{1,0:T(8,128)(2,1)S(1)} %get-tuple-element.116), channel_id=1, source_target_pairs={{0,12},{4,8},{8,4},{12,0},{16,28},{20,24},{24,20},{28,16},{1,13},{... | collective-permute-start | bytes 589832 | tf_op jit(solution)/shard_map/ppermute | solution.py:798
  65.6 11.8 %collective-permute-start.14 = (bf16[384,128]{1,0:T(8,128)(2,1)S(1)}, bf16[384,128]{1,0:T(8,128)(2,1)S(1)}, u32[]{:S(2)}, u32[]{:S(2)}) collective-permute-start(bf16[384,128]{1,0:T(8,128)(2,1)S(1)} %get-tuple-element.100), channel_id=1, source_target_pairs={{0,16},{4,20},{8,24},{12,28},{16,0},{20,4},{24,8},{28,12},{1,17},{... | collective-permute-start | bytes 294920 | tf_op jit(solution)/shard_map/ppermute | solution.py:798
  68.5 8.9 %collective-permute-start.15 = (bf16[384,128]{1,0:T(8,128)(2,1)S(1)}, bf16[384,128]{1,0:T(8,128)(2,1)S(1)}, u32[]{:S(2)}, u32[]{:S(2)}) collective-permute-start(bf16[384,128]{1,0:T(8,128)(2,1)S(1)} %get-tuple-element.101), channel_id=1, source_target_pairs={{0,20},{4,16},{8,28},{12,24},{16,4},{20,0},{24,12},{28,8},{1,21},{... | collective-permute-start | bytes 294920 | tf_op jit(solution)/shard_map/ppermute | solution.py:798
  77.8 3.3 %collective-permute-start.23 = (f32[8,128]{1,0:T(8,128)S(1)}, f32[8,128]{1,0:T(8,128)S(1)}, u32[]{:S(2)}, u32[]{:S(2)}) collective-permute-start(f32[8,128]{1,0:T(8,128)S(1)} %shard_map.99), channel_id=1, source_target_pairs={{0,3},{1,2},{2,1},{3,0},{4,7},{5,6},{6,5},{7,4},{8,11},{9,10},{10,... | collective-permute-start | bytes 12296 | tf_op jit(solution)/shard_map/ppermute | solution.py:823
  77.8 3.7 %collective-permute-start.22 = (f32[8,128]{1,0:T(8,128)S(1)}, f32[8,128]{1,0:T(8,128)S(1)}, u32[]{:S(2)}, u32[]{:S(2)}) collective-permute-start(f32[8,128]{1,0:T(8,128)S(1)} %shard_map.99), channel_id=1, source_target_pairs={{0,2},{1,3},{2,0},{3,1},{4,6},{5,7},{6,4},{7,5},{8,10},{9,11},{10,... | collective-permute-start | bytes 12296 | tf_op jit(solution)/shard_map/ppermute | solution.py:823
  (7 other events, 67.1 us)

commit v3 on v2

--- a/solution.py
+++ b/solution.py
@@ -866,10 +866,7 @@
         [queries, values, cotangent, key_vectors, key_rms, ids],
     )
     keys = swap_inside(sent[:half_count])
-    cross_sent = list(sent[half_count:])
-    for distance in range(half_count // 2):
-        cross_sent[distance], keys[1] = lax.optimization_barrier((cross_sent[distance], keys[1]))
-    cross = swap_across(cross_sent)
+    cross = swap_across(sent[half_count:])
     pattern_rows = block_pattern.transpose(1, 0, 2).reshape(block_count, -1).astype(jnp.float32)
     pattern_rows = jnp.pad(pattern_rows, ((0, 0), (0, LANES - cluster_count * block_count)))
     wide = pltpu.VMEM((half_len, 2 * HEAD_DIM), jnp.bfloat16)
@@ -917,9 +914,8 @@
     )
     far_sent, seconds = list(results[half_count:]), list(results[:half_count])
     near = half_count // 2
-    far_sent[:near], firsts = lax.optimization_barrier((far_sent[:near], firsts))
     far_parts = swap_across(far_sent)
-    seconds, far_parts[-1] = lax.optimization_barrier((seconds, far_parts[-1]))
+    seconds, firsts, far_parts[-1] = lax.optimization_barrier((seconds, firsts, far_parts[-1]))
     seconds = swap_inside(seconds)
     inner = call(
         functools.partial(inner_kernel, half_count),

time: 82.9 us -> 80 us (0.965)
  waiting for transfers between devices: 30 us -> 22.1 us
  starting transfers between devices: 36.9 us -> 41.9 us
    ppermute x18, waiting for transfers between devices: 27.1 us -> 19.3 us  [swap(): return lax.ppermute(block, 'seq', [(i, i ^ distance) for i in range(count)])]
    ppermute x18, starting transfers between devices: 27.6 us -> 32.6 us  [swap(): return lax.ppermute(block, 'seq', [(i, i ^ distance) for i in range(count)])]
  transfers between devices with their start and end apart: 25 -> 25, of which waited for: 13 -> 10; matrix products, arithmetic and copies ran while one was open for 0% -> 0% of each run, Pallas kernels for 11% -> 11%
where the time goes in v3:
time: 80 us; the launch traced here: 79.8 us
  starting transfers between devices  41.9 us (52%)
  waiting for transfers between devices  22.1 us (28%)
  Pallas kernels  14.7 us (18%)
  between operations  0.8 us (1%)
    ppermute x18, starting transfers between devices, swap(): return lax.ppermute(block, 'seq', [(i, i ^ distance) for i in range(count)])  32.6 us
    ppermute x18, waiting for transfers between devices, swap(): return lax.ppermute(block, 'seq', [(i, i ^ distance) for i in range(count)])  19.3 us
    pallas_call x8, Pallas kernels, call(): pl.pallas_call(kernel, out_shape=out_shapes, in_specs=[pl.BlockSpec(memor...  14.7 us
    all_to_all x1, starting transfers between devices, exchange_inside(): lax.all_to_all(parts, 'seq', split_axis=0, concat_axis=0, tiled=True, axi...  5.39 us
    ppermute x6, starting transfers between devices, sum_over_head(): lax.ppermute(block, 'head', [(i, i ^ d) for i in range(count)])  3.84 us
    ppermute x6, waiting for transfers between devices, sum_over_head(): lax.ppermute(block, 'head', [(i, i ^ d) for i in range(count)])  2.86 us
  transfers between devices with their start and end apart: 25, of which 10 were waited for; matrix products, arithmetic and copies ran while one was open for 0% of the time, Pallas kernels for 11%

profile of v3, /device:TPU:0, one launch (start us, length us, event | category | flops | bytes accessed | tf_op | source)
XLA Modules:
  0.0 79.8 jit_solution(11004718525586157445)
XLA Ops:
  0.6 2.2 %shard_map.93 = bf16[2304,256]{1,0:T(8,128)(2,1)} custom-call(bf16[192,1024]{1,0:T(8,128)(2,1)} %query_ref.3, bf16[192,1024]{1,0:T(8,128)(2,1)} %value_ref.3, bf16[192,1024]{1,0:T(8,128)(2,1)} %grad_ref.3), custom_call_target="tpu_custom_call" | custom-call | tf_op jit(solution)/shard_map/pallas_call | solution.py:783
  2.9 5.4 %all-to-all-start = ((bf16[4,576,256]{2,1,0:T(8,128)(2,1)}), bf16[4,576,256]{2,1,0:T(8,128)(2,1)S(1)}, u32[]{:S(2)}, u32[]{:S(2)}) async-start(bf16[4,576,256]{2,1,0:T(8,128)(2,1)} %bitcast.14), calls=%async_computation | async-start | bytes 2359296 | tf_op jit(solution)/shard_map/all_to_all | solution.py:813
  13.2 2.6 %collective-permute-start.3 = (bf16[400,128]{1,0:T(8,128)(2,1)S(1)}, bf16[400,128]{1,0:T(8,128)(2,1)S(1)}, u32[]{:S(2)}, u32[]{:S(2)}) collective-permute-start(bf16[400,128]{1,0:T(8,128)(2,1)S(1)} %get-tuple-element.59), channel_id=1, source_target_pairs={{0,16},{4,20},{8,24},{12,28},{16,0},{20,4},{24,8},{28,12},{1,17},{... | collective-permute-start | bytes 307208 | tf_op jit(solution)/shard_map/ppermute | solution.py:798
  15.9 1.5 %collective-permute-start.4 = (bf16[400,128]{1,0:T(8,128)(2,1)S(1)}, bf16[400,128]{1,0:T(8,128)(2,1)S(1)}, u32[]{:S(2)}, u32[]{:S(2)}) collective-permute-start(bf16[400,128]{1,0:T(8,128)(2,1)S(1)} %get-tuple-element.60), channel_id=1, source_target_pairs={{0,20},{4,16},{8,28},{12,24},{16,4},{20,0},{24,12},{28,8},{1,21},{... | collective-permute-start | bytes 307208 | tf_op jit(solution)/shard_map/ppermute | solution.py:798
  17.4 3.5 %collective-permute-start.5 = (bf16[400,128]{1,0:T(8,128)(2,1)S(1)}, bf16[400,128]{1,0:T(8,128)(2,1)S(1)}, u32[]{:S(2)}, u32[]{:S(2)}) collective-permute-start(bf16[400,128]{1,0:T(8,128)(2,1)S(1)} %get-tuple-element.61), channel_id=1, source_target_pairs={{0,24},{4,28},{8,16},{12,20},{16,8},{20,12},{24,0},{28,4},{1,25},{... | collective-permute-start | bytes 307208 | tf_op jit(solution)/shard_map/ppermute | solution.py:798
  21.0 1.7 %collective-permute-start.7 = (bf16[208,256]{1,0:T(8,128)(2,1)S(1)}, bf16[208,256]{1,0:T(8,128)(2,1)S(1)}, u32[]{:S(2)}, u32[]{:S(2)}) collective-permute-start(bf16[208,256]{1,0:T(8,128)(2,1)S(1)} %get-tuple-element.64), channel_id=1, source_target_pairs={{0,4},{4,0},{8,12},{12,8},{16,20},{20,16},{24,28},{28,24},{1,5},{5... | collective-permute-start | bytes 319496 | tf_op jit(solution)/shard_map/ppermute | solution.py:798
  22.7 1.8 %collective-permute-done.3.refs_0_ = bf16[400,128]{1,0:T(8,128)(2,1)S(1)} collective-permute-done((bf16[400,128]{1,0:T(8,128)(2,1)S(1)}, bf16[400,128]{1,0:T(8,128)(2,1)S(1)}, u32[]{:S(2)}, u32[]{:S(2)}) %collective-permute-start.3) | collective-permute-done | bytes 102432 | tf_op jit(solution)/shard_map/ppermute | solution.py:798
  24.5 5.1 %collective-permute-start.8 = (bf16[208,256]{1,0:T(8,128)(2,1)S(1)}, bf16[208,256]{1,0:T(8,128)(2,1)S(1)}, u32[]{:S(2)}, u32[]{:S(2)}) collective-permute-start(bf16[208,256]{1,0:T(8,128)(2,1)S(1)} %get-tuple-element.65), channel_id=1, source_target_pairs={{0,8},{4,12},{8,0},{12,4},{16,24},{20,28},{24,16},{28,20},{1,9},{5... | collective-permute-start | bytes 319496 | tf_op jit(solution)/shard_map/ppermute | solution.py:798
  29.6 3.1 %collective-permute-start.9 = (bf16[208,256]{1,0:T(8,128)(2,1)S(1)}, bf16[208,256]{1,0:T(8,128)(2,1)S(1)}, u32[]{:S(2)}, u32[]{:S(2)}) collective-permute-start(bf16[208,256]{1,0:T(8,128)(2,1)S(1)} %get-tuple-element.66), channel_id=1, source_target_pairs={{0,12},{4,8},{8,4},{12,0},{16,28},{20,24},{24,20},{28,16},{1,13},{... | collective-permute-start | bytes 319496 | tf_op jit(solution)/shard_map/ppermute | solution.py:798
  33.4 3.1 %collective-permute-done.6.refs_3_ = bf16[400,128]{1,0:T(8,128)(2,1)S(1)} collective-permute-done((bf16[400,128]{1,0:T(8,128)(2,1)S(1)}, bf16[400,128]{1,0:T(8,128)(2,1)S(1)}, u32[]{:S(2)}, u32[]{:S(2)}) %collective-permute-start.6) | collective-permute-done | bytes 102432 | tf_op jit(solution)/shard_map/ppermute | solution.py:798
  37.7 2.2 %shard_map.95.refs_8_ = f32[24,128]{1,0:T(8,128)S(1)} custom-call(s32[1]{0:T(128)} %bitcast.me_ref, f32[12,128]{1,0:T(8,128)S(1)} %pad.13.pattern_ref, bf16[2304,256]{1,0:T(8,128)(2,1)S(1)} %bitcast.11, bf16[400,128]{1,0:T(8,128)(2,1)S(1)} %collective-permute-done.3.refs_0_, bf16[400,128]{1,0:T(8,128)(2,1)S(1)} %collective-permute-done.4.refs_1_, ...), custom_call_target="tpu_custom_call" | custom-call | flops 301989888 | tf_op jit(solution)/shard_map/pallas_call | solution.py:783
  39.9 2.3 %collective-permute-start.10 = (f32[24,128]{1,0:T(8,128)S(1)}, f32[24,128]{1,0:T(8,128)S(1)}, u32[]{:S(2)}, u32[]{:S(2)}) collective-permute-start(f32[24,128]{1,0:T(8,128)S(1)} %shard_map.95.refs_8_), channel_id=1, source_target_pairs={{0,16},{4,20},{8,24},{12,28},{16,0},{20,4},{24,8},{28,12},{1,17},{... | collective-permute-start | bytes 36872 | tf_op jit(solution)/shard_map/ppermute | solution.py:798
  42.1 4.3 %shard_map.96 = (bf16[768,128]{1,0:T(8,128)(2,1)S(1)}, bf16[768,128]{1,0:T(8,128)(2,1)S(1)}, bf16[768,128]{1,0:T(8,128)(2,1)S(1)}, bf16[768,128]{1,0:T(8,128)(2,...) custom-call(s32[1]{0:T(128)} %bitcast.me_ref, ...), custom_call_target="tpu_custom_call" | custom-call | flops 1358954496 | tf_op jit(solution)/shard_map/pallas_call | solution.py:783
  47.6 2.4 %collective-permute-start.16 = (bf16[768,128]{1,0:T(8,128)(2,1)S(1)}, bf16[768,128]{1,0:T(8,128)(2,1)S(1)}, u32[]{:S(2)}, u32[]{:S(2)}) collective-permute-start(bf16[768,128]{1,0:T(8,128)(2,1)S(1)} %get-tuple-element.94), channel_id=1, source_target_pairs={{0,12},{4,8},{8,4},{12,0},{16,28},{20,24},{24,20},{28,16},{1,13},{... | collective-permute-start | bytes 589832 | tf_op jit(solution)/shard_map/ppermute | solution.py:798
  50.0 2.8 %shard_map.97 = (bf16[768,128]{1,0:T(8,128)(2,1)S(1)}, bf16[768,128]{1,0:T(8,128)(2,1)S(1)}, bf16[768,128]{1,0:T(8,128)(2,1)S(1)}, bf16[768,128]{1,0:T(8,128)(2,...) custom-call(s32[1]{0:T(128)} %bitcast.me_ref, ...), custom_call_target="tpu_custom_call" | custom-call | flops 905969664 | tf_op jit(solution)/shard_map/pallas_call | solution.py:783
  52.8 1.4 %collective-permute-start.17 = (bf16[384,128]{1,0:T(8,128)(2,1)S(1)}, bf16[384,128]{1,0:T(8,128)(2,1)S(1)}, u32[]{:S(2)}, u32[]{:S(2)}) collective-permute-start(bf16[384,128]{1,0:T(8,128)(2,1)S(1)} %get-tuple-element.95), channel_id=1, source_target_pairs={{0,28},{4,24},{8,20},{12,16},{16,12},{20,8},{24,4},{28,0},{1,29},{... | collective-permute-start | bytes 294920 | tf_op jit(solution)/shard_map/ppermute | solution.py:798
  54.8 6.4 %collective-permute-done.17.refs_3_ = bf16[384,128]{1,0:T(8,128)(2,1)S(1)} collective-permute-done((bf16[384,128]{1,0:T(8,128)(2,1)S(1)}, bf16[384,128]{1,0:T(8,128)(2,1)S(1)}, u32[]{:S(2)}, u32[]{:S(2)}) %collective-permute-start.17) | collective-permute-done | bytes 98336 | tf_op jit(solution)/shard_map/ppermute | solution.py:798
  61.3 1.8 %collective-permute-start.18 = (bf16[768,128]{1,0:T(8,128)(2,1)S(1)}, bf16[768,128]{1,0:T(8,128)(2,1)S(1)}, u32[]{:S(2)}, u32[]{:S(2)}) collective-permute-start(bf16[768,128]{1,0:T(8,128)(2,1)S(1)} %get-tuple-element.102), channel_id=1, source_target_pairs={{0,4},{4,0},{8,12},{12,8},{16,20},{20,16},{24,28},{28,24},{1,5},{5... | collective-permute-start | bytes 589832 | tf_op jit(solution)/shard_map/ppermute | solution.py:798
  63.1 1.7 %collective-permute-start.20 = (bf16[768,128]{1,0:T(8,128)(2,1)S(1)}, bf16[768,128]{1,0:T(8,128)(2,1)S(1)}, u32[]{:S(2)}, u32[]{:S(2)}) collective-permute-start(bf16[768,128]{1,0:T(8,128)(2,1)S(1)} %get-tuple-element.104), channel_id=1, source_target_pairs={{0,12},{4,8},{8,4},{12,0},{16,28},{20,24},{24,20},{28,16},{1,13},{... | collective-permute-start | bytes 589832 | tf_op jit(solution)/shard_map/ppermute | solution.py:798
  64.8 1.7 %collective-permute-start.12 = (bf16[384,128]{1,0:T(8,128)(2,1)S(1)}, bf16[384,128]{1,0:T(8,128)(2,1)S(1)}, u32[]{:S(2)}, u32[]{:S(2)}) collective-permute-start(bf16[384,128]{1,0:T(8,128)(2,1)S(1)} %get-tuple-element.85), channel_id=1, source_target_pairs={{0,20},{4,16},{8,28},{12,24},{16,4},{20,0},{24,12},{28,8},{1,21},{... | collective-permute-start | bytes 294920 | tf_op jit(solution)/shard_map/ppermute | solution.py:798
  66.6 1.8 %collective-permute-start.13 = (bf16[384,128]{1,0:T(8,128)(2,1)S(1)}, bf16[384,128]{1,0:T(8,128)(2,1)S(1)}, u32[]{:S(2)}, u32[]{:S(2)}) collective-permute-start(bf16[384,128]{1,0:T(8,128)(2,1)S(1)} %get-tuple-element.86), channel_id=1, source_target_pairs={{0,24},{4,28},{8,16},{12,20},{16,8},{20,12},{24,0},{28,4},{1,25},{... | collective-permute-start | bytes 294920 | tf_op jit(solution)/shard_map/ppermute | solution.py:798
  68.4 2.9 %collective-permute-done.12.refs_1_ = bf16[384,128]{1,0:T(8,128)(2,1)S(1)} collective-permute-done((bf16[384,128]{1,0:T(8,128)(2,1)S(1)}, bf16[384,128]{1,0:T(8,128)(2,1)S(1)}, u32[]{:S(2)}, u32[]{:S(2)}) %collective-permute-start.12) | collective-permute-done | bytes 98336 | tf_op jit(solution)/shard_map/ppermute | solution.py:798
  71.4 3.2 %collective-permute-done.13.refs_2_ = bf16[384,128]{1,0:T(8,128)(2,1)S(1)} collective-permute-done((bf16[384,128]{1,0:T(8,128)(2,1)S(1)}, bf16[384,128]{1,0:T(8,128)(2,1)S(1)}, u32[]{:S(2)}, u32[]{:S(2)}) %collective-permute-start.13) | collective-permute-done | bytes 98336 | tf_op jit(solution)/shard_map/ppermute | solution.py:798
  75.0 1.6 %collective-permute-start.22 = (f32[8,128]{1,0:T(8,128)S(1)}, f32[8,128]{1,0:T(8,128)S(1)}, u32[]{:S(2)}, u32[]{:S(2)}) collective-permute-start(f32[8,128]{1,0:T(8,128)S(1)} %shard_map.99), channel_id=1, source_target_pairs={{0,2},{1,3},{2,0},{3,1},{4,6},{5,7},{6,4},{7,5},{8,10},{9,11},{10,... | collective-permute-start | bytes 12296 | tf_op jit(solution)/shard_map/ppermute | solution.py:823
  (55 shorter events, 12.4 us)
Async XLA Ops:
  2.9 34.9 %all-to-all-start = ((bf16[4,576,256]{2,1,0:T(8,128)(2,1)}), bf16[4,576,256]{2,1,0:T(8,128)(2,1)S(1)}, u32[]{:S(2)}, u32[]{:S(2)}) async-start(bf16[4,576,256]{2,1,0:T(8,128)(2,1)} %bitcast.14), calls=%async_computation | async-start | bytes 2359296 | tf_op jit(solution)/shard_map/all_to_all | solution.py:813
  8.4 3.1 %collective-permute-start.2 = (f32[8,128]{1,0:T(8,128)S(1)}, f32[8,128]{1,0:T(8,128)S(1)}, u32[]{:S(2)}, u32[]{:S(2)}) collective-permute-start(f32[8,128]{1,0:T(8,128)S(1)} %pad_bitcast_fusion.1), channel_id=1, source_target_pairs={{0,3},{1,2},{2,1},{3,0},{4,7},{5,6},{6,5},{7,4},{8,11},{9,10},{10,... | collective-permute-start | bytes 12296 | tf_op jit(solution)/shard_map/ppermute | solution.py:823
  9.2 3.6 %collective-permute-start.1 = (f32[8,128]{1,0:T(8,128)S(1)}, f32[8,128]{1,0:T(8,128)S(1)}, u32[]{:S(2)}, u32[]{:S(2)}) collective-permute-start(f32[8,128]{1,0:T(8,128)S(1)} %pad_bitcast_fusion.1), channel_id=1, source_target_pairs={{0,2},{1,3},{2,0},{3,1},{4,6},{5,7},{6,4},{7,5},{8,10},{9,11},{10,... | collective-permute-start | bytes 12296 | tf_op jit(solution)/shard_map/ppermute | solution.py:823
  10.1 2.7 %collective-permute-start = (f32[8,128]{1,0:T(8,128)S(1)}, f32[8,128]{1,0:T(8,128)S(1)}, u32[]{:S(2)}, u32[]{:S(2)}) collective-permute-start(f32[8,128]{1,0:T(8,128)S(1)} %pad_bitcast_fusion.1), channel_id=1, source_target_pairs={{0,1},{1,0},{2,3},{3,2},{4,5},{5,4},{6,7},{7,6},{8,9},{9,8},{10,11... | collective-permute-start | bytes 12296 | tf_op jit(solution)/shard_map/ppermute | solution.py:823
  13.2 11.2 %collective-permute-start.3 = (bf16[400,128]{1,0:T(8,128)(2,1)S(1)}, bf16[400,128]{1,0:T(8,128)(2,1)S(1)}, u32[]{:S(2)}, u32[]{:S(2)}) collective-permute-start(bf16[400,128]{1,0:T(8,128)(2,1)S(1)} %get-tuple-element.59), channel_id=1, source_target_pairs={{0,16},{4,20},{8,24},{12,28},{16,0},{20,4},{24,8},{28,12},{1,17},{... | collective-permute-start | bytes 307208 | tf_op jit(solution)/shard_map/ppermute | solution.py:798
  15.9 13.7 %collective-permute-start.4 = (bf16[400,128]{1,0:T(8,128)(2,1)S(1)}, bf16[400,128]{1,0:T(8,128)(2,1)S(1)}, u32[]{:S(2)}, u32[]{:S(2)}) collective-permute-start(bf16[400,128]{1,0:T(8,128)(2,1)S(1)} %get-tuple-element.60), channel_id=1, source_target_pairs={{0,20},{4,16},{8,28},{12,24},{16,4},{20,0},{24,12},{28,8},{1,21},{... | collective-permute-start | bytes 307208 | tf_op jit(solution)/shard_map/ppermute | solution.py:798
  17.4 16.0 %collective-permute-start.5 = (bf16[400,128]{1,0:T(8,128)(2,1)S(1)}, bf16[400,128]{1,0:T(8,128)(2,1)S(1)}, u32[]{:S(2)}, u32[]{:S(2)}) collective-permute-start(bf16[400,128]{1,0:T(8,128)(2,1)S(1)} %get-tuple-element.61), channel_id=1, source_target_pairs={{0,24},{4,28},{8,16},{12,20},{16,8},{20,12},{24,0},{28,4},{1,25},{... | collective-permute-start | bytes 307208 | tf_op jit(solution)/shard_map/ppermute | solution.py:798
  20.9 15.6 %collective-permute-start.6 = (bf16[400,128]{1,0:T(8,128)(2,1)S(1)}, bf16[400,128]{1,0:T(8,128)(2,1)S(1)}, u32[]{:S(2)}, u32[]{:S(2)}) collective-permute-start(bf16[400,128]{1,0:T(8,128)(2,1)S(1)} %get-tuple-element.62), channel_id=1, source_target_pairs={{0,28},{4,24},{8,20},{12,16},{16,12},{20,8},{24,4},{28,0},{1,29},{... | collective-permute-start | bytes 307208 | tf_op jit(solution)/shard_map/ppermute | solution.py:798
  21.0 15.5 %collective-permute-start.7 = (bf16[208,256]{1,0:T(8,128)(2,1)S(1)}, bf16[208,256]{1,0:T(8,128)(2,1)S(1)}, u32[]{:S(2)}, u32[]{:S(2)}) collective-permute-start(bf16[208,256]{1,0:T(8,128)(2,1)S(1)} %get-tuple-element.64), channel_id=1, source_target_pairs={{0,4},{4,0},{8,12},{12,8},{16,20},{20,16},{24,28},{28,24},{1,5},{5... | collective-permute-start | bytes 319496 | tf_op jit(solution)/shard_map/ppermute | solution.py:798
  24.5 12.0 %collective-permute-start.8 = (bf16[208,256]{1,0:T(8,128)(2,1)S(1)}, bf16[208,256]{1,0:T(8,128)(2,1)S(1)}, u32[]{:S(2)}, u32[]{:S(2)}) collective-permute-start(bf16[208,256]{1,0:T(8,128)(2,1)S(1)} %get-tuple-element.65), channel_id=1, source_target_pairs={{0,8},{4,12},{8,0},{12,4},{16,24},{20,28},{24,16},{28,20},{1,9},{5... | collective-permute-start | bytes 319496 | tf_op jit(solution)/shard_map/ppermute | solution.py:798
  29.6 8.1 %collective-permute-start.9 = (bf16[208,256]{1,0:T(8,128)(2,1)S(1)}, bf16[208,256]{1,0:T(8,128)(2,1)S(1)}, u32[]{:S(2)}, u32[]{:S(2)}) collective-permute-start(bf16[208,256]{1,0:T(8,128)(2,1)S(1)} %get-tuple-element.66), channel_id=1, source_target_pairs={{0,12},{4,8},{8,4},{12,0},{16,28},{20,24},{24,20},{28,16},{1,13},{... | collective-permute-start | bytes 319496 | tf_op jit(solution)/shard_map/ppermute | solution.py:798
  39.9 6.6 %collective-permute-start.10 = (f32[24,128]{1,0:T(8,128)S(1)}, f32[24,128]{1,0:T(8,128)S(1)}, u32[]{:S(2)}, u32[]{:S(2)}) collective-permute-start(f32[24,128]{1,0:T(8,128)S(1)} %shard_map.95.refs_8_), channel_id=1, source_target_pairs={{0,16},{4,20},{8,24},{12,28},{16,0},{20,4},{24,8},{28,12},{1,17},{... | collective-permute-start | bytes 36872 | tf_op jit(solution)/shard_map/ppermute | solution.py:798
  46.5 14.8 %collective-permute-start.14 = (bf16[768,128]{1,0:T(8,128)(2,1)S(1)}, bf16[768,128]{1,0:T(8,128)(2,1)S(1)}, u32[]{:S(2)}, u32[]{:S(2)}) collective-permute-start(bf16[768,128]{1,0:T(8,128)(2,1)S(1)} %get-tuple-element.92), channel_id=1, source_target_pairs={{0,4},{4,0},{8,12},{12,8},{16,20},{20,16},{24,28},{28,24},{1,5},{5... | collective-permute-start | bytes 589832 | tf_op jit(solution)/shard_map/ppermute | solution.py:798
  47.1 14.2 %collective-permute-start.15 = (bf16[768,128]{1,0:T(8,128)(2,1)S(1)}, bf16[768,128]{1,0:T(8,128)(2,1)S(1)}, u32[]{:S(2)}, u32[]{:S(2)}) collective-permute-start(bf16[768,128]{1,0:T(8,128)(2,1)S(1)} %get-tuple-element.93), channel_id=1, source_target_pairs={{0,8},{4,12},{8,0},{12,4},{16,24},{20,28},{24,16},{28,20},{1,9},{5... | collective-permute-start | bytes 589832 | tf_op jit(solution)/shard_map/ppermute | solution.py:798
  47.6 13.7 %collective-permute-start.16 = (bf16[768,128]{1,0:T(8,128)(2,1)S(1)}, bf16[768,128]{1,0:T(8,128)(2,1)S(1)}, u32[]{:S(2)}, u32[]{:S(2)}) collective-permute-start(bf16[768,128]{1,0:T(8,128)(2,1)S(1)} %get-tuple-element.94), channel_id=1, source_target_pairs={{0,12},{4,8},{8,4},{12,0},{16,28},{20,24},{24,20},{28,16},{1,13},{... | collective-permute-start | bytes 589832 | tf_op jit(solution)/shard_map/ppermute | solution.py:798
  52.8 8.5 %collective-permute-start.17 = (bf16[384,128]{1,0:T(8,128)(2,1)S(1)}, bf16[384,128]{1,0:T(8,128)(2,1)S(1)}, u32[]{:S(2)}, u32[]{:S(2)}) collective-permute-start(bf16[384,128]{1,0:T(8,128)(2,1)S(1)} %get-tuple-element.95), channel_id=1, source_target_pairs={{0,28},{4,24},{8,20},{12,16},{16,12},{20,8},{24,4},{28,0},{1,29},{... | collective-permute-start | bytes 294920 | tf_op jit(solution)/shard_map/ppermute | solution.py:798
  54.2 12.4 %collective-permute-start.11 = (bf16[384,128]{1,0:T(8,128)(2,1)S(1)}, bf16[384,128]{1,0:T(8,128)(2,1)S(1)}, u32[]{:S(2)}, u32[]{:S(2)}) collective-permute-start(bf16[384,128]{1,0:T(8,128)(2,1)S(1)} %get-tuple-element.84), channel_id=1, source_target_pairs={{0,16},{4,20},{8,24},{12,28},{16,0},{20,4},{24,8},{28,12},{1,17},{... | collective-permute-start | bytes 294920 | tf_op jit(solution)/shard_map/ppermute | solution.py:798
  61.3 13.2 %collective-permute-start.18 = (bf16[768,128]{1,0:T(8,128)(2,1)S(1)}, bf16[768,128]{1,0:T(8,128)(2,1)S(1)}, u32[]{:S(2)}, u32[]{:S(2)}) collective-permute-start(bf16[768,128]{1,0:T(8,128)(2,1)S(1)} %get-tuple-element.102), channel_id=1, source_target_pairs={{0,4},{4,0},{8,12},{12,8},{16,20},{20,16},{24,28},{28,24},{1,5},{5... | collective-permute-start | bytes 589832 | tf_op jit(solution)/shard_map/ppermute | solution.py:798
  63.1 11.4 %collective-permute-start.19 = (bf16[768,128]{1,0:T(8,128)(2,1)S(1)}, bf16[768,128]{1,0:T(8,128)(2,1)S(1)}, u32[]{:S(2)}, u32[]{:S(2)}) collective-permute-start(bf16[768,128]{1,0:T(8,128)(2,1)S(1)} %get-tuple-element.103), channel_id=1, source_target_pairs={{0,8},{4,12},{8,0},{12,4},{16,24},{20,28},{24,16},{28,20},{1,9},{5... | collective-permute-start | bytes 589832 | tf_op jit(solution)/shard_map/ppermute | solution.py:798
  63.1 11.4 %collective-permute-start.20 = (bf16[768,128]{1,0:T(8,128)(2,1)S(1)}, bf16[768,128]{1,0:T(8,128)(2,1)S(1)}, u32[]{:S(2)}, u32[]{:S(2)}) collective-permute-start(bf16[768,128]{1,0:T(8,128)(2,1)S(1)} %get-tuple-element.104), channel_id=1, source_target_pairs={{0,12},{4,8},{8,4},{12,0},{16,28},{20,24},{24,20},{28,16},{1,13},{... | collective-permute-start | bytes 589832 | tf_op jit(solution)/shard_map/ppermute | solution.py:798
  64.8 6.5 %collective-permute-start.12 = (bf16[384,128]{1,0:T(8,128)(2,1)S(1)}, bf16[384,128]{1,0:T(8,128)(2,1)S(1)}, u32[]{:S(2)}, u32[]{:S(2)}) collective-permute-start(bf16[384,128]{1,0:T(8,128)(2,1)S(1)} %get-tuple-element.85), channel_id=1, source_target_pairs={{0,20},{4,16},{8,28},{12,24},{16,4},{20,0},{24,12},{28,8},{1,21},{... | collective-permute-start | bytes 294920 | tf_op jit(solution)/shard_map/ppermute | solution.py:798
  66.6 7.9 %collective-permute-start.13 = (bf16[384,128]{1,0:T(8,128)(2,1)S(1)}, bf16[384,128]{1,0:T(8,128)(2,1)S(1)}, u32[]{:S(2)}, u32[]{:S(2)}) collective-permute-start(bf16[384,128]{1,0:T(8,128)(2,1)S(1)} %get-tuple-element.86), channel_id=1, source_target_pairs={{0,24},{4,28},{8,16},{12,20},{16,8},{20,12},{24,0},{28,4},{1,25},{... | collective-permute-start | bytes 294920 | tf_op jit(solution)/shard_map/ppermute | solution.py:798
  74.9 3.3 %collective-permute-start.23 = (f32[8,128]{1,0:T(8,128)S(1)}, f32[8,128]{1,0:T(8,128)S(1)}, u32[]{:S(2)}, u32[]{:S(2)}) collective-permute-start(f32[8,128]{1,0:T(8,128)S(1)} %shard_map.99), channel_id=1, source_target_pairs={{0,3},{1,2},{2,1},{3,0},{4,7},{5,6},{6,5},{7,4},{8,11},{9,10},{10,... | collective-permute-start | bytes 12296 | tf_op jit(solution)/shard_map/ppermute | solution.py:823
  75.0 3.7 %collective-permute-start.22 = (f32[8,128]{1,0:T(8,128)S(1)}, f32[8,128]{1,0:T(8,128)S(1)}, u32[]{:S(2)}, u32[]{:S(2)}) collective-permute-start(f32[8,128]{1,0:T(8,128)S(1)} %shard_map.99), channel_id=1, source_target_pairs={{0,2},{1,3},{2,0},{3,1},{4,6},{5,7},{6,4},{7,5},{8,10},{9,11},{10,... | collective-permute-start | bytes 12296 | tf_op jit(solution)/shard_map/ppermute | solution.py:823
  (7 other events, 69.5 us)

commit v4 on v3

--- a/solution.py
+++ b/solution.py
@@ -20,6 +20,7 @@
 LANES = 128
 ID_ROWS = 16
 QUERY_TILE = 256
+STATS_TILE = 384
 VMEM_BYTES = 32 << 20
 PACK_VMEM_BYTES = 60 << 20
 
@@ -429,8 +430,8 @@
     )
 
 
-def own_tiles(half_len):
-    tile = QUERY_TILE if half_len % QUERY_TILE == 0 else BLK
+def own_tiles(half_len, tile=QUERY_TILE):
+    tile = tile if half_len % tile == 0 else BLK
     return [(first, slice(first, first + tile), first + tile) for first in range(0, half_len, tile)]
 
 
@@ -474,13 +475,13 @@
 
         @pl.when(slots.is_high)
         def _():
-            for first, rows, limit in own_tiles(slots.half_len):
+            for first, rows, limit in own_tiles(slots.half_len, STATS_TILE):
                 note(first, rows, limit, first)
 
         @pl.when(jnp.logical_not(slots.is_high))
         def _():
             slots.cross(column, query_all, grad_all)
-            for first, rows, _ in own_tiles(slots.half_len):
+            for first, rows, _ in own_tiles(slots.half_len, STATS_TILE):
                 note(first, rows, slots.half_len, None)
 
 
@@ -865,8 +866,10 @@
         [me],
         [queries, values, cotangent, key_vectors, key_rms, ids],
     )
-    keys = swap_inside(sent[:half_count])
     cross = swap_across(sent[half_count:])
+    key_sent = list(sent[:half_count])
+    key_sent[1], cross[0] = lax.optimization_barrier((key_sent[1], cross[0]))
+    keys = swap_inside(key_sent)
     pattern_rows = block_pattern.transpose(1, 0, 2).reshape(block_count, -1).astype(jnp.float32)
     pattern_rows = jnp.pad(pattern_rows, ((0, 0), (0, LANES - cluster_count * block_count)))
     wide = pltpu.VMEM((half_len, 2 * HEAD_DIM), jnp.bfloat16)

time: 80 us -> 79.4 us (level)
  starting transfers between devices: 41.9 us -> 37.8 us
  waiting for transfers between devices: 22.1 us -> 25.9 us
    ppermute x18, starting transfers between devices: 32.6 us -> 28.6 us  [swap(): return lax.ppermute(block, 'seq', [(i, i ^ distance) for i in range(count)])]
    ppermute x18, waiting for transfers between devices: 19.3 us -> 23 us  [swap(): return lax.ppermute(block, 'seq', [(i, i ^ distance) for i in range(count)])]
  transfers between devices with their start and end apart: 25 -> 25, of which waited for: 10 -> 11; matrix products, arithmetic and copies ran while one was open for 0% -> 0% of each run, Pallas kernels for 11% -> 11%
where the time goes in v4:
time: 79.4 us; the launch traced here: 79.1 us
  starting transfers between devices  37.8 us (48%)
  waiting for transfers between devices  25.9 us (33%)
  Pallas kernels  14.3 us (18%)
  between operations  0.8 us (1%)
    ppermute x18, starting transfers between devices, swap(): return lax.ppermute(block, 'seq', [(i, i ^ distance) for i in range(count)])  28.6 us
    ppermute x18, waiting for transfers between devices, swap(): return lax.ppermute(block, 'seq', [(i, i ^ distance) for i in range(count)])  23 us
    pallas_call x8, Pallas kernels, call(): pl.pallas_call(kernel, out_shape=out_shapes, in_specs=[pl.BlockSpec(memor...  14.3 us
    all_to_all x1, starting transfers between devices, exchange_inside(): lax.all_to_all(parts, 'seq', split_axis=0, concat_axis=0, tiled=True, axi...  5.39 us
    ppermute x6, starting transfers between devices, sum_over_head(): lax.ppermute(block, 'head', [(i, i ^ d) for i in range(count)])  3.84 us
    ppermute x6, waiting for transfers between devices, sum_over_head(): lax.ppermute(block, 'head', [(i, i ^ d) for i in range(count)])  2.86 us
  transfers between devices with their start and end apart: 25, of which 11 were waited for; matrix products, arithmetic and copies ran while one was open for 0% of the time, Pallas kernels for 11%

profile of v4, /device:TPU:0, one launch (start us, length us, event | category | flops | bytes accessed | tf_op | source)
XLA Modules:
  0.0 79.1 jit_solution(15912082595608818139)
XLA Ops:
  0.6 2.2 %shard_map.93 = bf16[2304,256]{1,0:T(8,128)(2,1)} custom-call(bf16[192,1024]{1,0:T(8,128)(2,1)} %query_ref.3, bf16[192,1024]{1,0:T(8,128)(2,1)} %value_ref.3, bf16[192,1024]{1,0:T(8,128)(2,1)} %grad_ref.3), custom_call_target="tpu_custom_call" | custom-call | tf_op jit(solution)/shard_map/pallas_call | solution.py:784
  2.9 5.4 %all-to-all-start = ((bf16[4,576,256]{2,1,0:T(8,128)(2,1)}), bf16[4,576,256]{2,1,0:T(8,128)(2,1)S(1)}, u32[]{:S(2)}, u32[]{:S(2)}) async-start(bf16[4,576,256]{2,1,0:T(8,128)(2,1)} %bitcast.14), calls=%async_computation | async-start | bytes 2359296 | tf_op jit(solution)/shard_map/all_to_all | solution.py:814
  10.4 1.1 %collective-permute-done.2 = f32[8,128]{1,0:T(8,128)S(1)} collective-permute-done((f32[8,128]{1,0:T(8,128)S(1)}, f32[8,128]{1,0:T(8,128)S(1)}, u32[]{:S(2)}, u32[]{:S(2)}) %collective-permute-start.2) | collective-permute-done | bytes 4128 | tf_op jit(solution)/shard_map/ppermute | solution.py:824
  11.5 1.3 %collective-permute-done.1 = f32[8,128]{1,0:T(8,128)S(1)} collective-permute-done((f32[8,128]{1,0:T(8,128)S(1)}, f32[8,128]{1,0:T(8,128)S(1)}, u32[]{:S(2)}, u32[]{:S(2)}) %collective-permute-start.1) | collective-permute-done | bytes 4128 | tf_op jit(solution)/shard_map/ppermute | solution.py:824
  13.2 2.6 %collective-permute-start.3 = (bf16[400,128]{1,0:T(8,128)(2,1)S(1)}, bf16[400,128]{1,0:T(8,128)(2,1)S(1)}, u32[]{:S(2)}, u32[]{:S(2)}) collective-permute-start(bf16[400,128]{1,0:T(8,128)(2,1)S(1)} %get-tuple-element.62), channel_id=1, source_target_pairs={{0,16},{4,20},{8,24},{12,28},{16,0},{20,4},{24,8},{28,12},{1,17},{... | collective-permute-start | bytes 307208 | tf_op jit(solution)/shard_map/ppermute | solution.py:799
  15.9 1.5 %collective-permute-start.4 = (bf16[400,128]{1,0:T(8,128)(2,1)S(1)}, bf16[400,128]{1,0:T(8,128)(2,1)S(1)}, u32[]{:S(2)}, u32[]{:S(2)}) collective-permute-start(bf16[400,128]{1,0:T(8,128)(2,1)S(1)} %get-tuple-element.64), channel_id=1, source_target_pairs={{0,20},{4,16},{8,28},{12,24},{16,4},{20,0},{24,12},{28,8},{1,21},{... | collective-permute-start | bytes 307208 | tf_op jit(solution)/shard_map/ppermute | solution.py:799
  17.4 3.5 %collective-permute-start.5 = (bf16[400,128]{1,0:T(8,128)(2,1)S(1)}, bf16[400,128]{1,0:T(8,128)(2,1)S(1)}, u32[]{:S(2)}, u32[]{:S(2)}) collective-permute-start(bf16[400,128]{1,0:T(8,128)(2,1)S(1)} %get-tuple-element.65), channel_id=1, source_target_pairs={{0,24},{4,28},{8,16},{12,20},{16,8},{20,12},{24,0},{28,4},{1,25},{... | collective-permute-start | bytes 307208 | tf_op jit(solution)/shard_map/ppermute | solution.py:799
  21.0 3.5 %collective-permute-done.3.refs_0_ = bf16[400,128]{1,0:T(8,128)(2,1)S(1)} collective-permute-done((bf16[400,128]{1,0:T(8,128)(2,1)S(1)}, bf16[400,128]{1,0:T(8,128)(2,1)S(1)}, u32[]{:S(2)}, u32[]{:S(2)}) %collective-permute-start.3) | collective-permute-done | bytes 102432 | tf_op jit(solution)/shard_map/ppermute | solution.py:799
  24.5 6.0 %collective-permute-start.9 = (bf16[208,256]{1,0:T(8,128)(2,1)S(1)}, bf16[208,256]{1,0:T(8,128)(2,1)S(1)}, u32[]{:S(2)}, u32[]{:S(2)}) collective-permute-start(bf16[208,256]{1,0:T(8,128)(2,1)S(1)} %get-tuple-element.70), channel_id=1, source_target_pairs={{0,12},{4,8},{8,4},{12,0},{16,28},{20,24},{24,20},{28,16},{1,13},{... | collective-permute-start | bytes 319496 | tf_op jit(solution)/shard_map/ppermute | solution.py:799
  31.2 2.2 %collective-permute-done.5.refs_2_ = bf16[400,128]{1,0:T(8,128)(2,1)S(1)} collective-permute-done((bf16[400,128]{1,0:T(8,128)(2,1)S(1)}, bf16[400,128]{1,0:T(8,128)(2,1)S(1)}, u32[]{:S(2)}, u32[]{:S(2)}) %collective-permute-start.5) | collective-permute-done | bytes 102432 | tf_op jit(solution)/shard_map/ppermute | solution.py:799
  33.4 3.1 %collective-permute-done.6.refs_3_ = bf16[400,128]{1,0:T(8,128)(2,1)S(1)} collective-permute-done((bf16[400,128]{1,0:T(8,128)(2,1)S(1)}, bf16[400,128]{1,0:T(8,128)(2,1)S(1)}, u32[]{:S(2)}, u32[]{:S(2)}) %collective-permute-start.6) | collective-permute-done | bytes 102432 | tf_op jit(solution)/shard_map/ppermute | solution.py:799
  36.5 1.1 %collective-permute-done.9.refs_7_ = bf16[208,256]{1,0:T(8,128)(2,1)S(1)} collective-permute-done((bf16[208,256]{1,0:T(8,128)(2,1)S(1)}, bf16[208,256]{1,0:T(8,128)(2,1)S(1)}, u32[]{:S(2)}, u32[]{:S(2)}) %collective-permute-start.9) | collective-permute-done | bytes 106528 | tf_op jit(solution)/shard_map/ppermute | solution.py:799
  37.9 1.8 %shard_map.95.refs_8_ = f32[24,128]{1,0:T(8,128)S(1)} custom-call(s32[1]{0:T(128)} %bitcast.me_ref, f32[12,128]{1,0:T(8,128)S(1)} %pad.13.pattern_ref, bf16[2304,256]{1,0:T(8,128)(2,1)S(1)} %bitcast.11, bf16[400,128]{1,0:T(8,128)(2,1)S(1)} %collective-permute-done.3.refs_0_, bf16[400,128]{1,0:T(8,128)(2,1)S(1)} %collective-permute-done.4.refs_1_, ...), custom_call_target="tpu_custom_call" | custom-call | flops 301989888 | tf_op jit(solution)/shard_map/pallas_call | solution.py:784
  39.7 2.6 %collective-permute-start.10 = (f32[24,128]{1,0:T(8,128)S(1)}, f32[24,128]{1,0:T(8,128)S(1)}, u32[]{:S(2)}, u32[]{:S(2)}) collective-permute-start(f32[24,128]{1,0:T(8,128)S(1)} %shard_map.95.refs_8_), channel_id=1, source_target_pairs={{0,16},{4,20},{8,24},{12,28},{16,0},{20,4},{24,8},{28,12},{1,17},{... | collective-permute-start | bytes 36872 | tf_op jit(solution)/shard_map/ppermute | solution.py:799
  42.3 4.3 %shard_map.96 = (bf16[768,128]{1,0:T(8,128)(2,1)S(1)}, bf16[768,128]{1,0:T(8,128)(2,1)S(1)}, bf16[768,128]{1,0:T(8,128)(2,1)S(1)}, bf16[768,128]{1,0:T(8,128)(2,...) custom-call(s32[1]{0:T(128)} %bitcast.me_ref, ...), custom_call_target="tpu_custom_call" | custom-call | flops 1358954496 | tf_op jit(solution)/shard_map/pallas_call | solution.py:784
  47.9 2.3 %collective-permute-start.16 = (bf16[768,128]{1,0:T(8,128)(2,1)S(1)}, bf16[768,128]{1,0:T(8,128)(2,1)S(1)}, u32[]{:S(2)}, u32[]{:S(2)}) collective-permute-start(bf16[768,128]{1,0:T(8,128)(2,1)S(1)} %get-tuple-element.98), channel_id=1, source_target_pairs={{0,12},{4,8},{8,4},{12,0},{16,28},{20,24},{24,20},{28,16},{1,13},{... | collective-permute-start | bytes 589832 | tf_op jit(solution)/shard_map/ppermute | solution.py:799
  50.2 2.8 %shard_map.97 = (bf16[768,128]{1,0:T(8,128)(2,1)S(1)}, bf16[768,128]{1,0:T(8,128)(2,1)S(1)}, bf16[768,128]{1,0:T(8,128)(2,1)S(1)}, bf16[768,128]{1,0:T(8,128)(2,...) custom-call(s32[1]{0:T(128)} %bitcast.me_ref, ...), custom_call_target="tpu_custom_call" | custom-call | flops 905969664 | tf_op jit(solution)/shard_map/pallas_call | solution.py:784
  53.0 1.9 %collective-permute-start.17 = (bf16[384,128]{1,0:T(8,128)(2,1)S(1)}, bf16[384,128]{1,0:T(8,128)(2,1)S(1)}, u32[]{:S(2)}, u32[]{:S(2)}) collective-permute-start(bf16[384,128]{1,0:T(8,128)(2,1)S(1)} %get-tuple-element.99), channel_id=1, source_target_pairs={{0,28},{4,24},{8,20},{12,16},{16,12},{20,8},{24,4},{28,0},{1,29},{... | collective-permute-start | bytes 294920 | tf_op jit(solution)/shard_map/ppermute | solution.py:799
  55.2 6.6 %collective-permute-done.17.refs_3_ = bf16[384,128]{1,0:T(8,128)(2,1)S(1)} collective-permute-done((bf16[384,128]{1,0:T(8,128)(2,1)S(1)}, bf16[384,128]{1,0:T(8,128)(2,1)S(1)}, u32[]{:S(2)}, u32[]{:S(2)}) %collective-permute-start.17) | collective-permute-done | bytes 98336 | tf_op jit(solution)/shard_map/ppermute | solution.py:799
  62.0 3.4 %collective-permute-start.20 = (bf16[768,128]{1,0:T(8,128)(2,1)S(1)}, bf16[768,128]{1,0:T(8,128)(2,1)S(1)}, u32[]{:S(2)}, u32[]{:S(2)}) collective-permute-start(bf16[768,128]{1,0:T(8,128)(2,1)S(1)} %get-tuple-element.108), channel_id=1, source_target_pairs={{0,12},{4,8},{8,4},{12,0},{16,28},{20,24},{24,20},{28,16},{1,13},{... | collective-permute-start | bytes 589832 | tf_op jit(solution)/shard_map/ppermute | solution.py:799
  65.4 2.4 %collective-permute-start.13 = (bf16[384,128]{1,0:T(8,128)(2,1)S(1)}, bf16[384,128]{1,0:T(8,128)(2,1)S(1)}, u32[]{:S(2)}, u32[]{:S(2)}) collective-permute-start(bf16[384,128]{1,0:T(8,128)(2,1)S(1)} %get-tuple-element.90), channel_id=1, source_target_pairs={{0,24},{4,28},{8,16},{12,20},{16,8},{20,12},{24,0},{28,4},{1,25},{... | collective-permute-start | bytes 294920 | tf_op jit(solution)/shard_map/ppermute | solution.py:799
  67.7 4.3 %collective-permute-done.12.refs_1_ = bf16[384,128]{1,0:T(8,128)(2,1)S(1)} collective-permute-done((bf16[384,128]{1,0:T(8,128)(2,1)S(1)}, bf16[384,128]{1,0:T(8,128)(2,1)S(1)}, u32[]{:S(2)}, u32[]{:S(2)}) %collective-permute-start.12) | collective-permute-done | bytes 98336 | tf_op jit(solution)/shard_map/ppermute | solution.py:799
  72.0 1.8 %collective-permute-done.13.refs_2_ = bf16[384,128]{1,0:T(8,128)(2,1)S(1)} collective-permute-done((bf16[384,128]{1,0:T(8,128)(2,1)S(1)}, bf16[384,128]{1,0:T(8,128)(2,1)S(1)}, u32[]{:S(2)}, u32[]{:S(2)}) %collective-permute-start.13) | collective-permute-done | bytes 98336 | tf_op jit(solution)/shard_map/ppermute | solution.py:799
  76.2 1.4 %shard_map.98 = (bf16[192,1024]{1,0:T(8,128)(2,1)}, bf16[192,1024]{1,0:T(8,128)(2,1)}, bf16[192,1024]{1,0:T(8,128)(2,1)}) custom-call(s32[1]{0:T(128)} %bitcast.me_ref, bf16[384,128]{1,0:T(8,128)(2,1)S(1)} %collective-permute-done.11.refs_0_, bf16[384,128]{1,0:T(8,128)(2,1)S(1)} %collective-permute-done.12.refs_1_, ...), custom_call_target="tpu_custom_call" | custom-call | tf_op jit(solution)/shard_map/pallas_call | solution.py:784
  (55 shorter events, 9.3 us)
Async XLA Ops:
  2.9 35.0 %all-to-all-start = ((bf16[4,576,256]{2,1,0:T(8,128)(2,1)}), bf16[4,576,256]{2,1,0:T(8,128)(2,1)S(1)}, u32[]{:S(2)}, u32[]{:S(2)}) async-start(bf16[4,576,256]{2,1,0:T(8,128)(2,1)} %bitcast.14), calls=%async_computation | async-start | bytes 2359296 | tf_op jit(solution)/shard_map/all_to_all | solution.py:814
  8.4 3.1 %collective-permute-start.2 = (f32[8,128]{1,0:T(8,128)S(1)}, f32[8,128]{1,0:T(8,128)S(1)}, u32[]{:S(2)}, u32[]{:S(2)}) collective-permute-start(f32[8,128]{1,0:T(8,128)S(1)} %pad_bitcast_fusion.1), channel_id=1, source_target_pairs={{0,3},{1,2},{2,1},{3,0},{4,7},{5,6},{6,5},{7,4},{8,11},{9,10},{10,... | collective-permute-start | bytes 12296 | tf_op jit(solution)/shard_map/ppermute | solution.py:824
  9.2 3.6 %collective-permute-start.1 = (f32[8,128]{1,0:T(8,128)S(1)}, f32[8,128]{1,0:T(8,128)S(1)}, u32[]{:S(2)}, u32[]{:S(2)}) collective-permute-start(f32[8,128]{1,0:T(8,128)S(1)} %pad_bitcast_fusion.1), channel_id=1, source_target_pairs={{0,2},{1,3},{2,0},{3,1},{4,6},{5,7},{6,4},{7,5},{8,10},{9,11},{10,... | collective-permute-start | bytes 12296 | tf_op jit(solution)/shard_map/ppermute | solution.py:824
  10.1 2.7 %collective-permute-start = (f32[8,128]{1,0:T(8,128)S(1)}, f32[8,128]{1,0:T(8,128)S(1)}, u32[]{:S(2)}, u32[]{:S(2)}) collective-permute-start(f32[8,128]{1,0:T(8,128)S(1)} %pad_bitcast_fusion.1), channel_id=1, source_target_pairs={{0,1},{1,0},{2,3},{3,2},{4,5},{5,4},{6,7},{7,6},{8,9},{9,8},{10,11... | collective-permute-start | bytes 12296 | tf_op jit(solution)/shard_map/ppermute | solution.py:824
  13.2 11.2 %collective-permute-start.3 = (bf16[400,128]{1,0:T(8,128)(2,1)S(1)}, bf16[400,128]{1,0:T(8,128)(2,1)S(1)}, u32[]{:S(2)}, u32[]{:S(2)}) collective-permute-start(bf16[400,128]{1,0:T(8,128)(2,1)S(1)} %get-tuple-element.62), channel_id=1, source_target_pairs={{0,16},{4,20},{8,24},{12,28},{16,0},{20,4},{24,8},{28,12},{1,17},{... | collective-permute-start | bytes 307208 | tf_op jit(solution)/shard_map/ppermute | solution.py:799
  15.9 14.6 %collective-permute-start.4 = (bf16[400,128]{1,0:T(8,128)(2,1)S(1)}, bf16[400,128]{1,0:T(8,128)(2,1)S(1)}, u32[]{:S(2)}, u32[]{:S(2)}) collective-permute-start(bf16[400,128]{1,0:T(8,128)(2,1)S(1)} %get-tuple-element.64), channel_id=1, source_target_pairs={{0,20},{4,16},{8,28},{12,24},{16,4},{20,0},{24,12},{28,8},{1,21},{... | collective-permute-start | bytes 307208 | tf_op jit(solution)/shard_map/ppermute | solution.py:799
  17.4 16.0 %collective-permute-start.5 = (bf16[400,128]{1,0:T(8,128)(2,1)S(1)}, bf16[400,128]{1,0:T(8,128)(2,1)S(1)}, u32[]{:S(2)}, u32[]{:S(2)}) collective-permute-start(bf16[400,128]{1,0:T(8,128)(2,1)S(1)} %get-tuple-element.65), channel_id=1, source_target_pairs={{0,24},{4,28},{8,16},{12,20},{16,8},{20,12},{24,0},{28,4},{1,25},{... | collective-permute-start | bytes 307208 | tf_op jit(solution)/shard_map/ppermute | solution.py:799
  20.9 15.6 %collective-permute-start.6 = (bf16[400,128]{1,0:T(8,128)(2,1)S(1)}, bf16[400,128]{1,0:T(8,128)(2,1)S(1)}, u32[]{:S(2)}, u32[]{:S(2)}) collective-permute-start(bf16[400,128]{1,0:T(8,128)(2,1)S(1)} %get-tuple-element.66), channel_id=1, source_target_pairs={{0,28},{4,24},{8,20},{12,16},{16,12},{20,8},{24,4},{28,0},{1,29},{... | collective-permute-start | bytes 307208 | tf_op jit(solution)/shard_map/ppermute | solution.py:799
  21.0 15.5 %collective-permute-start.8 = (bf16[208,256]{1,0:T(8,128)(2,1)S(1)}, bf16[208,256]{1,0:T(8,128)(2,1)S(1)}, u32[]{:S(2)}, u32[]{:S(2)}) collective-permute-start(bf16[208,256]{1,0:T(8,128)(2,1)S(1)} %get-tuple-element.69), channel_id=1, source_target_pairs={{0,8},{4,12},{8,0},{12,4},{16,24},{20,28},{24,16},{28,20},{1,9},{5... | collective-permute-start | bytes 319496 | tf_op jit(solution)/shard_map/ppermute | solution.py:799
  24.5 13.1 %collective-permute-start.9 = (bf16[208,256]{1,0:T(8,128)(2,1)S(1)}, bf16[208,256]{1,0:T(8,128)(2,1)S(1)}, u32[]{:S(2)}, u32[]{:S(2)}) collective-permute-start(bf16[208,256]{1,0:T(8,128)(2,1)S(1)} %get-tuple-element.70), channel_id=1, source_target_pairs={{0,12},{4,8},{8,4},{12,0},{16,28},{20,24},{24,20},{28,16},{1,13},{... | collective-permute-start | bytes 319496 | tf_op jit(solution)/shard_map/ppermute | solution.py:799
  30.5 7.4 %collective-permute-start.7 = (bf16[208,256]{1,0:T(8,128)(2,1)S(1)}, bf16[208,256]{1,0:T(8,128)(2,1)S(1)}, u32[]{:S(2)}, u32[]{:S(2)}) collective-permute-start(bf16[208,256]{1,0:T(8,128)(2,1)S(1)} %get-tuple-element.68), channel_id=1, source_target_pairs={{0,4},{4,0},{8,12},{12,8},{16,20},{20,16},{24,28},{28,24},{1,5},{5... | collective-permute-start | bytes 319496 | tf_op jit(solution)/shard_map/ppermute | solution.py:799
  39.7 6.9 %collective-permute-start.10 = (f32[24,128]{1,0:T(8,128)S(1)}, f32[24,128]{1,0:T(8,128)S(1)}, u32[]{:S(2)}, u32[]{:S(2)}) collective-permute-start(f32[24,128]{1,0:T(8,128)S(1)} %shard_map.95.refs_8_), channel_id=1, source_target_pairs={{0,16},{4,20},{8,24},{12,28},{16,0},{20,4},{24,8},{28,12},{1,17},{... | collective-permute-start | bytes 36872 | tf_op jit(solution)/shard_map/ppermute | solution.py:799
  46.7 15.1 %collective-permute-start.14 = (bf16[768,128]{1,0:T(8,128)(2,1)S(1)}, bf16[768,128]{1,0:T(8,128)(2,1)S(1)}, u32[]{:S(2)}, u32[]{:S(2)}) collective-permute-start(bf16[768,128]{1,0:T(8,128)(2,1)S(1)} %get-tuple-element.96), channel_id=1, source_target_pairs={{0,4},{4,0},{8,12},{12,8},{16,20},{20,16},{24,28},{28,24},{1,5},{5... | collective-permute-start | bytes 589832 | tf_op jit(solution)/shard_map/ppermute | solution.py:799
  47.1 14.7 %collective-permute-start.15 = (bf16[768,128]{1,0:T(8,128)(2,1)S(1)}, bf16[768,128]{1,0:T(8,128)(2,1)S(1)}, u32[]{:S(2)}, u32[]{:S(2)}) collective-permute-start(bf16[768,128]{1,0:T(8,128)(2,1)S(1)} %get-tuple-element.97), channel_id=1, source_target_pairs={{0,8},{4,12},{8,0},{12,4},{16,24},{20,28},{24,16},{28,20},{1,9},{5... | collective-permute-start | bytes 589832 | tf_op jit(solution)/shard_map/ppermute | solution.py:799
  47.9 13.9 %collective-permute-start.16 = (bf16[768,128]{1,0:T(8,128)(2,1)S(1)}, bf16[768,128]{1,0:T(8,128)(2,1)S(1)}, u32[]{:S(2)}, u32[]{:S(2)}) collective-permute-start(bf16[768,128]{1,0:T(8,128)(2,1)S(1)} %get-tuple-element.98), channel_id=1, source_target_pairs={{0,12},{4,8},{8,4},{12,0},{16,28},{20,24},{24,20},{28,16},{1,13},{... | collective-permute-start | bytes 589832 | tf_op jit(solution)/shard_map/ppermute | solution.py:799
  53.0 8.8 %collective-permute-start.17 = (bf16[384,128]{1,0:T(8,128)(2,1)S(1)}, bf16[384,128]{1,0:T(8,128)(2,1)S(1)}, u32[]{:S(2)}, u32[]{:S(2)}) collective-permute-start(bf16[384,128]{1,0:T(8,128)(2,1)S(1)} %get-tuple-element.99), channel_id=1, source_target_pairs={{0,28},{4,24},{8,20},{12,16},{16,12},{20,8},{24,4},{28,0},{1,29},{... | collective-permute-start | bytes 294920 | tf_op jit(solution)/shard_map/ppermute | solution.py:799
  54.9 10.5 %collective-permute-start.11 = (bf16[384,128]{1,0:T(8,128)(2,1)S(1)}, bf16[384,128]{1,0:T(8,128)(2,1)S(1)}, u32[]{:S(2)}, u32[]{:S(2)}) collective-permute-start(bf16[384,128]{1,0:T(8,128)(2,1)S(1)} %get-tuple-element.88), channel_id=1, source_target_pairs={{0,16},{4,20},{8,24},{12,28},{16,0},{20,4},{24,8},{28,12},{1,17},{... | collective-permute-start | bytes 294920 | tf_op jit(solution)/shard_map/ppermute | solution.py:799
  61.8 12.1 %collective-permute-start.18 = (bf16[768,128]{1,0:T(8,128)(2,1)S(1)}, bf16[768,128]{1,0:T(8,128)(2,1)S(1)}, u32[]{:S(2)}, u32[]{:S(2)}) collective-permute-start(bf16[768,128]{1,0:T(8,128)(2,1)S(1)} %get-tuple-element.106), channel_id=1, source_target_pairs={{0,4},{4,0},{8,12},{12,8},{16,20},{20,16},{24,28},{28,24},{1,5},{5... | collective-permute-start | bytes 589832 | tf_op jit(solution)/shard_map/ppermute | solution.py:799
  62.0 11.9 %collective-permute-start.19 = (bf16[768,128]{1,0:T(8,128)(2,1)S(1)}, bf16[768,128]{1,0:T(8,128)(2,1)S(1)}, u32[]{:S(2)}, u32[]{:S(2)}) collective-permute-start(bf16[768,128]{1,0:T(8,128)(2,1)S(1)} %get-tuple-element.107), channel_id=1, source_target_pairs={{0,8},{4,12},{8,0},{12,4},{16,24},{20,28},{24,16},{28,20},{1,9},{5... | collective-permute-start | bytes 589832 | tf_op jit(solution)/shard_map/ppermute | solution.py:799
  62.0 11.9 %collective-permute-start.20 = (bf16[768,128]{1,0:T(8,128)(2,1)S(1)}, bf16[768,128]{1,0:T(8,128)(2,1)S(1)}, u32[]{:S(2)}, u32[]{:S(2)}) collective-permute-start(bf16[768,128]{1,0:T(8,128)(2,1)S(1)} %get-tuple-element.108), channel_id=1, source_target_pairs={{0,12},{4,8},{8,4},{12,0},{16,28},{20,24},{24,20},{28,16},{1,13},{... | collective-permute-start | bytes 589832 | tf_op jit(solution)/shard_map/ppermute | solution.py:799
  65.4 6.7 %collective-permute-start.12 = (bf16[384,128]{1,0:T(8,128)(2,1)S(1)}, bf16[384,128]{1,0:T(8,128)(2,1)S(1)}, u32[]{:S(2)}, u32[]{:S(2)}) collective-permute-start(bf16[384,128]{1,0:T(8,128)(2,1)S(1)} %get-tuple-element.89), channel_id=1, source_target_pairs={{0,20},{4,16},{8,28},{12,24},{16,4},{20,0},{24,12},{28,8},{1,21},{... | collective-permute-start | bytes 294920 | tf_op jit(solution)/shard_map/ppermute | solution.py:799
  65.4 8.5 %collective-permute-start.13 = (bf16[384,128]{1,0:T(8,128)(2,1)S(1)}, bf16[384,128]{1,0:T(8,128)(2,1)S(1)}, u32[]{:S(2)}, u32[]{:S(2)}) collective-permute-start(bf16[384,128]{1,0:T(8,128)(2,1)S(1)} %get-tuple-element.90), channel_id=1, source_target_pairs={{0,24},{4,28},{8,16},{12,20},{16,8},{20,12},{24,0},{28,4},{1,25},{... | collective-permute-start | bytes 294920 | tf_op jit(solution)/shard_map/ppermute | solution.py:799
  74.3 3.3 %collective-permute-start.23 = (f32[8,128]{1,0:T(8,128)S(1)}, f32[8,128]{1,0:T(8,128)S(1)}, u32[]{:S(2)}, u32[]{:S(2)}) collective-permute-start(f32[8,128]{1,0:T(8,128)S(1)} %shard_map.99), channel_id=1, source_target_pairs={{0,3},{1,2},{2,1},{3,0},{4,7},{5,6},{6,5},{7,4},{8,11},{9,10},{10,... | collective-permute-start | bytes 12296 | tf_op jit(solution)/shard_map/ppermute | solution.py:824
  74.3 3.7 %collective-permute-start.22 = (f32[8,128]{1,0:T(8,128)S(1)}, f32[8,128]{1,0:T(8,128)S(1)}, u32[]{:S(2)}, u32[]{:S(2)}) collective-permute-start(f32[8,128]{1,0:T(8,128)S(1)} %shard_map.99), channel_id=1, source_target_pairs={{0,2},{1,3},{2,0},{3,1},{4,6},{5,7},{6,4},{7,5},{8,10},{9,11},{10,... | collective-permute-start | bytes 12296 | tf_op jit(solution)/shard_map/ppermute | solution.py:824
  (7 other events, 68.3 us)

commit v5 on v4

--- a/solution.py
+++ b/solution.py
@@ -442,7 +442,7 @@
 
 def stats_kernel(shape, stat_rows, me_ref, pattern_ref, packed_ref, *refs):
     half_count = shape[1]
-    cross_refs, key_refs = refs[:half_count], refs[half_count : 2 * half_count]
+    cross_refs, key_refs = refs[:half_count], refs[half_count : 2 * half_count][::-1]
     out_ref, query_all, key_all, value_all, grad_all, ids, other_ids = refs[2 * half_count :]
     slots = Slots(shape, me_ref, pattern_ref, packed_ref, key_refs, cross_refs)
     single = packed_ref.shape[1] // 2
@@ -498,7 +498,7 @@
 
 def first_kernel(shape, me_ref, pattern_ref, packed_ref, *refs):
     half_count = shape[1]
-    cross_refs, key_refs = refs[:half_count], refs[half_count : 2 * half_count]
+    cross_refs, key_refs = refs[:half_count], refs[half_count : 2 * half_count][::-1]
     refs = refs[2 * half_count + 1 :]
     result_refs, cross_out_refs = refs[:half_count], refs[half_count : 2 * half_count]
     second_ref, sums_ref = refs[2 * half_count : 2 * half_count + 2]
@@ -593,7 +593,7 @@
 
 def second_head_kernel(shape, stat_rows, me_ref, pattern_ref, packed_ref, *refs):
     half_count = shape[1]
-    cross_refs, key_refs = refs[:half_count], refs[half_count : 2 * half_count]
+    cross_refs, key_refs = refs[:half_count], refs[half_count : 2 * half_count][::-1]
     own_stats_ref, far_stats_ref, early_ref, sums_ref = refs[2 * half_count : 2 * half_count + 4]
     refs = refs[2 * half_count + 4 :]
     first_cross_refs, result_refs, cross_out_refs = [
@@ -878,7 +878,7 @@
     turned = pltpu.VMEM((HEAD_DIM, half_len), jnp.bfloat16)
     ids_column = pltpu.VMEM((half_len, 1), jnp.float32)
     block_flops = 12 * half_len * half_len * single
-    inputs = [pattern_rows, packed] + cross + keys
+    inputs = [pattern_rows, packed] + cross + keys[::-1]
     stats = call(
         functools.partial(stats_kernel, shape, stat_rows),
         jax.ShapeDtypeStruct((3 * stat_rows * (single // HEAD_DIM), LANES), jnp.float32),
@@ -918,7 +918,8 @@
     far_sent, seconds = list(results[half_count:]), list(results[:half_count])
     near = half_count // 2
     far_parts = swap_across(far_sent)
-    seconds, firsts, far_parts[-1] = lax.optimization_barrier((seconds, firsts, far_parts[-1]))
+    seconds[2:], firsts, far_parts[-1] = lax.optimization_barrier((seconds[2:], firsts, far_parts[-1]))
+    seconds[1], far_parts[0] = lax.optimization_barrier((seconds[1], far_parts[0]))
     seconds = swap_inside(seconds)
     inner = call(
         functools.partial(inner_kernel, half_count),
@@ -949,6 +950,8 @@
     fits = (
         count % 2 == 0
         and count & (count - 1) == 0
+        and count >= 4
+        and tokens <= ID_ROWS * LANES
         and features % (count * HEAD_DIM) == 0
         and tokens % ID_ROWS == 0
         and tokens * count % (2 * BLK) == 0

time: 79.4 us -> 79.1 us (level)
  waiting for transfers between devices: 25.9 us -> 21.9 us
  starting transfers between devices: 37.8 us -> 41.5 us
    ppermute x18, waiting for transfers between devices: 23 us -> 19 us  [swap(): return lax.ppermute(block, 'seq', [(i, i ^ distance) for i in range(count)])]
    ppermute x18, starting transfers between devices: 28.6 us -> 32.3 us  [swap(): return lax.ppermute(block, 'seq', [(i, i ^ distance) for i in range(count)])]
where the time goes in v5:
time: 79.1 us; the launch traced here: 78.9 us
  starting transfers between devices  41.5 us (52%)
  waiting for transfers between devices  21.9 us (28%)
  Pallas kernels  14.3 us (18%)
  between operations  0.8 us (1%)
    ppermute x18, starting transfers between devices, swap(): return lax.ppermute(block, 'seq', [(i, i ^ distance) for i in range(count)])  32.3 us
    ppermute x18, waiting for transfers between devices, swap(): return lax.ppermute(block, 'seq', [(i, i ^ distance) for i in range(count)])  19 us
    pallas_call x8, Pallas kernels, call(): pl.pallas_call(kernel, out_shape=out_shapes, in_specs=[pl.BlockSpec(memor...  14.3 us
    all_to_all x1, starting transfers between devices, exchange_inside(): lax.all_to_all(parts, 'seq', split_axis=0, concat_axis=0, tiled=True, axi...  5.39 us
    ppermute x6, starting transfers between devices, sum_over_head(): lax.ppermute(block, 'head', [(i, i ^ d) for i in range(count)])  3.84 us
    ppermute x6, waiting for transfers between devices, sum_over_head(): lax.ppermute(block, 'head', [(i, i ^ d) for i in range(count)])  2.86 us
  transfers between devices with their start and end apart: 25, of which 11 were waited for; matrix products, arithmetic and copies ran while one was open for 0% of the time, Pallas kernels for 11%

profile of v5, /device:TPU:0, one launch (start us, length us, event | category | flops | bytes accessed | tf_op | source)
XLA Modules:
  0.0 78.9 jit_solution(10266572043087893150)
XLA Ops:
  0.6 2.2 %shard_map.93 = bf16[2304,256]{1,0:T(8,128)(2,1)} custom-call(bf16[192,1024]{1,0:T(8,128)(2,1)} %query_ref.3, bf16[192,1024]{1,0:T(8,128)(2,1)} %value_ref.3, bf16[192,1024]{1,0:T(8,128)(2,1)} %grad_ref.3), custom_call_target="tpu_custom_call" | custom-call | tf_op jit(solution)/shard_map/pallas_call | solution.py:784
  2.9 5.4 %all-to-all-start = ((bf16[4,576,256]{2,1,0:T(8,128)(2,1)}), bf16[4,576,256]{2,1,0:T(8,128)(2,1)S(1)}, u32[]{:S(2)}, u32[]{:S(2)}) async-start(bf16[4,576,256]{2,1,0:T(8,128)(2,1)} %bitcast.14), calls=%async_computation | async-start | bytes 2359296 | tf_op jit(solution)/shard_map/all_to_all | solution.py:814
  13.2 2.6 %collective-permute-start.3 = (bf16[400,128]{1,0:T(8,128)(2,1)S(1)}, bf16[400,128]{1,0:T(8,128)(2,1)S(1)}, u32[]{:S(2)}, u32[]{:S(2)}) collective-permute-start(bf16[400,128]{1,0:T(8,128)(2,1)S(1)} %get-tuple-element.62), channel_id=1, source_target_pairs={{0,16},{4,20},{8,24},{12,28},{16,0},{20,4},{24,8},{28,12},{1,17},{... | collective-permute-start | bytes 307208 | tf_op jit(solution)/shard_map/ppermute | solution.py:799
  15.9 1.5 %collective-permute-start.4 = (bf16[400,128]{1,0:T(8,128)(2,1)S(1)}, bf16[400,128]{1,0:T(8,128)(2,1)S(1)}, u32[]{:S(2)}, u32[]{:S(2)}) collective-permute-start(bf16[400,128]{1,0:T(8,128)(2,1)S(1)} %get-tuple-element.64), channel_id=1, source_target_pairs={{0,20},{4,16},{8,28},{12,24},{16,4},{20,0},{24,12},{28,8},{1,21},{... | collective-permute-start | bytes 307208 | tf_op jit(solution)/shard_map/ppermute | solution.py:799
  17.4 3.5 %collective-permute-start.5 = (bf16[400,128]{1,0:T(8,128)(2,1)S(1)}, bf16[400,128]{1,0:T(8,128)(2,1)S(1)}, u32[]{:S(2)}, u32[]{:S(2)}) collective-permute-start(bf16[400,128]{1,0:T(8,128)(2,1)S(1)} %get-tuple-element.65), channel_id=1, source_target_pairs={{0,24},{4,28},{8,16},{12,20},{16,8},{20,12},{24,0},{28,4},{1,25},{... | collective-permute-start | bytes 307208 | tf_op jit(solution)/shard_map/ppermute | solution.py:799
  21.8 2.7 %collective-permute-done.3.refs_0_ = bf16[400,128]{1,0:T(8,128)(2,1)S(1)} collective-permute-done((bf16[400,128]{1,0:T(8,128)(2,1)S(1)}, bf16[400,128]{1,0:T(8,128)(2,1)S(1)}, u32[]{:S(2)}, u32[]{:S(2)}) %collective-permute-start.3) | collective-permute-done | bytes 102432 | tf_op jit(solution)/shard_map/ppermute | solution.py:799
  24.5 5.1 %collective-permute-start.8 = (bf16[208,256]{1,0:T(8,128)(2,1)S(1)}, bf16[208,256]{1,0:T(8,128)(2,1)S(1)}, u32[]{:S(2)}, u32[]{:S(2)}) collective-permute-start(bf16[208,256]{1,0:T(8,128)(2,1)S(1)} %get-tuple-element.68), channel_id=1, source_target_pairs={{0,8},{4,12},{8,0},{12,4},{16,24},{20,28},{24,16},{28,20},{1,9},{5... | collective-permute-start | bytes 319496 | tf_op jit(solution)/shard_map/ppermute | solution.py:799
  29.6 1.5 %collective-permute-start.9 = (bf16[208,256]{1,0:T(8,128)(2,1)S(1)}, bf16[208,256]{1,0:T(8,128)(2,1)S(1)}, u32[]{:S(2)}, u32[]{:S(2)}) collective-permute-start(bf16[208,256]{1,0:T(8,128)(2,1)S(1)} %get-tuple-element.69), channel_id=1, source_target_pairs={{0,4},{4,0},{8,12},{12,8},{16,20},{20,16},{24,28},{28,24},{1,5},{5... | collective-permute-start | bytes 319496 | tf_op jit(solution)/shard_map/ppermute | solution.py:799
  31.2 2.2 %collective-permute-done.5.refs_2_ = bf16[400,128]{1,0:T(8,128)(2,1)S(1)} collective-permute-done((bf16[400,128]{1,0:T(8,128)(2,1)S(1)}, bf16[400,128]{1,0:T(8,128)(2,1)S(1)}, u32[]{:S(2)}, u32[]{:S(2)}) %collective-permute-start.5) | collective-permute-done | bytes 102432 | tf_op jit(solution)/shard_map/ppermute | solution.py:799
  33.4 3.1 %collective-permute-done.6.refs_3_ = bf16[400,128]{1,0:T(8,128)(2,1)S(1)} collective-permute-done((bf16[400,128]{1,0:T(8,128)(2,1)S(1)}, bf16[400,128]{1,0:T(8,128)(2,1)S(1)}, u32[]{:S(2)}, u32[]{:S(2)}) %collective-permute-start.6) | collective-permute-done | bytes 102432 | tf_op jit(solution)/shard_map/ppermute | solution.py:799
  36.7 1.8 %shard_map.95.refs_8_ = f32[24,128]{1,0:T(8,128)S(1)} custom-call(s32[1]{0:T(128)} %bitcast.me_ref, f32[12,128]{1,0:T(8,128)S(1)} %pad.13.pattern_ref, bf16[2304,256]{1,0:T(8,128)(2,1)S(1)} %bitcast.11, bf16[400,128]{1,0:T(8,128)(2,1)S(1)} %collective-permute-done.3.refs_0_, bf16[400,128]{1,0:T(8,128)(2,1)S(1)} %collective-permute-done.4.refs_1_, ...), custom_call_target="tpu_custom_call" | custom-call | flops 301989888 | tf_op jit(solution)/shard_map/pallas_call | solution.py:784
  38.5 3.3 %collective-permute-start.10 = (f32[24,128]{1,0:T(8,128)S(1)}, f32[24,128]{1,0:T(8,128)S(1)}, u32[]{:S(2)}, u32[]{:S(2)}) collective-permute-start(f32[24,128]{1,0:T(8,128)S(1)} %shard_map.95.refs_8_), channel_id=1, source_target_pairs={{0,16},{4,20},{8,24},{12,28},{16,0},{20,4},{24,8},{28,12},{1,17},{... | collective-permute-start | bytes 36872 | tf_op jit(solution)/shard_map/ppermute | solution.py:799
  41.8 4.3 %shard_map.96 = (bf16[768,128]{1,0:T(8,128)(2,1)S(1)}, bf16[768,128]{1,0:T(8,128)(2,1)S(1)}, bf16[768,128]{1,0:T(8,128)(2,1)S(1)}, bf16[768,128]{1,0:T(8,128)(2,...) custom-call(s32[1]{0:T(128)} %bitcast.me_ref, ...), custom_call_target="tpu_custom_call" | custom-call | flops 1358954496 | tf_op jit(solution)/shard_map/pallas_call | solution.py:784
  47.2 2.5 %collective-permute-start.16 = (bf16[768,128]{1,0:T(8,128)(2,1)S(1)}, bf16[768,128]{1,0:T(8,128)(2,1)S(1)}, u32[]{:S(2)}, u32[]{:S(2)}) collective-permute-start(bf16[768,128]{1,0:T(8,128)(2,1)S(1)} %get-tuple-element.98), channel_id=1, source_target_pairs={{0,12},{4,8},{8,4},{12,0},{16,28},{20,24},{24,20},{28,16},{1,13},{... | collective-permute-start | bytes 589832 | tf_op jit(solution)/shard_map/ppermute | solution.py:799
  49.7 2.8 %shard_map.97 = (bf16[768,128]{1,0:T(8,128)(2,1)S(1)}, bf16[768,128]{1,0:T(8,128)(2,1)S(1)}, bf16[768,128]{1,0:T(8,128)(2,1)S(1)}, bf16[768,128]{1,0:T(8,128)(2,...) custom-call(s32[1]{0:T(128)} %bitcast.me_ref, ...), custom_call_target="tpu_custom_call" | custom-call | flops 905969664 | tf_op jit(solution)/shard_map/pallas_call | solution.py:784
  52.8 2.6 %collective-permute-start.17 = (bf16[384,128]{1,0:T(8,128)(2,1)S(1)}, bf16[384,128]{1,0:T(8,128)(2,1)S(1)}, u32[]{:S(2)}, u32[]{:S(2)}) collective-permute-start(bf16[384,128]{1,0:T(8,128)(2,1)S(1)} %get-tuple-element.99), channel_id=1, source_target_pairs={{0,28},{4,24},{8,20},{12,16},{16,12},{20,8},{24,4},{28,0},{1,29},{... | collective-permute-start | bytes 294920 | tf_op jit(solution)/shard_map/ppermute | solution.py:799
  55.4 3.1 %collective-permute-done.11.refs_0_ = bf16[384,128]{1,0:T(8,128)(2,1)S(1)} collective-permute-done((bf16[384,128]{1,0:T(8,128)(2,1)S(1)}, bf16[384,128]{1,0:T(8,128)(2,1)S(1)}, u32[]{:S(2)}, u32[]{:S(2)}) %collective-permute-start.11) | collective-permute-done | bytes 98336 | tf_op jit(solution)/shard_map/ppermute | solution.py:799
  59.4 2.0 %collective-permute-done.17.refs_3_ = bf16[384,128]{1,0:T(8,128)(2,1)S(1)} collective-permute-done((bf16[384,128]{1,0:T(8,128)(2,1)S(1)}, bf16[384,128]{1,0:T(8,128)(2,1)S(1)}, u32[]{:S(2)}, u32[]{:S(2)}) %collective-permute-start.17) | collective-permute-done | bytes 98336 | tf_op jit(solution)/shard_map/ppermute | solution.py:799
  62.6 1.9 %collective-permute-start.20 = (bf16[768,128]{1,0:T(8,128)(2,1)S(1)}, bf16[768,128]{1,0:T(8,128)(2,1)S(1)}, u32[]{:S(2)}, u32[]{:S(2)}) collective-permute-start(bf16[768,128]{1,0:T(8,128)(2,1)S(1)} %get-tuple-element.108), channel_id=1, source_target_pairs={{0,12},{4,8},{8,4},{12,0},{16,28},{20,24},{24,20},{28,16},{1,13},{... | collective-permute-start | bytes 589832 | tf_op jit(solution)/shard_map/ppermute | solution.py:799
  65.7 2.1 %collective-permute-start.13 = (bf16[384,128]{1,0:T(8,128)(2,1)S(1)}, bf16[384,128]{1,0:T(8,128)(2,1)S(1)}, u32[]{:S(2)}, u32[]{:S(2)}) collective-permute-start(bf16[384,128]{1,0:T(8,128)(2,1)S(1)} %get-tuple-element.92), channel_id=1, source_target_pairs={{0,24},{4,28},{8,16},{12,20},{16,8},{20,12},{24,0},{28,4},{1,25},{... | collective-permute-start | bytes 294920 | tf_op jit(solution)/shard_map/ppermute | solution.py:799
  67.9 3.1 %collective-permute-done.12.refs_1_ = bf16[384,128]{1,0:T(8,128)(2,1)S(1)} collective-permute-done((bf16[384,128]{1,0:T(8,128)(2,1)S(1)}, bf16[384,128]{1,0:T(8,128)(2,1)S(1)}, u32[]{:S(2)}, u32[]{:S(2)}) %collective-permute-start.12) | collective-permute-done | bytes 98336 | tf_op jit(solution)/shard_map/ppermute | solution.py:799
  71.0 2.6 %collective-permute-done.13.refs_2_ = bf16[384,128]{1,0:T(8,128)(2,1)S(1)} collective-permute-done((bf16[384,128]{1,0:T(8,128)(2,1)S(1)}, bf16[384,128]{1,0:T(8,128)(2,1)S(1)}, u32[]{:S(2)}, u32[]{:S(2)}) %collective-permute-start.13) | collective-permute-done | bytes 98336 | tf_op jit(solution)/shard_map/ppermute | solution.py:799
  74.1 1.4 %collective-permute-start.22 = (f32[8,128]{1,0:T(8,128)S(1)}, f32[8,128]{1,0:T(8,128)S(1)}, u32[]{:S(2)}, u32[]{:S(2)}) collective-permute-start(f32[8,128]{1,0:T(8,128)S(1)} %shard_map.99), channel_id=1, source_target_pairs={{0,2},{1,3},{2,0},{3,1},{4,6},{5,7},{6,4},{7,5},{8,10},{9,11},{10,... | collective-permute-start | bytes 12296 | tf_op jit(solution)/shard_map/ppermute | solution.py:824
  75.9 1.4 %shard_map.98 = (bf16[192,1024]{1,0:T(8,128)(2,1)}, bf16[192,1024]{1,0:T(8,128)(2,1)}, bf16[192,1024]{1,0:T(8,128)(2,1)}) custom-call(s32[1]{0:T(128)} %bitcast.me_ref, bf16[384,128]{1,0:T(8,128)(2,1)S(1)} %collective-permute-done.11.refs_0_, bf16[384,128]{1,0:T(8,128)(2,1)S(1)} %collective-permute-done.12.refs_1_, ...), custom_call_target="tpu_custom_call" | custom-call | tf_op jit(solution)/shard_map/pallas_call | solution.py:784
  (55 shorter events, 13.3 us)
Async XLA Ops:
  2.9 33.8 %all-to-all-start = ((bf16[4,576,256]{2,1,0:T(8,128)(2,1)}), bf16[4,576,256]{2,1,0:T(8,128)(2,1)S(1)}, u32[]{:S(2)}, u32[]{:S(2)}) async-start(bf16[4,576,256]{2,1,0:T(8,128)(2,1)} %bitcast.14), calls=%async_computation | async-start | bytes 2359296 | tf_op jit(solution)/shard_map/all_to_all | solution.py:814
  8.4 3.1 %collective-permute-start.2 = (f32[8,128]{1,0:T(8,128)S(1)}, f32[8,128]{1,0:T(8,128)S(1)}, u32[]{:S(2)}, u32[]{:S(2)}) collective-permute-start(f32[8,128]{1,0:T(8,128)S(1)} %pad_bitcast_fusion.1), channel_id=1, source_target_pairs={{0,3},{1,2},{2,1},{3,0},{4,7},{5,6},{6,5},{7,4},{8,11},{9,10},{10,... | collective-permute-start | bytes 12296 | tf_op jit(solution)/shard_map/ppermute | solution.py:824
  9.2 3.6 %collective-permute-start.1 = (f32[8,128]{1,0:T(8,128)S(1)}, f32[8,128]{1,0:T(8,128)S(1)}, u32[]{:S(2)}, u32[]{:S(2)}) collective-permute-start(f32[8,128]{1,0:T(8,128)S(1)} %pad_bitcast_fusion.1), channel_id=1, source_target_pairs={{0,2},{1,3},{2,0},{3,1},{4,6},{5,7},{6,4},{7,5},{8,10},{9,11},{10,... | collective-permute-start | bytes 12296 | tf_op jit(solution)/shard_map/ppermute | solution.py:824
  10.1 2.7 %collective-permute-start = (f32[8,128]{1,0:T(8,128)S(1)}, f32[8,128]{1,0:T(8,128)S(1)}, u32[]{:S(2)}, u32[]{:S(2)}) collective-permute-start(f32[8,128]{1,0:T(8,128)S(1)} %pad_bitcast_fusion.1), channel_id=1, source_target_pairs={{0,1},{1,0},{2,3},{3,2},{4,5},{5,4},{6,7},{7,6},{8,9},{9,8},{10,11... | collective-permute-start | bytes 12296 | tf_op jit(solution)/shard_map/ppermute | solution.py:824
  13.2 11.2 %collective-permute-start.3 = (bf16[400,128]{1,0:T(8,128)(2,1)S(1)}, bf16[400,128]{1,0:T(8,128)(2,1)S(1)}, u32[]{:S(2)}, u32[]{:S(2)}) collective-permute-start(bf16[400,128]{1,0:T(8,128)(2,1)S(1)} %get-tuple-element.62), channel_id=1, source_target_pairs={{0,16},{4,20},{8,24},{12,28},{16,0},{20,4},{24,8},{28,12},{1,17},{... | collective-permute-start | bytes 307208 | tf_op jit(solution)/shard_map/ppermute | solution.py:799
  15.9 13.7 %collective-permute-start.4 = (bf16[400,128]{1,0:T(8,128)(2,1)S(1)}, bf16[400,128]{1,0:T(8,128)(2,1)S(1)}, u32[]{:S(2)}, u32[]{:S(2)}) collective-permute-start(bf16[400,128]{1,0:T(8,128)(2,1)S(1)} %get-tuple-element.64), channel_id=1, source_target_pairs={{0,20},{4,16},{8,28},{12,24},{16,4},{20,0},{24,12},{28,8},{1,21},{... | collective-permute-start | bytes 307208 | tf_op jit(solution)/shard_map/ppermute | solution.py:799
  17.4 16.0 %collective-permute-start.5 = (bf16[400,128]{1,0:T(8,128)(2,1)S(1)}, bf16[400,128]{1,0:T(8,128)(2,1)S(1)}, u32[]{:S(2)}, u32[]{:S(2)}) collective-permute-start(bf16[400,128]{1,0:T(8,128)(2,1)S(1)} %get-tuple-element.65), channel_id=1, source_target_pairs={{0,24},{4,28},{8,16},{12,20},{16,8},{20,12},{24,0},{28,4},{1,25},{... | collective-permute-start | bytes 307208 | tf_op jit(solution)/shard_map/ppermute | solution.py:799
  20.9 15.6 %collective-permute-start.6 = (bf16[400,128]{1,0:T(8,128)(2,1)S(1)}, bf16[400,128]{1,0:T(8,128)(2,1)S(1)}, u32[]{:S(2)}, u32[]{:S(2)}) collective-permute-start(bf16[400,128]{1,0:T(8,128)(2,1)S(1)} %get-tuple-element.66), channel_id=1, source_target_pairs={{0,28},{4,24},{8,20},{12,16},{16,12},{20,8},{24,4},{28,0},{1,29},{... | collective-permute-start | bytes 307208 | tf_op jit(solution)/shard_map/ppermute | solution.py:799
  21.0 15.5 %collective-permute-start.7 = (bf16[208,256]{1,0:T(8,128)(2,1)S(1)}, bf16[208,256]{1,0:T(8,128)(2,1)S(1)}, u32[]{:S(2)}, u32[]{:S(2)}) collective-permute-start(bf16[208,256]{1,0:T(8,128)(2,1)S(1)} %get-tuple-element.67), channel_id=1, source_target_pairs={{0,12},{4,8},{8,4},{12,0},{16,28},{20,24},{24,20},{28,16},{1,13},{... | collective-permute-start | bytes 319496 | tf_op jit(solution)/shard_map/ppermute | solution.py:799
  24.5 12.2 %collective-permute-start.8 = (bf16[208,256]{1,0:T(8,128)(2,1)S(1)}, bf16[208,256]{1,0:T(8,128)(2,1)S(1)}, u32[]{:S(2)}, u32[]{:S(2)}) collective-permute-start(bf16[208,256]{1,0:T(8,128)(2,1)S(1)} %get-tuple-element.68), channel_id=1, source_target_pairs={{0,8},{4,12},{8,0},{12,4},{16,24},{20,28},{24,16},{28,20},{1,9},{5... | collective-permute-start | bytes 319496 | tf_op jit(solution)/shard_map/ppermute | solution.py:799
  29.6 7.0 %collective-permute-start.9 = (bf16[208,256]{1,0:T(8,128)(2,1)S(1)}, bf16[208,256]{1,0:T(8,128)(2,1)S(1)}, u32[]{:S(2)}, u32[]{:S(2)}) collective-permute-start(bf16[208,256]{1,0:T(8,128)(2,1)S(1)} %get-tuple-element.69), channel_id=1, source_target_pairs={{0,4},{4,0},{8,12},{12,8},{16,20},{20,16},{24,28},{28,24},{1,5},{5... | collective-permute-start | bytes 319496 | tf_op jit(solution)/shard_map/ppermute | solution.py:799
  38.5 7.7 %collective-permute-start.10 = (f32[24,128]{1,0:T(8,128)S(1)}, f32[24,128]{1,0:T(8,128)S(1)}, u32[]{:S(2)}, u32[]{:S(2)}) collective-permute-start(f32[24,128]{1,0:T(8,128)S(1)} %shard_map.95.refs_8_), channel_id=1, source_target_pairs={{0,16},{4,20},{8,24},{12,28},{16,0},{20,4},{24,8},{28,12},{1,17},{... | collective-permute-start | bytes 36872 | tf_op jit(solution)/shard_map/ppermute | solution.py:799
  46.2 15.2 %collective-permute-start.14 = (bf16[768,128]{1,0:T(8,128)(2,1)S(1)}, bf16[768,128]{1,0:T(8,128)(2,1)S(1)}, u32[]{:S(2)}, u32[]{:S(2)}) collective-permute-start(bf16[768,128]{1,0:T(8,128)(2,1)S(1)} %get-tuple-element.96), channel_id=1, source_target_pairs={{0,4},{4,0},{8,12},{12,8},{16,20},{20,16},{24,28},{28,24},{1,5},{5... | collective-permute-start | bytes 589832 | tf_op jit(solution)/shard_map/ppermute | solution.py:799
  46.7 14.7 %collective-permute-start.15 = (bf16[768,128]{1,0:T(8,128)(2,1)S(1)}, bf16[768,128]{1,0:T(8,128)(2,1)S(1)}, u32[]{:S(2)}, u32[]{:S(2)}) collective-permute-start(bf16[768,128]{1,0:T(8,128)(2,1)S(1)} %get-tuple-element.97), channel_id=1, source_target_pairs={{0,8},{4,12},{8,0},{12,4},{16,24},{20,28},{24,16},{28,20},{1,9},{5... | collective-permute-start | bytes 589832 | tf_op jit(solution)/shard_map/ppermute | solution.py:799
  47.2 14.2 %collective-permute-start.16 = (bf16[768,128]{1,0:T(8,128)(2,1)S(1)}, bf16[768,128]{1,0:T(8,128)(2,1)S(1)}, u32[]{:S(2)}, u32[]{:S(2)}) collective-permute-start(bf16[768,128]{1,0:T(8,128)(2,1)S(1)} %get-tuple-element.98), channel_id=1, source_target_pairs={{0,12},{4,8},{8,4},{12,0},{16,28},{20,24},{24,20},{28,16},{1,13},{... | collective-permute-start | bytes 589832 | tf_op jit(solution)/shard_map/ppermute | solution.py:799
  52.5 6.0 %collective-permute-start.11 = (bf16[384,128]{1,0:T(8,128)(2,1)S(1)}, bf16[384,128]{1,0:T(8,128)(2,1)S(1)}, u32[]{:S(2)}, u32[]{:S(2)}) collective-permute-start(bf16[384,128]{1,0:T(8,128)(2,1)S(1)} %get-tuple-element.89), channel_id=1, source_target_pairs={{0,16},{4,20},{8,24},{12,28},{16,0},{20,4},{24,8},{28,12},{1,17},{... | collective-permute-start | bytes 294920 | tf_op jit(solution)/shard_map/ppermute | solution.py:799
  52.8 8.6 %collective-permute-start.17 = (bf16[384,128]{1,0:T(8,128)(2,1)S(1)}, bf16[384,128]{1,0:T(8,128)(2,1)S(1)}, u32[]{:S(2)}, u32[]{:S(2)}) collective-permute-start(bf16[384,128]{1,0:T(8,128)(2,1)S(1)} %get-tuple-element.99), channel_id=1, source_target_pairs={{0,28},{4,24},{8,20},{12,16},{16,12},{20,8},{24,4},{28,0},{1,29},{... | collective-permute-start | bytes 294920 | tf_op jit(solution)/shard_map/ppermute | solution.py:799
  58.5 15.1 %collective-permute-start.18 = (bf16[768,128]{1,0:T(8,128)(2,1)S(1)}, bf16[768,128]{1,0:T(8,128)(2,1)S(1)}, u32[]{:S(2)}, u32[]{:S(2)}) collective-permute-start(bf16[768,128]{1,0:T(8,128)(2,1)S(1)} %get-tuple-element.106), channel_id=1, source_target_pairs={{0,4},{4,0},{8,12},{12,8},{16,20},{20,16},{24,28},{28,24},{1,5},{5... | collective-permute-start | bytes 589832 | tf_op jit(solution)/shard_map/ppermute | solution.py:799
  61.4 12.3 %collective-permute-start.19 = (bf16[768,128]{1,0:T(8,128)(2,1)S(1)}, bf16[768,128]{1,0:T(8,128)(2,1)S(1)}, u32[]{:S(2)}, u32[]{:S(2)}) collective-permute-start(bf16[768,128]{1,0:T(8,128)(2,1)S(1)} %get-tuple-element.107), channel_id=1, source_target_pairs={{0,8},{4,12},{8,0},{12,4},{16,24},{20,28},{24,16},{28,20},{1,9},{5... | collective-permute-start | bytes 589832 | tf_op jit(solution)/shard_map/ppermute | solution.py:799
  62.6 11.0 %collective-permute-start.20 = (bf16[768,128]{1,0:T(8,128)(2,1)S(1)}, bf16[768,128]{1,0:T(8,128)(2,1)S(1)}, u32[]{:S(2)}, u32[]{:S(2)}) collective-permute-start(bf16[768,128]{1,0:T(8,128)(2,1)S(1)} %get-tuple-element.108), channel_id=1, source_target_pairs={{0,12},{4,8},{8,4},{12,0},{16,28},{20,24},{24,20},{28,16},{1,13},{... | collective-permute-start | bytes 589832 | tf_op jit(solution)/shard_map/ppermute | solution.py:799
  64.4 6.5 %collective-permute-start.12 = (bf16[384,128]{1,0:T(8,128)(2,1)S(1)}, bf16[384,128]{1,0:T(8,128)(2,1)S(1)}, u32[]{:S(2)}, u32[]{:S(2)}) collective-permute-start(bf16[384,128]{1,0:T(8,128)(2,1)S(1)} %get-tuple-element.91), channel_id=1, source_target_pairs={{0,20},{4,16},{8,28},{12,24},{16,4},{20,0},{24,12},{28,8},{1,21},{... | collective-permute-start | bytes 294920 | tf_op jit(solution)/shard_map/ppermute | solution.py:799
  65.7 7.9 %collective-permute-start.13 = (bf16[384,128]{1,0:T(8,128)(2,1)S(1)}, bf16[384,128]{1,0:T(8,128)(2,1)S(1)}, u32[]{:S(2)}, u32[]{:S(2)}) collective-permute-start(bf16[384,128]{1,0:T(8,128)(2,1)S(1)} %get-tuple-element.92), channel_id=1, source_target_pairs={{0,24},{4,28},{8,16},{12,20},{16,8},{20,12},{24,0},{28,4},{1,25},{... | collective-permute-start | bytes 294920 | tf_op jit(solution)/shard_map/ppermute | solution.py:799
  74.0 3.3 %collective-permute-start.23 = (f32[8,128]{1,0:T(8,128)S(1)}, f32[8,128]{1,0:T(8,128)S(1)}, u32[]{:S(2)}, u32[]{:S(2)}) collective-permute-start(f32[8,128]{1,0:T(8,128)S(1)} %shard_map.99), channel_id=1, source_target_pairs={{0,3},{1,2},{2,1},{3,0},{4,7},{5,6},{6,5},{7,4},{8,11},{9,10},{10,... | collective-permute-start | bytes 12296 | tf_op jit(solution)/shard_map/ppermute | solution.py:824
  74.1 3.7 %collective-permute-start.22 = (f32[8,128]{1,0:T(8,128)S(1)}, f32[8,128]{1,0:T(8,128)S(1)}, u32[]{:S(2)}, u32[]{:S(2)}) collective-permute-start(f32[8,128]{1,0:T(8,128)S(1)} %shard_map.99), channel_id=1, source_target_pairs={{0,2},{1,3},{2,0},{3,1},{4,6},{5,7},{6,4},{7,5},{8,10},{9,11},{10,... | collective-permute-start | bytes 12296 | tf_op jit(solution)/shard_map/ppermute | solution.py:824
  (7 other events, 68.0 us)

commit v6 on v5

--- a/solution.py
+++ b/solution.py
@@ -718,15 +718,15 @@
     tokens, features = key_ref.shape
     width = features // half_count
     inside = me_ref[0] & (half_count - 1)
-    rms = column_of(rms_ref[...], 0, tokens)
-    inner = column_of(inner_ref[...], 0, tokens) / feature_total
+    inverse = 1.0 / column_of(rms_ref[...], 0, tokens)
+    inner = column_of(inner_ref[...], 0, tokens) * inverse / feature_total
     for distance in range(half_count):
         columns = pl.ds(pl.multiple_of((inside ^ distance) * width, LANES), width)
-        normed_float = key_ref[:, columns].astype(jnp.float32) / rms
+        key_float = key_ref[:, columns].astype(jnp.float32)
         grad_float = normed_grad_of(
             half_count, me_ref, first_refs[distance], second_refs[distance], cross_refs[distance]
         )
-        key_out_ref[:, columns] = ((grad_float - normed_float * inner) / rms).astype(jnp.bfloat16)
+        key_out_ref[:, columns] = ((grad_float - key_float * inner) * inverse).astype(jnp.bfloat16)
 
 
 def final_kernel(half_count, me_ref, *refs):

time: 79.1 us -> 79.1 us (level)
  no operation moved by 1% of the time
where the time goes in v6:
time: 79.1 us; the launch traced here: 78.8 us
  starting transfers between devices  41.5 us (52%)
  waiting for transfers between devices  21.9 us (28%)
  Pallas kernels  14.3 us (18%)
  between operations  0.8 us (1%)
    ppermute x18, starting transfers between devices, swap(): return lax.ppermute(block, 'seq', [(i, i ^ distance) for i in range(count)])  32.3 us
    ppermute x18, waiting for transfers between devices, swap(): return lax.ppermute(block, 'seq', [(i, i ^ distance) for i in range(count)])  19 us
    pallas_call x8, Pallas kernels, call(): pl.pallas_call(kernel, out_shape=out_shapes, in_specs=[pl.BlockSpec(memor...  14.3 us
    all_to_all x1, starting transfers between devices, exchange_inside(): lax.all_to_all(parts, 'seq', split_axis=0, concat_axis=0, tiled=True, axi...  5.39 us
    ppermute x6, starting transfers between devices, sum_over_head(): lax.ppermute(block, 'head', [(i, i ^ d) for i in range(count)])  3.84 us
    ppermute x6, waiting for transfers between devices, sum_over_head(): lax.ppermute(block, 'head', [(i, i ^ d) for i in range(count)])  2.86 us
  transfers between devices with their start and end apart: 25, of which 11 were waited for; matrix products, arithmetic and copies ran while one was open for 0% of the time, Pallas kernels for 11%

profile of v6, /device:TPU:0, one launch (start us, length us, event | category | flops | bytes accessed | tf_op | source)
XLA Modules:
  0.0 78.8 jit_solution(16867062609233199910)
XLA Ops:
  0.6 2.2 %shard_map.93 = bf16[2304,256]{1,0:T(8,128)(2,1)} custom-call(bf16[192,1024]{1,0:T(8,128)(2,1)} %query_ref.3, bf16[192,1024]{1,0:T(8,128)(2,1)} %value_ref.3, bf16[192,1024]{1,0:T(8,128)(2,1)} %grad_ref.3), custom_call_target="tpu_custom_call" | custom-call | tf_op jit(solution)/shard_map/pallas_call | solution.py:784
  2.9 5.4 %all-to-all-start = ((bf16[4,576,256]{2,1,0:T(8,128)(2,1)}), bf16[4,576,256]{2,1,0:T(8,128)(2,1)S(1)}, u32[]{:S(2)}, u32[]{:S(2)}) async-start(bf16[4,576,256]{2,1,0:T(8,128)(2,1)} %bitcast.14), calls=%async_computation | async-start | bytes 2359296 | tf_op jit(solution)/shard_map/all_to_all | solution.py:814
  13.2 2.6 %collective-permute-start.3 = (bf16[400,128]{1,0:T(8,128)(2,1)S(1)}, bf16[400,128]{1,0:T(8,128)(2,1)S(1)}, u32[]{:S(2)}, u32[]{:S(2)}) collective-permute-start(bf16[400,128]{1,0:T(8,128)(2,1)S(1)} %get-tuple-element.62), channel_id=1, source_target_pairs={{0,16},{4,20},{8,24},{12,28},{16,0},{20,4},{24,8},{28,12},{1,17},{... | collective-permute-start | bytes 307208 | tf_op jit(solution)/shard_map/ppermute | solution.py:799
  15.9 1.5 %collective-permute-start.4 = (bf16[400,128]{1,0:T(8,128)(2,1)S(1)}, bf16[400,128]{1,0:T(8,128)(2,1)S(1)}, u32[]{:S(2)}, u32[]{:S(2)}) collective-permute-start(bf16[400,128]{1,0:T(8,128)(2,1)S(1)} %get-tuple-element.64), channel_id=1, source_target_pairs={{0,20},{4,16},{8,28},{12,24},{16,4},{20,0},{24,12},{28,8},{1,21},{... | collective-permute-start | bytes 307208 | tf_op jit(solution)/shard_map/ppermute | solution.py:799
  17.4 3.5 %collective-permute-start.5 = (bf16[400,128]{1,0:T(8,128)(2,1)S(1)}, bf16[400,128]{1,0:T(8,128)(2,1)S(1)}, u32[]{:S(2)}, u32[]{:S(2)}) collective-permute-start(bf16[400,128]{1,0:T(8,128)(2,1)S(1)} %get-tuple-element.65), channel_id=1, source_target_pairs={{0,24},{4,28},{8,16},{12,20},{16,8},{20,12},{24,0},{28,4},{1,25},{... | collective-permute-start | bytes 307208 | tf_op jit(solution)/shard_map/ppermute | solution.py:799
  21.8 2.7 %collective-permute-done.3.refs_0_ = bf16[400,128]{1,0:T(8,128)(2,1)S(1)} collective-permute-done((bf16[400,128]{1,0:T(8,128)(2,1)S(1)}, bf16[400,128]{1,0:T(8,128)(2,1)S(1)}, u32[]{:S(2)}, u32[]{:S(2)}) %collective-permute-start.3) | collective-permute-done | bytes 102432 | tf_op jit(solution)/shard_map/ppermute | solution.py:799
  24.5 5.1 %collective-permute-start.8 = (bf16[208,256]{1,0:T(8,128)(2,1)S(1)}, bf16[208,256]{1,0:T(8,128)(2,1)S(1)}, u32[]{:S(2)}, u32[]{:S(2)}) collective-permute-start(bf16[208,256]{1,0:T(8,128)(2,1)S(1)} %get-tuple-element.68), channel_id=1, source_target_pairs={{0,8},{4,12},{8,0},{12,4},{16,24},{20,28},{24,16},{28,20},{1,9},{5... | collective-permute-start | bytes 319496 | tf_op jit(solution)/shard_map/ppermute | solution.py:799
  29.6 1.5 %collective-permute-start.9 = (bf16[208,256]{1,0:T(8,128)(2,1)S(1)}, bf16[208,256]{1,0:T(8,128)(2,1)S(1)}, u32[]{:S(2)}, u32[]{:S(2)}) collective-permute-start(bf16[208,256]{1,0:T(8,128)(2,1)S(1)} %get-tuple-element.69), channel_id=1, source_target_pairs={{0,4},{4,0},{8,12},{12,8},{16,20},{20,16},{24,28},{28,24},{1,5},{5... | collective-permute-start | bytes 319496 | tf_op jit(solution)/shard_map/ppermute | solution.py:799
  31.2 2.2 %collective-permute-done.5.refs_2_ = bf16[400,128]{1,0:T(8,128)(2,1)S(1)} collective-permute-done((bf16[400,128]{1,0:T(8,128)(2,1)S(1)}, bf16[400,128]{1,0:T(8,128)(2,1)S(1)}, u32[]{:S(2)}, u32[]{:S(2)}) %collective-permute-start.5) | collective-permute-done | bytes 102432 | tf_op jit(solution)/shard_map/ppermute | solution.py:799
  33.4 3.1 %collective-permute-done.6.refs_3_ = bf16[400,128]{1,0:T(8,128)(2,1)S(1)} collective-permute-done((bf16[400,128]{1,0:T(8,128)(2,1)S(1)}, bf16[400,128]{1,0:T(8,128)(2,1)S(1)}, u32[]{:S(2)}, u32[]{:S(2)}) %collective-permute-start.6) | collective-permute-done | bytes 102432 | tf_op jit(solution)/shard_map/ppermute | solution.py:799
  36.7 1.8 %shard_map.95.refs_8_ = f32[24,128]{1,0:T(8,128)S(1)} custom-call(s32[1]{0:T(128)} %bitcast.me_ref, f32[12,128]{1,0:T(8,128)S(1)} %pad.13.pattern_ref, bf16[2304,256]{1,0:T(8,128)(2,1)S(1)} %bitcast.11, bf16[400,128]{1,0:T(8,128)(2,1)S(1)} %collective-permute-done.3.refs_0_, bf16[400,128]{1,0:T(8,128)(2,1)S(1)} %collective-permute-done.4.refs_1_, ...), custom_call_target="tpu_custom_call" | custom-call | flops 301989888 | tf_op jit(solution)/shard_map/pallas_call | solution.py:784
  38.5 3.3 %collective-permute-start.10 = (f32[24,128]{1,0:T(8,128)S(1)}, f32[24,128]{1,0:T(8,128)S(1)}, u32[]{:S(2)}, u32[]{:S(2)}) collective-permute-start(f32[24,128]{1,0:T(8,128)S(1)} %shard_map.95.refs_8_), channel_id=1, source_target_pairs={{0,16},{4,20},{8,24},{12,28},{16,0},{20,4},{24,8},{28,12},{1,17},{... | collective-permute-start | bytes 36872 | tf_op jit(solution)/shard_map/ppermute | solution.py:799
  41.8 4.3 %shard_map.96 = (bf16[768,128]{1,0:T(8,128)(2,1)S(1)}, bf16[768,128]{1,0:T(8,128)(2,1)S(1)}, bf16[768,128]{1,0:T(8,128)(2,1)S(1)}, bf16[768,128]{1,0:T(8,128)(2,...) custom-call(s32[1]{0:T(128)} %bitcast.me_ref, ...), custom_call_target="tpu_custom_call" | custom-call | flops 1358954496 | tf_op jit(solution)/shard_map/pallas_call | solution.py:784
  47.2 2.5 %collective-permute-start.16 = (bf16[768,128]{1,0:T(8,128)(2,1)S(1)}, bf16[768,128]{1,0:T(8,128)(2,1)S(1)}, u32[]{:S(2)}, u32[]{:S(2)}) collective-permute-start(bf16[768,128]{1,0:T(8,128)(2,1)S(1)} %get-tuple-element.98), channel_id=1, source_target_pairs={{0,12},{4,8},{8,4},{12,0},{16,28},{20,24},{24,20},{28,16},{1,13},{... | collective-permute-start | bytes 589832 | tf_op jit(solution)/shard_map/ppermute | solution.py:799
  49.7 2.8 %shard_map.97 = (bf16[768,128]{1,0:T(8,128)(2,1)S(1)}, bf16[768,128]{1,0:T(8,128)(2,1)S(1)}, bf16[768,128]{1,0:T(8,128)(2,1)S(1)}, bf16[768,128]{1,0:T(8,128)(2,...) custom-call(s32[1]{0:T(128)} %bitcast.me_ref, ...), custom_call_target="tpu_custom_call" | custom-call | flops 905969664 | tf_op jit(solution)/shard_map/pallas_call | solution.py:784
  52.8 2.6 %collective-permute-start.17 = (bf16[384,128]{1,0:T(8,128)(2,1)S(1)}, bf16[384,128]{1,0:T(8,128)(2,1)S(1)}, u32[]{:S(2)}, u32[]{:S(2)}) collective-permute-start(bf16[384,128]{1,0:T(8,128)(2,1)S(1)} %get-tuple-element.99), channel_id=1, source_target_pairs={{0,28},{4,24},{8,20},{12,16},{16,12},{20,8},{24,4},{28,0},{1,29},{... | collective-permute-start | bytes 294920 | tf_op jit(solution)/shard_map/ppermute | solution.py:799
  55.4 3.1 %collective-permute-done.11.refs_0_ = bf16[384,128]{1,0:T(8,128)(2,1)S(1)} collective-permute-done((bf16[384,128]{1,0:T(8,128)(2,1)S(1)}, bf16[384,128]{1,0:T(8,128)(2,1)S(1)}, u32[]{:S(2)}, u32[]{:S(2)}) %collective-permute-start.11) | collective-permute-done | bytes 98336 | tf_op jit(solution)/shard_map/ppermute | solution.py:799
  59.4 2.0 %collective-permute-done.17.refs_3_ = bf16[384,128]{1,0:T(8,128)(2,1)S(1)} collective-permute-done((bf16[384,128]{1,0:T(8,128)(2,1)S(1)}, bf16[384,128]{1,0:T(8,128)(2,1)S(1)}, u32[]{:S(2)}, u32[]{:S(2)}) %collective-permute-start.17) | collective-permute-done | bytes 98336 | tf_op jit(solution)/shard_map/ppermute | solution.py:799
  62.6 1.9 %collective-permute-start.20 = (bf16[768,128]{1,0:T(8,128)(2,1)S(1)}, bf16[768,128]{1,0:T(8,128)(2,1)S(1)}, u32[]{:S(2)}, u32[]{:S(2)}) collective-permute-start(bf16[768,128]{1,0:T(8,128)(2,1)S(1)} %get-tuple-element.108), channel_id=1, source_target_pairs={{0,12},{4,8},{8,4},{12,0},{16,28},{20,24},{24,20},{28,16},{1,13},{... | collective-permute-start | bytes 589832 | tf_op jit(solution)/shard_map/ppermute | solution.py:799
  65.7 2.1 %collective-permute-start.13 = (bf16[384,128]{1,0:T(8,128)(2,1)S(1)}, bf16[384,128]{1,0:T(8,128)(2,1)S(1)}, u32[]{:S(2)}, u32[]{:S(2)}) collective-permute-start(bf16[384,128]{1,0:T(8,128)(2,1)S(1)} %get-tuple-element.92), channel_id=1, source_target_pairs={{0,24},{4,28},{8,16},{12,20},{16,8},{20,12},{24,0},{28,4},{1,25},{... | collective-permute-start | bytes 294920 | tf_op jit(solution)/shard_map/ppermute | solution.py:799
  67.9 3.1 %collective-permute-done.12.refs_1_ = bf16[384,128]{1,0:T(8,128)(2,1)S(1)} collective-permute-done((bf16[384,128]{1,0:T(8,128)(2,1)S(1)}, bf16[384,128]{1,0:T(8,128)(2,1)S(1)}, u32[]{:S(2)}, u32[]{:S(2)}) %collective-permute-start.12) | collective-permute-done | bytes 98336 | tf_op jit(solution)/shard_map/ppermute | solution.py:799
  71.0 2.6 %collective-permute-done.13.refs_2_ = bf16[384,128]{1,0:T(8,128)(2,1)S(1)} collective-permute-done((bf16[384,128]{1,0:T(8,128)(2,1)S(1)}, bf16[384,128]{1,0:T(8,128)(2,1)S(1)}, u32[]{:S(2)}, u32[]{:S(2)}) %collective-permute-start.13) | collective-permute-done | bytes 98336 | tf_op jit(solution)/shard_map/ppermute | solution.py:799
  74.1 1.4 %collective-permute-start.22 = (f32[8,128]{1,0:T(8,128)S(1)}, f32[8,128]{1,0:T(8,128)S(1)}, u32[]{:S(2)}, u32[]{:S(2)}) collective-permute-start(f32[8,128]{1,0:T(8,128)S(1)} %shard_map.99), channel_id=1, source_target_pairs={{0,2},{1,3},{2,0},{3,1},{4,6},{5,7},{6,4},{7,5},{8,10},{9,11},{10,... | collective-permute-start | bytes 12296 | tf_op jit(solution)/shard_map/ppermute | solution.py:824
  75.9 1.4 %shard_map.98 = (bf16[192,1024]{1,0:T(8,128)(2,1)}, bf16[192,1024]{1,0:T(8,128)(2,1)}, bf16[192,1024]{1,0:T(8,128)(2,1)}) custom-call(s32[1]{0:T(128)} %bitcast.me_ref, bf16[384,128]{1,0:T(8,128)(2,1)S(1)} %collective-permute-done.11.refs_0_, bf16[384,128]{1,0:T(8,128)(2,1)S(1)} %collective-permute-done.12.refs_1_, ...), custom_call_target="tpu_custom_call" | custom-call | tf_op jit(solution)/shard_map/pallas_call | solution.py:784
  (55 shorter events, 13.3 us)
Async XLA Ops:
  2.9 33.8 %all-to-all-start = ((bf16[4,576,256]{2,1,0:T(8,128)(2,1)}), bf16[4,576,256]{2,1,0:T(8,128)(2,1)S(1)}, u32[]{:S(2)}, u32[]{:S(2)}) async-start(bf16[4,576,256]{2,1,0:T(8,128)(2,1)} %bitcast.14), calls=%async_computation | async-start | bytes 2359296 | tf_op jit(solution)/shard_map/all_to_all | solution.py:814
  8.4 3.1 %collective-permute-start.2 = (f32[8,128]{1,0:T(8,128)S(1)}, f32[8,128]{1,0:T(8,128)S(1)}, u32[]{:S(2)}, u32[]{:S(2)}) collective-permute-start(f32[8,128]{1,0:T(8,128)S(1)} %pad_bitcast_fusion.1), channel_id=1, source_target_pairs={{0,3},{1,2},{2,1},{3,0},{4,7},{5,6},{6,5},{7,4},{8,11},{9,10},{10,... | collective-permute-start | bytes 12296 | tf_op jit(solution)/shard_map/ppermute | solution.py:824
  9.2 3.6 %collective-permute-start.1 = (f32[8,128]{1,0:T(8,128)S(1)}, f32[8,128]{1,0:T(8,128)S(1)}, u32[]{:S(2)}, u32[]{:S(2)}) collective-permute-start(f32[8,128]{1,0:T(8,128)S(1)} %pad_bitcast_fusion.1), channel_id=1, source_target_pairs={{0,2},{1,3},{2,0},{3,1},{4,6},{5,7},{6,4},{7,5},{8,10},{9,11},{10,... | collective-permute-start | bytes 12296 | tf_op jit(solution)/shard_map/ppermute | solution.py:824
  10.1 2.7 %collective-permute-start = (f32[8,128]{1,0:T(8,128)S(1)}, f32[8,128]{1,0:T(8,128)S(1)}, u32[]{:S(2)}, u32[]{:S(2)}) collective-permute-start(f32[8,128]{1,0:T(8,128)S(1)} %pad_bitcast_fusion.1), channel_id=1, source_target_pairs={{0,1},{1,0},{2,3},{3,2},{4,5},{5,4},{6,7},{7,6},{8,9},{9,8},{10,11... | collective-permute-start | bytes 12296 | tf_op jit(solution)/shard_map/ppermute | solution.py:824
  13.2 11.2 %collective-permute-start.3 = (bf16[400,128]{1,0:T(8,128)(2,1)S(1)}, bf16[400,128]{1,0:T(8,128)(2,1)S(1)}, u32[]{:S(2)}, u32[]{:S(2)}) collective-permute-start(bf16[400,128]{1,0:T(8,128)(2,1)S(1)} %get-tuple-element.62), channel_id=1, source_target_pairs={{0,16},{4,20},{8,24},{12,28},{16,0},{20,4},{24,8},{28,12},{1,17},{... | collective-permute-start | bytes 307208 | tf_op jit(solution)/shard_map/ppermute | solution.py:799
  15.9 13.7 %collective-permute-start.4 = (bf16[400,128]{1,0:T(8,128)(2,1)S(1)}, bf16[400,128]{1,0:T(8,128)(2,1)S(1)}, u32[]{:S(2)}, u32[]{:S(2)}) collective-permute-start(bf16[400,128]{1,0:T(8,128)(2,1)S(1)} %get-tuple-element.64), channel_id=1, source_target_pairs={{0,20},{4,16},{8,28},{12,24},{16,4},{20,0},{24,12},{28,8},{1,21},{... | collective-permute-start | bytes 307208 | tf_op jit(solution)/shard_map/ppermute | solution.py:799
  17.4 16.0 %collective-permute-start.5 = (bf16[400,128]{1,0:T(8,128)(2,1)S(1)}, bf16[400,128]{1,0:T(8,128)(2,1)S(1)}, u32[]{:S(2)}, u32[]{:S(2)}) collective-permute-start(bf16[400,128]{1,0:T(8,128)(2,1)S(1)} %get-tuple-element.65), channel_id=1, source_target_pairs={{0,24},{4,28},{8,16},{12,20},{16,8},{20,12},{24,0},{28,4},{1,25},{... | collective-permute-start | bytes 307208 | tf_op jit(solution)/shard_map/ppermute | solution.py:799
  20.9 15.6 %collective-permute-start.6 = (bf16[400,128]{1,0:T(8,128)(2,1)S(1)}, bf16[400,128]{1,0:T(8,128)(2,1)S(1)}, u32[]{:S(2)}, u32[]{:S(2)}) collective-permute-start(bf16[400,128]{1,0:T(8,128)(2,1)S(1)} %get-tuple-element.66), channel_id=1, source_target_pairs={{0,28},{4,24},{8,20},{12,16},{16,12},{20,8},{24,4},{28,0},{1,29},{... | collective-permute-start | bytes 307208 | tf_op jit(solution)/shard_map/ppermute | solution.py:799
  21.0 15.5 %collective-permute-start.7 = (bf16[208,256]{1,0:T(8,128)(2,1)S(1)}, bf16[208,256]{1,0:T(8,128)(2,1)S(1)}, u32[]{:S(2)}, u32[]{:S(2)}) collective-permute-start(bf16[208,256]{1,0:T(8,128)(2,1)S(1)} %get-tuple-element.67), channel_id=1, source_target_pairs={{0,12},{4,8},{8,4},{12,0},{16,28},{20,24},{24,20},{28,16},{1,13},{... | collective-permute-start | bytes 319496 | tf_op jit(solution)/shard_map/ppermute | solution.py:799
  24.5 12.2 %collective-permute-start.8 = (bf16[208,256]{1,0:T(8,128)(2,1)S(1)}, bf16[208,256]{1,0:T(8,128)(2,1)S(1)}, u32[]{:S(2)}, u32[]{:S(2)}) collective-permute-start(bf16[208,256]{1,0:T(8,128)(2,1)S(1)} %get-tuple-element.68), channel_id=1, source_target_pairs={{0,8},{4,12},{8,0},{12,4},{16,24},{20,28},{24,16},{28,20},{1,9},{5... | collective-permute-start | bytes 319496 | tf_op jit(solution)/shard_map/ppermute | solution.py:799
  29.6 7.0 %collective-permute-start.9 = (bf16[208,256]{1,0:T(8,128)(2,1)S(1)}, bf16[208,256]{1,0:T(8,128)(2,1)S(1)}, u32[]{:S(2)}, u32[]{:S(2)}) collective-permute-start(bf16[208,256]{1,0:T(8,128)(2,1)S(1)} %get-tuple-element.69), channel_id=1, source_target_pairs={{0,4},{4,0},{8,12},{12,8},{16,20},{20,16},{24,28},{28,24},{1,5},{5... | collective-permute-start | bytes 319496 | tf_op jit(solution)/shard_map/ppermute | solution.py:799
  38.5 7.7 %collective-permute-start.10 = (f32[24,128]{1,0:T(8,128)S(1)}, f32[24,128]{1,0:T(8,128)S(1)}, u32[]{:S(2)}, u32[]{:S(2)}) collective-permute-start(f32[24,128]{1,0:T(8,128)S(1)} %shard_map.95.refs_8_), channel_id=1, source_target_pairs={{0,16},{4,20},{8,24},{12,28},{16,0},{20,4},{24,8},{28,12},{1,17},{... | collective-permute-start | bytes 36872 | tf_op jit(solution)/shard_map/ppermute | solution.py:799
  46.2 15.2 %collective-permute-start.14 = (bf16[768,128]{1,0:T(8,128)(2,1)S(1)}, bf16[768,128]{1,0:T(8,128)(2,1)S(1)}, u32[]{:S(2)}, u32[]{:S(2)}) collective-permute-start(bf16[768,128]{1,0:T(8,128)(2,1)S(1)} %get-tuple-element.96), channel_id=1, source_target_pairs={{0,4},{4,0},{8,12},{12,8},{16,20},{20,16},{24,28},{28,24},{1,5},{5... | collective-permute-start | bytes 589832 | tf_op jit(solution)/shard_map/ppermute | solution.py:799
  46.7 14.7 %collective-permute-start.15 = (bf16[768,128]{1,0:T(8,128)(2,1)S(1)}, bf16[768,128]{1,0:T(8,128)(2,1)S(1)}, u32[]{:S(2)}, u32[]{:S(2)}) collective-permute-start(bf16[768,128]{1,0:T(8,128)(2,1)S(1)} %get-tuple-element.97), channel_id=1, source_target_pairs={{0,8},{4,12},{8,0},{12,4},{16,24},{20,28},{24,16},{28,20},{1,9},{5... | collective-permute-start | bytes 589832 | tf_op jit(solution)/shard_map/ppermute | solution.py:799
  47.2 14.2 %collective-permute-start.16 = (bf16[768,128]{1,0:T(8,128)(2,1)S(1)}, bf16[768,128]{1,0:T(8,128)(2,1)S(1)}, u32[]{:S(2)}, u32[]{:S(2)}) collective-permute-start(bf16[768,128]{1,0:T(8,128)(2,1)S(1)} %get-tuple-element.98), channel_id=1, source_target_pairs={{0,12},{4,8},{8,4},{12,0},{16,28},{20,24},{24,20},{28,16},{1,13},{... | collective-permute-start | bytes 589832 | tf_op jit(solution)/shard_map/ppermute | solution.py:799
  52.5 6.0 %collective-permute-start.11 = (bf16[384,128]{1,0:T(8,128)(2,1)S(1)}, bf16[384,128]{1,0:T(8,128)(2,1)S(1)}, u32[]{:S(2)}, u32[]{:S(2)}) collective-permute-start(bf16[384,128]{1,0:T(8,128)(2,1)S(1)} %get-tuple-element.89), channel_id=1, source_target_pairs={{0,16},{4,20},{8,24},{12,28},{16,0},{20,4},{24,8},{28,12},{1,17},{... | collective-permute-start | bytes 294920 | tf_op jit(solution)/shard_map/ppermute | solution.py:799
  52.8 8.6 %collective-permute-start.17 = (bf16[384,128]{1,0:T(8,128)(2,1)S(1)}, bf16[384,128]{1,0:T(8,128)(2,1)S(1)}, u32[]{:S(2)}, u32[]{:S(2)}) collective-permute-start(bf16[384,128]{1,0:T(8,128)(2,1)S(1)} %get-tuple-element.99), channel_id=1, source_target_pairs={{0,28},{4,24},{8,20},{12,16},{16,12},{20,8},{24,4},{28,0},{1,29},{... | collective-permute-start | bytes 294920 | tf_op jit(solution)/shard_map/ppermute | solution.py:799
  58.5 15.1 %collective-permute-start.18 = (bf16[768,128]{1,0:T(8,128)(2,1)S(1)}, bf16[768,128]{1,0:T(8,128)(2,1)S(1)}, u32[]{:S(2)}, u32[]{:S(2)}) collective-permute-start(bf16[768,128]{1,0:T(8,128)(2,1)S(1)} %get-tuple-element.106), channel_id=1, source_target_pairs={{0,4},{4,0},{8,12},{12,8},{16,20},{20,16},{24,28},{28,24},{1,5},{5... | collective-permute-start | bytes 589832 | tf_op jit(solution)/shard_map/ppermute | solution.py:799
  61.4 12.3 %collective-permute-start.19 = (bf16[768,128]{1,0:T(8,128)(2,1)S(1)}, bf16[768,128]{1,0:T(8,128)(2,1)S(1)}, u32[]{:S(2)}, u32[]{:S(2)}) collective-permute-start(bf16[768,128]{1,0:T(8,128)(2,1)S(1)} %get-tuple-element.107), channel_id=1, source_target_pairs={{0,8},{4,12},{8,0},{12,4},{16,24},{20,28},{24,16},{28,20},{1,9},{5... | collective-permute-start | bytes 589832 | tf_op jit(solution)/shard_map/ppermute | solution.py:799
  62.6 11.0 %collective-permute-start.20 = (bf16[768,128]{1,0:T(8,128)(2,1)S(1)}, bf16[768,128]{1,0:T(8,128)(2,1)S(1)}, u32[]{:S(2)}, u32[]{:S(2)}) collective-permute-start(bf16[768,128]{1,0:T(8,128)(2,1)S(1)} %get-tuple-element.108), channel_id=1, source_target_pairs={{0,12},{4,8},{8,4},{12,0},{16,28},{20,24},{24,20},{28,16},{1,13},{... | collective-permute-start | bytes 589832 | tf_op jit(solution)/shard_map/ppermute | solution.py:799
  64.4 6.5 %collective-permute-start.12 = (bf16[384,128]{1,0:T(8,128)(2,1)S(1)}, bf16[384,128]{1,0:T(8,128)(2,1)S(1)}, u32[]{:S(2)}, u32[]{:S(2)}) collective-permute-start(bf16[384,128]{1,0:T(8,128)(2,1)S(1)} %get-tuple-element.91), channel_id=1, source_target_pairs={{0,20},{4,16},{8,28},{12,24},{16,4},{20,0},{24,12},{28,8},{1,21},{... | collective-permute-start | bytes 294920 | tf_op jit(solution)/shard_map/ppermute | solution.py:799
  65.7 7.9 %collective-permute-start.13 = (bf16[384,128]{1,0:T(8,128)(2,1)S(1)}, bf16[384,128]{1,0:T(8,128)(2,1)S(1)}, u32[]{:S(2)}, u32[]{:S(2)}) collective-permute-start(bf16[384,128]{1,0:T(8,128)(2,1)S(1)} %get-tuple-element.92), channel_id=1, source_target_pairs={{0,24},{4,28},{8,16},{12,20},{16,8},{20,12},{24,0},{28,4},{1,25},{... | collective-permute-start | bytes 294920 | tf_op jit(solution)/shard_map/ppermute | solution.py:799
  74.0 3.3 %collective-permute-start.23 = (f32[8,128]{1,0:T(8,128)S(1)}, f32[8,128]{1,0:T(8,128)S(1)}, u32[]{:S(2)}, u32[]{:S(2)}) collective-permute-start(f32[8,128]{1,0:T(8,128)S(1)} %shard_map.99), channel_id=1, source_target_pairs={{0,3},{1,2},{2,1},{3,0},{4,7},{5,6},{6,5},{7,4},{8,11},{9,10},{10,... | collective-permute-start | bytes 12296 | tf_op jit(solution)/shard_map/ppermute | solution.py:824
  74.1 3.7 %collective-permute-start.22 = (f32[8,128]{1,0:T(8,128)S(1)}, f32[8,128]{1,0:T(8,128)S(1)}, u32[]{:S(2)}, u32[]{:S(2)}) collective-permute-start(f32[8,128]{1,0:T(8,128)S(1)} %shard_map.99), channel_id=1, source_target_pairs={{0,2},{1,3},{2,0},{3,1},{4,6},{5,7},{6,4},{7,5},{8,10},{9,11},{10,... | collective-permute-start | bytes 12296 | tf_op jit(solution)/shard_map/ppermute | solution.py:824
  (7 other events, 68.0 us)

commit v7 on v6

--- a/solution.py
+++ b/solution.py
@@ -904,7 +904,8 @@
     )
     *firsts, far_stats = lax.optimization_barrier((*firsts, far_stats))
     rest = firsts[half_count:]
-    firsts = swap_inside(firsts[:half_count])
+    own_first, near_first, *rest_firsts = firsts[:half_count]
+    rest_firsts = [swap(block, d) for d, block in enumerate(rest_firsts, 2)]
     results = call(
         functools.partial(second_head_kernel, shape, stat_rows),
         [half_array(4 * tokens, single)] * half_count
@@ -918,7 +919,12 @@
     far_sent, seconds = list(results[half_count:]), list(results[:half_count])
     near = half_count // 2
     far_parts = swap_across(far_sent)
-    seconds[2:], firsts, far_parts[-1] = lax.optimization_barrier((seconds[2:], firsts, far_parts[-1]))
+    near_first, far_sent = lax.optimization_barrier((near_first, far_sent))
+    firsts = [own_first, swap(near_first, 1)] + rest_firsts
+    seconds[2:], rest_firsts, far_parts[-1] = lax.optimization_barrier(
+        (seconds[2:], rest_firsts, far_parts[-1])
+    )
+    firsts[2:] = rest_firsts
     seconds[1], far_parts[0] = lax.optimization_barrier((seconds[1], far_parts[0]))
     seconds = swap_inside(seconds)
     inner = call(

time: 79.1 us -> 79.8 us (level)
  waiting for transfers between devices: 21.9 us -> 23.2 us
  starting transfers between devices: 41.5 us -> 40.7 us
    ppermute x18, waiting for transfers between devices: 19 us -> 20.4 us  [swap(): return lax.ppermute(block, 'seq', [(i, i ^ distance) for i in range(count)])]
  transfers between devices with their start and end apart: 25 -> 25, of which waited for: 11 -> 9; matrix products, arithmetic and copies ran while one was open for 0% -> 0% of each run, Pallas kernels for 11% -> 11%
where the time goes in v7:
time: 79.8 us; the launch traced here: 79.4 us
  starting transfers between devices  40.7 us (51%)
  waiting for transfers between devices  23.2 us (29%)
  Pallas kernels  14.3 us (18%)
  between operations  0.81 us (1%)
    ppermute x18, starting transfers between devices, swap(): return lax.ppermute(block, 'seq', [(i, i ^ distance) for i in range(count)])  31.5 us
    ppermute x18, waiting for transfers between devices, swap(): return lax.ppermute(block, 'seq', [(i, i ^ distance) for i in range(count)])  20.4 us
    pallas_call x8, Pallas kernels, call(): pl.pallas_call(kernel, out_shape=out_shapes, in_specs=[pl.BlockSpec(memor...  14.3 us
    all_to_all x1, starting transfers between devices, exchange_inside(): lax.all_to_all(parts, 'seq', split_axis=0, concat_axis=0, tiled=True, axi...  5.39 us
    ppermute x6, starting transfers between devices, sum_over_head(): lax.ppermute(block, 'head', [(i, i ^ d) for i in range(count)])  3.84 us
    ppermute x6, waiting for transfers between devices, sum_over_head(): lax.ppermute(block, 'head', [(i, i ^ d) for i in range(count)])  2.86 us
  transfers between devices with their start and end apart: 25, of which 9 were waited for; matrix products, arithmetic and copies ran while one was open for 0% of the time, Pallas kernels for 11%

profile of v7, /device:TPU:0, one launch (start us, length us, event | category | flops | bytes accessed | tf_op | source)
XLA Modules:
  0.0 79.4 jit_solution(872194683320853549)
XLA Ops:
  0.6 2.2 %shard_map.93 = bf16[2304,256]{1,0:T(8,128)(2,1)} custom-call(bf16[192,1024]{1,0:T(8,128)(2,1)} %query_ref.3, bf16[192,1024]{1,0:T(8,128)(2,1)} %value_ref.3, bf16[192,1024]{1,0:T(8,128)(2,1)} %grad_ref.3), custom_call_target="tpu_custom_call" | custom-call | tf_op jit(solution)/shard_map/pallas_call | solution.py:784
  2.9 5.4 %all-to-all-start = ((bf16[4,576,256]{2,1,0:T(8,128)(2,1)}), bf16[4,576,256]{2,1,0:T(8,128)(2,1)S(1)}, u32[]{:S(2)}, u32[]{:S(2)}) async-start(bf16[4,576,256]{2,1,0:T(8,128)(2,1)} %bitcast.14), calls=%async_computation | async-start | bytes 2359296 | tf_op jit(solution)/shard_map/all_to_all | solution.py:814
  11.5 1.3 %collective-permute-done.1 = f32[8,128]{1,0:T(8,128)S(1)} collective-permute-done((f32[8,128]{1,0:T(8,128)S(1)}, f32[8,128]{1,0:T(8,128)S(1)}, u32[]{:S(2)}, u32[]{:S(2)}) %collective-permute-start.1) | collective-permute-done | bytes 4128 | tf_op jit(solution)/shard_map/ppermute | solution.py:824
  13.2 2.6 %collective-permute-start.3 = (bf16[400,128]{1,0:T(8,128)(2,1)S(1)}, bf16[400,128]{1,0:T(8,128)(2,1)S(1)}, u32[]{:S(2)}, u32[]{:S(2)}) collective-permute-start(bf16[400,128]{1,0:T(8,128)(2,1)S(1)} %get-tuple-element.61), channel_id=1, source_target_pairs={{0,16},{4,20},{8,24},{12,28},{16,0},{20,4},{24,8},{28,12},{1,17},{... | collective-permute-start | bytes 307208 | tf_op jit(solution)/shard_map/ppermute | solution.py:799
  15.9 1.5 %collective-permute-start.4 = (bf16[400,128]{1,0:T(8,128)(2,1)S(1)}, bf16[400,128]{1,0:T(8,128)(2,1)S(1)}, u32[]{:S(2)}, u32[]{:S(2)}) collective-permute-start(bf16[400,128]{1,0:T(8,128)(2,1)S(1)} %get-tuple-element.63), channel_id=1, source_target_pairs={{0,20},{4,16},{8,28},{12,24},{16,4},{20,0},{24,12},{28,8},{1,21},{... | collective-permute-start | bytes 307208 | tf_op jit(solution)/shard_map/ppermute | solution.py:799
  17.4 3.5 %collective-permute-start.5 = (bf16[400,128]{1,0:T(8,128)(2,1)S(1)}, bf16[400,128]{1,0:T(8,128)(2,1)S(1)}, u32[]{:S(2)}, u32[]{:S(2)}) collective-permute-start(bf16[400,128]{1,0:T(8,128)(2,1)S(1)} %get-tuple-element.64), channel_id=1, source_target_pairs={{0,24},{4,28},{8,16},{12,20},{16,8},{20,12},{24,0},{28,4},{1,25},{... | collective-permute-start | bytes 307208 | tf_op jit(solution)/shard_map/ppermute | solution.py:799
  21.8 2.7 %collective-permute-done.3.refs_0_ = bf16[400,128]{1,0:T(8,128)(2,1)S(1)} collective-permute-done((bf16[400,128]{1,0:T(8,128)(2,1)S(1)}, bf16[400,128]{1,0:T(8,128)(2,1)S(1)}, u32[]{:S(2)}, u32[]{:S(2)}) %collective-permute-start.3) | collective-permute-done | bytes 102432 | tf_op jit(solution)/shard_map/ppermute | solution.py:799
  24.5 5.1 %collective-permute-start.8 = (bf16[208,256]{1,0:T(8,128)(2,1)S(1)}, bf16[208,256]{1,0:T(8,128)(2,1)S(1)}, u32[]{:S(2)}, u32[]{:S(2)}) collective-permute-start(bf16[208,256]{1,0:T(8,128)(2,1)S(1)} %get-tuple-element.67), channel_id=1, source_target_pairs={{0,8},{4,12},{8,0},{12,4},{16,24},{20,28},{24,16},{28,20},{1,9},{5... | collective-permute-start | bytes 319496 | tf_op jit(solution)/shard_map/ppermute | solution.py:799
  29.6 1.5 %collective-permute-start.9 = (bf16[208,256]{1,0:T(8,128)(2,1)S(1)}, bf16[208,256]{1,0:T(8,128)(2,1)S(1)}, u32[]{:S(2)}, u32[]{:S(2)}) collective-permute-start(bf16[208,256]{1,0:T(8,128)(2,1)S(1)} %get-tuple-element.68), channel_id=1, source_target_pairs={{0,4},{4,0},{8,12},{12,8},{16,20},{20,16},{24,28},{28,24},{1,5},{5... | collective-permute-start | bytes 319496 | tf_op jit(solution)/shard_map/ppermute | solution.py:799
  31.2 2.2 %collective-permute-done.5.refs_2_ = bf16[400,128]{1,0:T(8,128)(2,1)S(1)} collective-permute-done((bf16[400,128]{1,0:T(8,128)(2,1)S(1)}, bf16[400,128]{1,0:T(8,128)(2,1)S(1)}, u32[]{:S(2)}, u32[]{:S(2)}) %collective-permute-start.5) | collective-permute-done | bytes 102432 | tf_op jit(solution)/shard_map/ppermute | solution.py:799
  33.4 3.1 %collective-permute-done.6.refs_3_ = bf16[400,128]{1,0:T(8,128)(2,1)S(1)} collective-permute-done((bf16[400,128]{1,0:T(8,128)(2,1)S(1)}, bf16[400,128]{1,0:T(8,128)(2,1)S(1)}, u32[]{:S(2)}, u32[]{:S(2)}) %collective-permute-start.6) | collective-permute-done | bytes 102432 | tf_op jit(solution)/shard_map/ppermute | solution.py:799
  36.7 1.8 %shard_map.95.refs_8_ = f32[24,128]{1,0:T(8,128)S(1)} custom-call(s32[1]{0:T(128)} %bitcast.me_ref, f32[12,128]{1,0:T(8,128)S(1)} %pad.13.pattern_ref, bf16[2304,256]{1,0:T(8,128)(2,1)S(1)} %bitcast.11, bf16[400,128]{1,0:T(8,128)(2,1)S(1)} %collective-permute-done.3.refs_0_, bf16[400,128]{1,0:T(8,128)(2,1)S(1)} %collective-permute-done.4.refs_1_, ...), custom_call_target="tpu_custom_call" | custom-call | flops 301989888 | tf_op jit(solution)/shard_map/pallas_call | solution.py:784
  38.5 3.3 %collective-permute-start.10 = (f32[24,128]{1,0:T(8,128)S(1)}, f32[24,128]{1,0:T(8,128)S(1)}, u32[]{:S(2)}, u32[]{:S(2)}) collective-permute-start(f32[24,128]{1,0:T(8,128)S(1)} %shard_map.95.refs_8_), channel_id=1, source_target_pairs={{0,16},{4,20},{8,24},{12,28},{16,0},{20,4},{24,8},{28,12},{1,17},{... | collective-permute-start | bytes 36872 | tf_op jit(solution)/shard_map/ppermute | solution.py:799
  41.8 4.3 %shard_map.96 = (bf16[768,128]{1,0:T(8,128)(2,1)S(1)}, bf16[768,128]{1,0:T(8,128)(2,1)S(1)}, bf16[768,128]{1,0:T(8,128)(2,1)S(1)}, bf16[768,128]{1,0:T(8,128)(2,...) custom-call(s32[1]{0:T(128)} %bitcast.me_ref, ...), custom_call_target="tpu_custom_call" | custom-call | flops 1358954496 | tf_op jit(solution)/shard_map/pallas_call | solution.py:784
  46.3 1.9 %collective-permute-start.15 = (bf16[768,128]{1,0:T(8,128)(2,1)S(1)}, bf16[768,128]{1,0:T(8,128)(2,1)S(1)}, u32[]{:S(2)}, u32[]{:S(2)}) collective-permute-start(bf16[768,128]{1,0:T(8,128)(2,1)S(1)} %get-tuple-element.95), channel_id=1, source_target_pairs={{0,12},{4,8},{8,4},{12,0},{16,28},{20,24},{24,20},{28,16},{1,13},{... | collective-permute-start | bytes 589832 | tf_op jit(solution)/shard_map/ppermute | solution.py:799
  48.1 2.8 %shard_map.97 = (bf16[768,128]{1,0:T(8,128)(2,1)S(1)}, bf16[768,128]{1,0:T(8,128)(2,1)S(1)}, bf16[768,128]{1,0:T(8,128)(2,1)S(1)}, bf16[768,128]{1,0:T(8,128)(2,...) custom-call(s32[1]{0:T(128)} %bitcast.me_ref, ...), custom_call_target="tpu_custom_call" | custom-call | flops 905969664 | tf_op jit(solution)/shard_map/pallas_call | solution.py:784
  51.9 2.6 %collective-permute-start.16 = (bf16[384,128]{1,0:T(8,128)(2,1)S(1)}, bf16[384,128]{1,0:T(8,128)(2,1)S(1)}, u32[]{:S(2)}, u32[]{:S(2)}) collective-permute-start(bf16[384,128]{1,0:T(8,128)(2,1)S(1)} %get-tuple-element.96), channel_id=1, source_target_pairs={{0,28},{4,24},{8,20},{12,16},{16,12},{20,8},{24,4},{28,0},{1,29},{... | collective-permute-start | bytes 294920 | tf_op jit(solution)/shard_map/ppermute | solution.py:799
  55.3 6.3 %collective-permute-done.11.refs_0_ = bf16[384,128]{1,0:T(8,128)(2,1)S(1)} collective-permute-done((bf16[384,128]{1,0:T(8,128)(2,1)S(1)}, bf16[384,128]{1,0:T(8,128)(2,1)S(1)}, u32[]{:S(2)}, u32[]{:S(2)}) %collective-permute-start.11) | collective-permute-done | bytes 98336 | tf_op jit(solution)/shard_map/ppermute | solution.py:799
  61.6 1.7 %collective-permute-start.17 = (bf16[768,128]{1,0:T(8,128)(2,1)S(1)}, bf16[768,128]{1,0:T(8,128)(2,1)S(1)}, u32[]{:S(2)}, u32[]{:S(2)}) collective-permute-start(bf16[768,128]{1,0:T(8,128)(2,1)S(1)} %get-tuple-element.100), channel_id=1, source_target_pairs={{0,4},{4,0},{8,12},{12,8},{16,20},{20,16},{24,28},{28,24},{1,5},{5... | collective-permute-start | bytes 589832 | tf_op jit(solution)/shard_map/ppermute | solution.py:799
  63.7 3.3 %collective-permute-start.19 = (bf16[768,128]{1,0:T(8,128)(2,1)S(1)}, bf16[768,128]{1,0:T(8,128)(2,1)S(1)}, u32[]{:S(2)}, u32[]{:S(2)}) collective-permute-start(bf16[768,128]{1,0:T(8,128)(2,1)S(1)} %get-tuple-element.105), channel_id=1, source_target_pairs={{0,8},{4,12},{8,0},{12,4},{16,24},{20,28},{24,16},{28,20},{1,9},{5... | collective-permute-start | bytes 589832 | tf_op jit(solution)/shard_map/ppermute | solution.py:799
  67.0 1.3 %collective-permute-start.13 = (bf16[384,128]{1,0:T(8,128)(2,1)S(1)}, bf16[384,128]{1,0:T(8,128)(2,1)S(1)}, u32[]{:S(2)}, u32[]{:S(2)}) collective-permute-start(bf16[384,128]{1,0:T(8,128)(2,1)S(1)} %get-tuple-element.91), channel_id=1, source_target_pairs={{0,24},{4,28},{8,16},{12,20},{16,8},{20,12},{24,0},{28,4},{1,25},{... | collective-permute-start | bytes 294920 | tf_op jit(solution)/shard_map/ppermute | solution.py:799
  68.4 5.8 %collective-permute-done.13.refs_2_ = bf16[384,128]{1,0:T(8,128)(2,1)S(1)} collective-permute-done((bf16[384,128]{1,0:T(8,128)(2,1)S(1)}, bf16[384,128]{1,0:T(8,128)(2,1)S(1)}, u32[]{:S(2)}, u32[]{:S(2)}) %collective-permute-start.13) | collective-permute-done | bytes 98336 | tf_op jit(solution)/shard_map/ppermute | solution.py:799
  74.7 1.8 %collective-permute-start.22 = (f32[8,128]{1,0:T(8,128)S(1)}, f32[8,128]{1,0:T(8,128)S(1)}, u32[]{:S(2)}, u32[]{:S(2)}) collective-permute-start(f32[8,128]{1,0:T(8,128)S(1)} %shard_map.99), channel_id=1, source_target_pairs={{0,2},{1,3},{2,0},{3,1},{4,6},{5,7},{6,4},{7,5},{8,10},{9,11},{10,... | collective-permute-start | bytes 12296 | tf_op jit(solution)/shard_map/ppermute | solution.py:824
  76.5 1.4 %shard_map.98 = (bf16[192,1024]{1,0:T(8,128)(2,1)}, bf16[192,1024]{1,0:T(8,128)(2,1)}, bf16[192,1024]{1,0:T(8,128)(2,1)}) custom-call(s32[1]{0:T(128)} %bitcast.me_ref, bf16[384,128]{1,0:T(8,128)(2,1)S(1)} %collective-permute-done.11.refs_0_, bf16[384,128]{1,0:T(8,128)(2,1)S(1)} %collective-permute-done.12.refs_1_, ...), custom_call_target="tpu_custom_call" | custom-call | tf_op jit(solution)/shard_map/pallas_call | solution.py:784
  (55 shorter events, 9.3 us)
Async XLA Ops:
  2.9 33.8 %all-to-all-start = ((bf16[4,576,256]{2,1,0:T(8,128)(2,1)}), bf16[4,576,256]{2,1,0:T(8,128)(2,1)S(1)}, u32[]{:S(2)}, u32[]{:S(2)}) async-start(bf16[4,576,256]{2,1,0:T(8,128)(2,1)} %bitcast.14), calls=%async_computation | async-start | bytes 2359296 | tf_op jit(solution)/shard_map/all_to_all | solution.py:814
  8.4 3.1 %collective-permute-start.2 = (f32[8,128]{1,0:T(8,128)S(1)}, f32[8,128]{1,0:T(8,128)S(1)}, u32[]{:S(2)}, u32[]{:S(2)}) collective-permute-start(f32[8,128]{1,0:T(8,128)S(1)} %pad_bitcast_fusion.1), channel_id=1, source_target_pairs={{0,3},{1,2},{2,1},{3,0},{4,7},{5,6},{6,5},{7,4},{8,11},{9,10},{10,... | collective-permute-start | bytes 12296 | tf_op jit(solution)/shard_map/ppermute | solution.py:824
  9.2 3.6 %collective-permute-start.1 = (f32[8,128]{1,0:T(8,128)S(1)}, f32[8,128]{1,0:T(8,128)S(1)}, u32[]{:S(2)}, u32[]{:S(2)}) collective-permute-start(f32[8,128]{1,0:T(8,128)S(1)} %pad_bitcast_fusion.1), channel_id=1, source_target_pairs={{0,2},{1,3},{2,0},{3,1},{4,6},{5,7},{6,4},{7,5},{8,10},{9,11},{10,... | collective-permute-start | bytes 12296 | tf_op jit(solution)/shard_map/ppermute | solution.py:824
  10.1 2.7 %collective-permute-start = (f32[8,128]{1,0:T(8,128)S(1)}, f32[8,128]{1,0:T(8,128)S(1)}, u32[]{:S(2)}, u32[]{:S(2)}) collective-permute-start(f32[8,128]{1,0:T(8,128)S(1)} %pad_bitcast_fusion.1), channel_id=1, source_target_pairs={{0,1},{1,0},{2,3},{3,2},{4,5},{5,4},{6,7},{7,6},{8,9},{9,8},{10,11... | collective-permute-start | bytes 12296 | tf_op jit(solution)/shard_map/ppermute | solution.py:824
  13.2 11.2 %collective-permute-start.3 = (bf16[400,128]{1,0:T(8,128)(2,1)S(1)}, bf16[400,128]{1,0:T(8,128)(2,1)S(1)}, u32[]{:S(2)}, u32[]{:S(2)}) collective-permute-start(bf16[400,128]{1,0:T(8,128)(2,1)S(1)} %get-tuple-element.61), channel_id=1, source_target_pairs={{0,16},{4,20},{8,24},{12,28},{16,0},{20,4},{24,8},{28,12},{1,17},{... | collective-permute-start | bytes 307208 | tf_op jit(solution)/shard_map/ppermute | solution.py:799
  15.9 13.7 %collective-permute-start.4 = (bf16[400,128]{1,0:T(8,128)(2,1)S(1)}, bf16[400,128]{1,0:T(8,128)(2,1)S(1)}, u32[]{:S(2)}, u32[]{:S(2)}) collective-permute-start(bf16[400,128]{1,0:T(8,128)(2,1)S(1)} %get-tuple-element.63), channel_id=1, source_target_pairs={{0,20},{4,16},{8,28},{12,24},{16,4},{20,0},{24,12},{28,8},{1,21},{... | collective-permute-start | bytes 307208 | tf_op jit(solution)/shard_map/ppermute | solution.py:799
  17.4 16.0 %collective-permute-start.5 = (bf16[400,128]{1,0:T(8,128)(2,1)S(1)}, bf16[400,128]{1,0:T(8,128)(2,1)S(1)}, u32[]{:S(2)}, u32[]{:S(2)}) collective-permute-start(bf16[400,128]{1,0:T(8,128)(2,1)S(1)} %get-tuple-element.64), channel_id=1, source_target_pairs={{0,24},{4,28},{8,16},{12,20},{16,8},{20,12},{24,0},{28,4},{1,25},{... | collective-permute-start | bytes 307208 | tf_op jit(solution)/shard_map/ppermute | solution.py:799
  20.9 15.6 %collective-permute-start.6 = (bf16[400,128]{1,0:T(8,128)(2,1)S(1)}, bf16[400,128]{1,0:T(8,128)(2,1)S(1)}, u32[]{:S(2)}, u32[]{:S(2)}) collective-permute-start(bf16[400,128]{1,0:T(8,128)(2,1)S(1)} %get-tuple-element.65), channel_id=1, source_target_pairs={{0,28},{4,24},{8,20},{12,16},{16,12},{20,8},{24,4},{28,0},{1,29},{... | collective-permute-start | bytes 307208 | tf_op jit(solution)/shard_map/ppermute | solution.py:799
  21.0 15.5 %collective-permute-start.7 = (bf16[208,256]{1,0:T(8,128)(2,1)S(1)}, bf16[208,256]{1,0:T(8,128)(2,1)S(1)}, u32[]{:S(2)}, u32[]{:S(2)}) collective-permute-start(bf16[208,256]{1,0:T(8,128)(2,1)S(1)} %get-tuple-element.66), channel_id=1, source_target_pairs={{0,12},{4,8},{8,4},{12,0},{16,28},{20,24},{24,20},{28,16},{1,13},{... | collective-permute-start | bytes 319496 | tf_op jit(solution)/shard_map/ppermute | solution.py:799
  24.5 12.2 %collective-permute-start.8 = (bf16[208,256]{1,0:T(8,128)(2,1)S(1)}, bf16[208,256]{1,0:T(8,128)(2,1)S(1)}, u32[]{:S(2)}, u32[]{:S(2)}) collective-permute-start(bf16[208,256]{1,0:T(8,128)(2,1)S(1)} %get-tuple-element.67), channel_id=1, source_target_pairs={{0,8},{4,12},{8,0},{12,4},{16,24},{20,28},{24,16},{28,20},{1,9},{5... | collective-permute-start | bytes 319496 | tf_op jit(solution)/shard_map/ppermute | solution.py:799
  29.6 7.0 %collective-permute-start.9 = (bf16[208,256]{1,0:T(8,128)(2,1)S(1)}, bf16[208,256]{1,0:T(8,128)(2,1)S(1)}, u32[]{:S(2)}, u32[]{:S(2)}) collective-permute-start(bf16[208,256]{1,0:T(8,128)(2,1)S(1)} %get-tuple-element.68), channel_id=1, source_target_pairs={{0,4},{4,0},{8,12},{12,8},{16,20},{20,16},{24,28},{28,24},{1,5},{5... | collective-permute-start | bytes 319496 | tf_op jit(solution)/shard_map/ppermute | solution.py:799
  38.5 7.7 %collective-permute-start.10 = (f32[24,128]{1,0:T(8,128)S(1)}, f32[24,128]{1,0:T(8,128)S(1)}, u32[]{:S(2)}, u32[]{:S(2)}) collective-permute-start(f32[24,128]{1,0:T(8,128)S(1)} %shard_map.95.refs_8_), channel_id=1, source_target_pairs={{0,16},{4,20},{8,24},{12,28},{16,0},{20,4},{24,8},{28,12},{1,17},{... | collective-permute-start | bytes 36872 | tf_op jit(solution)/shard_map/ppermute | solution.py:799
  46.2 17.5 %collective-permute-start.14 = (bf16[768,128]{1,0:T(8,128)(2,1)S(1)}, bf16[768,128]{1,0:T(8,128)(2,1)S(1)}, u32[]{:S(2)}, u32[]{:S(2)}) collective-permute-start(bf16[768,128]{1,0:T(8,128)(2,1)S(1)} %get-tuple-element.94), channel_id=1, source_target_pairs={{0,8},{4,12},{8,0},{12,4},{16,24},{20,28},{24,16},{28,20},{1,9},{5... | collective-permute-start | bytes 589832 | tf_op jit(solution)/shard_map/ppermute | solution.py:799
  46.3 17.4 %collective-permute-start.15 = (bf16[768,128]{1,0:T(8,128)(2,1)S(1)}, bf16[768,128]{1,0:T(8,128)(2,1)S(1)}, u32[]{:S(2)}, u32[]{:S(2)}) collective-permute-start(bf16[768,128]{1,0:T(8,128)(2,1)S(1)} %get-tuple-element.95), channel_id=1, source_target_pairs={{0,12},{4,8},{8,4},{12,0},{16,28},{20,24},{24,20},{28,16},{1,13},{... | collective-permute-start | bytes 589832 | tf_op jit(solution)/shard_map/ppermute | solution.py:799
  50.9 10.7 %collective-permute-start.11 = (bf16[384,128]{1,0:T(8,128)(2,1)S(1)}, bf16[384,128]{1,0:T(8,128)(2,1)S(1)}, u32[]{:S(2)}, u32[]{:S(2)}) collective-permute-start(bf16[384,128]{1,0:T(8,128)(2,1)S(1)} %get-tuple-element.88), channel_id=1, source_target_pairs={{0,16},{4,20},{8,24},{12,28},{16,0},{20,4},{24,8},{28,12},{1,17},{... | collective-permute-start | bytes 294920 | tf_op jit(solution)/shard_map/ppermute | solution.py:799
  51.9 11.5 %collective-permute-start.16 = (bf16[384,128]{1,0:T(8,128)(2,1)S(1)}, bf16[384,128]{1,0:T(8,128)(2,1)S(1)}, u32[]{:S(2)}, u32[]{:S(2)}) collective-permute-start(bf16[384,128]{1,0:T(8,128)(2,1)S(1)} %get-tuple-element.96), channel_id=1, source_target_pairs={{0,28},{4,24},{8,20},{12,16},{16,12},{20,8},{24,4},{28,0},{1,29},{... | collective-permute-start | bytes 294920 | tf_op jit(solution)/shard_map/ppermute | solution.py:799
  54.5 12.6 %collective-permute-start.12 = (bf16[384,128]{1,0:T(8,128)(2,1)S(1)}, bf16[384,128]{1,0:T(8,128)(2,1)S(1)}, u32[]{:S(2)}, u32[]{:S(2)}) collective-permute-start(bf16[384,128]{1,0:T(8,128)(2,1)S(1)} %get-tuple-element.90), channel_id=1, source_target_pairs={{0,20},{4,16},{8,28},{12,24},{16,4},{20,0},{24,12},{28,8},{1,21},{... | collective-permute-start | bytes 294920 | tf_op jit(solution)/shard_map/ppermute | solution.py:799
  61.6 12.6 %collective-permute-start.17 = (bf16[768,128]{1,0:T(8,128)(2,1)S(1)}, bf16[768,128]{1,0:T(8,128)(2,1)S(1)}, u32[]{:S(2)}, u32[]{:S(2)}) collective-permute-start(bf16[768,128]{1,0:T(8,128)(2,1)S(1)} %get-tuple-element.100), channel_id=1, source_target_pairs={{0,4},{4,0},{8,12},{12,8},{16,20},{20,16},{24,28},{28,24},{1,5},{5... | collective-permute-start | bytes 589832 | tf_op jit(solution)/shard_map/ppermute | solution.py:799
  63.3 10.9 %collective-permute-start.18 = (bf16[768,128]{1,0:T(8,128)(2,1)S(1)}, bf16[768,128]{1,0:T(8,128)(2,1)S(1)}, u32[]{:S(2)}, u32[]{:S(2)}) collective-permute-start(bf16[768,128]{1,0:T(8,128)(2,1)S(1)} %get-tuple-element.104), channel_id=1, source_target_pairs={{0,4},{4,0},{8,12},{12,8},{16,20},{20,16},{24,28},{28,24},{1,5},{5... | collective-permute-start | bytes 589832 | tf_op jit(solution)/shard_map/ppermute | solution.py:799
  63.7 10.6 %collective-permute-start.19 = (bf16[768,128]{1,0:T(8,128)(2,1)S(1)}, bf16[768,128]{1,0:T(8,128)(2,1)S(1)}, u32[]{:S(2)}, u32[]{:S(2)}) collective-permute-start(bf16[768,128]{1,0:T(8,128)(2,1)S(1)} %get-tuple-element.105), channel_id=1, source_target_pairs={{0,8},{4,12},{8,0},{12,4},{16,24},{20,28},{24,16},{28,20},{1,9},{5... | collective-permute-start | bytes 589832 | tf_op jit(solution)/shard_map/ppermute | solution.py:799
  66.9 7.3 %collective-permute-start.20 = (bf16[768,128]{1,0:T(8,128)(2,1)S(1)}, bf16[768,128]{1,0:T(8,128)(2,1)S(1)}, u32[]{:S(2)}, u32[]{:S(2)}) collective-permute-start(bf16[768,128]{1,0:T(8,128)(2,1)S(1)} %get-tuple-element.106), channel_id=1, source_target_pairs={{0,12},{4,8},{8,4},{12,0},{16,28},{20,24},{24,20},{28,16},{1,13},{... | collective-permute-start | bytes 589832 | tf_op jit(solution)/shard_map/ppermute | solution.py:799
  67.0 7.2 %collective-permute-start.13 = (bf16[384,128]{1,0:T(8,128)(2,1)S(1)}, bf16[384,128]{1,0:T(8,128)(2,1)S(1)}, u32[]{:S(2)}, u32[]{:S(2)}) collective-permute-start(bf16[384,128]{1,0:T(8,128)(2,1)S(1)} %get-tuple-element.91), channel_id=1, source_target_pairs={{0,24},{4,28},{8,16},{12,20},{16,8},{20,12},{24,0},{28,4},{1,25},{... | collective-permute-start | bytes 294920 | tf_op jit(solution)/shard_map/ppermute | solution.py:799
  74.6 3.3 %collective-permute-start.23 = (f32[8,128]{1,0:T(8,128)S(1)}, f32[8,128]{1,0:T(8,128)S(1)}, u32[]{:S(2)}, u32[]{:S(2)}) collective-permute-start(f32[8,128]{1,0:T(8,128)S(1)} %shard_map.99), channel_id=1, source_target_pairs={{0,3},{1,2},{2,1},{3,0},{4,7},{5,6},{6,5},{7,4},{8,11},{9,10},{10,... | collective-permute-start | bytes 12296 | tf_op jit(solution)/shard_map/ppermute | solution.py:824
  74.7 3.7 %collective-permute-start.22 = (f32[8,128]{1,0:T(8,128)S(1)}, f32[8,128]{1,0:T(8,128)S(1)}, u32[]{:S(2)}, u32[]{:S(2)}) collective-permute-start(f32[8,128]{1,0:T(8,128)S(1)} %shard_map.99), channel_id=1, source_target_pairs={{0,2},{1,3},{2,0},{3,1},{4,6},{5,7},{6,4},{7,5},{8,10},{9,11},{10,... | collective-permute-start | bytes 12296 | tf_op jit(solution)/shard_map/ppermute | solution.py:824
  (7 other events, 67.6 us)
